TPU v7x, 512 devices: a whole 4x8x8 slice. The times are simulated.
512 devices in a mesh: batch: 8 (over x, y_hi), px: 4 (over y_lo), py: 16 (over z, core).
Axes of the slice: x: 4, y: 8 (y_hi: 2, y_lo: 4; y = y_hi * 4 + y_lo), z: 8, core: 2. Of those that a mesh axis runs over, the one named last changes fastest.
Arguments:
- field: bfloat16 [8, 16, 128, 128, 128], P('batch', None, 'px', 'py'), may hold values from -6 to 6
- cotangent: bfloat16 [8, 16, 128, 128, 128], P('batch', None, 'px', 'py'), may hold values from -6 to 6
- spec_weight: float32 [2, 16, 16, 16, 16, 16], P(None, None, None, 'py', 'px'), may hold values from -15 to 15
- skip_weight: bfloat16 [16, 16], replicated, may hold values from -1.5 to 1.5
- skip_bias: float32 [16], replicated, may hold values from -1 to 1
- mlp_in: bfloat16 [16, 16], replicated, may hold values from -1.5 to 1.5
- mlp_out: bfloat16 [16, 16], replicated, may hold values from -1.5 to 1.5
Outputs:
- grad_input: bfloat16 [8, 16, 128, 128, 128], P('batch', None, 'px', 'py')
- grad_spectral: float32 [2, 16, 16, 16, 16, 16], P(None, None, None, 'py', 'px', 'batch')
- grad_skip: float32 [16, 16], replicated
- grad_bias: float32 [16], replicated
- grad_mlp_in: float32 [16, 16], replicated
- grad_mlp_out: float32 [16, 16], replicated
All inputs are finite; a program needn't handle non-finite values.
Results may differ from a plain program's by a relative error of at most 0.014.
Values sent between devices are 32-bit elements; how exact they have to be, the bound alone decides.
No kernel may reach another device: no remote copies, remote signals or barrier semaphores. Data moves between devices by JAX's collectives and lax.ppermute only.
A program may use at most 128 MiB of HBM per device.

v0:
```python
import math

import jax
import jax.numpy as jnp
from jax import lax
from jax.sharding import PartitionSpec as P

precise = lax.Precision.HIGHEST


def signed(indices, total_modes):
    return jnp.where(indices < total_modes // 2, indices, indices - total_modes)


def phases(frequency, positions, length):
    residue = frequency[:, None] * positions[None, :] % length
    angles = residue.astype(jnp.float32) * (2.0 * math.pi / length)
    return (jnp.cos(angles), jnp.sin(angles))


def exact(pattern, left_operand, right_operand):
    return jnp.einsum(pattern, left_operand, right_operand, precision=precise)


def lowdot(pattern, left_operand, right_operand):
    return jnp.einsum(pattern, left_operand, right_operand, preferred_element_type=jnp.float32)


def shards(field, cotangent, spec_weight, skip_weight, skip_bias, mlp_in, mlp_out):
    samples, channels, first_cells, second_cells, depth = field.shape
    first_split = lax.axis_size("px")
    second_split = lax.axis_size("py")
    depth_owned = spec_weight.shape[3]
    second_owned = spec_weight.shape[4]
    first_modes = spec_weight.shape[5]
    first_width = first_cells * first_split
    second_width = second_cells * second_split
    depth_modes = depth_owned * second_split
    second_modes = second_owned * first_split
    norm_scale = 1.0 / math.sqrt(first_width * second_width * depth)
    first_freq = signed(jnp.arange(first_modes, dtype=jnp.int32), first_modes)
    depth_cosine, depth_sine = phases(
        jnp.arange(depth_modes, dtype=jnp.int32), jnp.arange(depth, dtype=jnp.int32), depth
    )
    depth_cosine_low = depth_cosine.astype(jnp.bfloat16)
    depth_sine_low = depth_sine.astype(jnp.bfloat16)
    first_cosine, first_sine = phases(
        first_freq, jnp.arange(first_width, dtype=jnp.int32), first_width
    )
    second_cosine, second_sine = phases(
        signed(jnp.arange(second_modes, dtype=jnp.int32), second_modes),
        jnp.arange(second_width, dtype=jnp.int32),
        second_width,
    )
    second_cosine = second_cosine.reshape(second_modes, second_split, second_cells)
    second_sine = second_sine.reshape(second_modes, second_split, second_cells)
    weight_real = spec_weight[0]
    weight_imaginary = spec_weight[1]

    def depth_section(values):
        flat_values = values.reshape(samples, channels, first_cells * second_cells, depth)
        depth_real = lowdot("kz,scqz->sckq", depth_cosine_low, flat_values)
        depth_imaginary = -lowdot("kz,scqz->sckq", depth_sine_low, flat_values)
        return (depth_real, depth_imaginary)

    def forward(values):
        depth_real, depth_imaginary = depth_section(values)
        depth_real, depth_imaginary = (
            lax.all_to_all(depth_real, "py", split_axis=2, concat_axis=3, tiled=True),
            lax.all_to_all(depth_imaginary, "py", split_axis=2, concat_axis=3, tiled=True),
        )
        split_shape = (samples, channels, depth_owned, second_split, first_cells, second_cells)
        depth_real = depth_real.reshape(split_shape)
        depth_imaginary = depth_imaginary.reshape(split_shape)
        second_real = exact("sckpxy,mpy->sckmx", depth_real, second_cosine) + exact(
            "sckpxy,mpy->sckmx", depth_imaginary, second_sine
        )
        second_imaginary = exact("sckpxy,mpy->sckmx", depth_imaginary, second_cosine) - exact(
            "sckpxy,mpy->sckmx", depth_real, second_sine
        )
        second_real, second_imaginary = (
            lax.all_to_all(second_real, "px", split_axis=3, concat_axis=4, tiled=True),
            lax.all_to_all(second_imaginary, "px", split_axis=3, concat_axis=4, tiled=True),
        )
        first_real = exact("sckmx,jx->sckmj", second_real, first_cosine) + exact(
            "sckmx,jx->sckmj", second_imaginary, first_sine
        )
        first_imaginary = exact("sckmx,jx->sckmj", second_imaginary, first_cosine) - exact(
            "sckmx,jx->sckmj", second_real, first_sine
        )
        return jnp.stack([first_real, first_imaginary]) * norm_scale

    def inverse(spectra):
        spectra_real = spectra[0]
        spectra_imaginary = spectra[1]
        first_real = exact("sckmj,jx->sckmx", spectra_real, first_cosine) - exact(
            "sckmj,jx->sckmx", spectra_imaginary, first_sine
        )
        first_imaginary = exact("sckmj,jx->sckmx", spectra_imaginary, first_cosine) + exact(
            "sckmj,jx->sckmx", spectra_real, first_sine
        )
        first_real, first_imaginary = (
            lax.all_to_all(first_real, "px", split_axis=4, concat_axis=3, tiled=True),
            lax.all_to_all(first_imaginary, "px", split_axis=4, concat_axis=3, tiled=True),
        )
        second_real = exact("sckmx,mpy->sckpxy", first_real, second_cosine) - exact(
            "sckmx,mpy->sckpxy", first_imaginary, second_sine
        )
        second_imaginary = exact("sckmx,mpy->sckpxy", first_imaginary, second_cosine) + exact(
            "sckmx,mpy->sckpxy", first_real, second_sine
        )
        flat_shape = (samples, channels, depth_owned, second_split * first_cells * second_cells)
        second_real = second_real.reshape(flat_shape)
        second_imaginary = second_imaginary.reshape(flat_shape)
        second_real, second_imaginary = (
            lax.all_to_all(second_real, "py", split_axis=3, concat_axis=2, tiled=True),
            lax.all_to_all(second_imaginary, "py", split_axis=3, concat_axis=2, tiled=True),
        )
        synthesis = exact("sckq,kz->scqz", second_real, depth_cosine) - exact(
            "sckq,kz->scqz", second_imaginary, depth_sine
        )
        return synthesis.reshape(samples, channels, first_cells, second_cells, depth) * norm_scale

    input_spectra = forward(field)
    mixed_real = exact("sckmj,cokmj->sokmj", input_spectra[0], weight_real) - exact(
        "sckmj,cokmj->sokmj", input_spectra[1], weight_imaginary
    )
    mixed_imaginary = exact("sckmj,cokmj->sokmj", input_spectra[1], weight_real) + exact(
        "sckmj,cokmj->sokmj", input_spectra[0], weight_imaginary
    )
    spectral_part = inverse(jnp.stack([mixed_real, mixed_imaginary]))
    preact = (
        spectral_part
        + lowdot("oc,scxyz->soxyz", skip_weight, field)
        + skip_bias[None, :, None, None, None]
    )
    hidden = jax.nn.gelu(preact).astype(jnp.bfloat16)
    inner_sum = lowdot("hc,scxyz->shxyz", mlp_in, hidden)
    activated = jax.nn.gelu(inner_sum).astype(jnp.bfloat16)
    d_activated = lowdot("ch,scxyz->shxyz", mlp_out, cotangent)
    inner_back = jax.vjp(jax.nn.gelu, inner_sum)[1]
    d_inner = inner_back(d_activated)[0].astype(jnp.bfloat16)
    d_hidden = lowdot("hc,shxyz->scxyz", mlp_in, d_inner)
    preact_back = jax.vjp(jax.nn.gelu, preact)[1]
    d_preact = preact_back(d_hidden)[0].astype(jnp.bfloat16)
    skip_grad = lowdot("soxyz,scxyz->oc", d_preact, field)
    bias_grad = jnp.sum(d_preact.astype(jnp.float32), axis=(0, 2, 3, 4))
    inner_grad = lowdot("shxyz,scxyz->hc", d_inner, hidden)
    outer_grad = lowdot("scxyz,shxyz->ch", cotangent, activated)
    skip_grad, bias_grad, inner_grad, outer_grad = lax.psum(
        (skip_grad, bias_grad, inner_grad, outer_grad), ("batch", "px", "py")
    )
    grad_spectra = forward(d_preact)
    part_real = exact("sckmj,sokmj->cokmj", input_spectra[0], grad_spectra[0]) + exact(
        "sckmj,sokmj->cokmj", input_spectra[1], grad_spectra[1]
    )
    part_imaginary = exact("sckmj,sokmj->cokmj", input_spectra[0], grad_spectra[1]) - exact(
        "sckmj,sokmj->cokmj", input_spectra[1], grad_spectra[0]
    )
    grad_spectral = lax.psum_scatter(
        jnp.stack([part_real, part_imaginary]), "batch", scatter_dimension=5, tiled=True
    )
    back_real = exact("sokmj,cokmj->sckmj", grad_spectra[0], weight_real) + exact(
        "sokmj,cokmj->sckmj", grad_spectra[1], weight_imaginary
    )
    back_imaginary = exact("sokmj,cokmj->sckmj", grad_spectra[1], weight_real) - exact(
        "sokmj,cokmj->sckmj", grad_spectra[0], weight_imaginary
    )
    spectral_back = inverse(jnp.stack([back_real, back_imaginary]))
    grad_input = (lowdot("oc,soxyz->scxyz", skip_weight, d_preact) + spectral_back).astype(
        jnp.bfloat16
    )
    grad_scale = 1.0 / math.sqrt(
        samples * lax.axis_size("batch") * first_width * second_width * depth
    )
    return (
        grad_input,
        grad_spectral,
        skip_grad * grad_scale,
        bias_grad * grad_scale,
        inner_grad * grad_scale,
        outer_grad * grad_scale,
    )


def solution(mesh):
    placed = (
        P("batch", None, "px", "py", None),
        P("batch", None, "px", "py", None),
        P(None, None, None, "py", "px", None),
        P(),
        P(),
        P(),
        P(),
    )
    return jax.shard_map(
        shards,
        mesh=mesh,
        in_specs=placed,
        out_specs=(
            P("batch", None, "px", "py", None),
            P(None, None, None, "py", "px", "batch"),
            P(),
            P(),
            P(),
            P(),
        ),
        check_vma=False,
    )
```

profile of v0, /device:TPU:1, one launch (start us, length us, event | category | flops | bytes accessed | tf_op | source)
XLA Modules:
  0.0 584.4 jit_solution(10843902132529069504)
XLA Ops:
  9.7 11.8 %all-to-all-start.1 = ((f32[1,16,16,256]{3,1,0,2:T(8,128)}), f32[1,16,16,256]{3,1,0,2:T(8,128)S(1)}, u32[]{:S(2)}, u32[]{:S(2)}) async-start(f32[1,16,16,256]{3,1,0,2:T(8,128)} %copy.115), calls=%async_computation.1 | async-start | bytes 524288 | tf_op jit(solution)/shard_map/all_to_all | solution.py:70
  22.8 10.4 %all-to-all-done.1 = f32[1,16,16,256]{3,1,0,2:T(8,128)S(1)} async-done(((f32[1,16,16,256]{3,1,0,2:T(8,128)}), f32[1,16,16,256]{3,1,0,2:T(8,128)S(1)}, u32[]{:S(2)}, u32[]{:S(2)}) %all-to-all-start.1) | async-done | bytes 262176 | tf_op jit(solution)/shard_map/all_to_all | solution.py:70
  40.8 6.9 %all-to-all-done = f32[1,16,16,256]{3,1,0,2:T(8,128)S(1)} async-done(((f32[1,16,16,256]{3,1,0,2:T(8,128)}), f32[1,16,16,256]{3,1,0,2:T(8,128)S(1)}, u32[]{:S(2)}, u32[]{:S(2)}) %all-to-all-start) | async-done | bytes 262176 | tf_op jit(solution)/shard_map/all_to_all | solution.py:69
  55.5 4.6 all-to-all-start.2
  96.9 20.4 %reduce.22 = f32[4096,16]{1,0:T(8,128)} reduce(f32[4096,1,1,16]{3,2,1,0:T(1,128)} %bitcast.599, f32[]{:T(128)} %broadcast.652), dimensions={1,2}, to_apply=%bitcast.527.reduce_sub_computation | reduce | bytes 524292
  120.3 8.5 %all-to-all-start.7 = ((f32[16,1,4096]{2,1,0:T(1,128)}), f32[16,1,4096]{2,1,0:T(1,128)S(1)}, u32[]{:S(2)}, u32[]{:S(2)}) async-start(f32[16,1,4096]{2,1,0:T(1,128)} %reshape.617), calls=%async_computation.7 | async-start | bytes 524288 | tf_op jit(solution)/shard_map/all_to_all | solution.py:117
  133.4 20.3 %reduce.20 = f32[4096,16]{1,0:T(8,128)} reduce(f32[4096,1,1,16]{3,2,1,0:T(1,128)} %bitcast.600, f32[]{:T(128)} %broadcast.652), dimensions={1,2}, to_apply=%bitcast.525.reduce_sub_computation | reduce | bytes 524292
  156.8 7.4 %all-to-all-start.6 = ((f32[16,1,4096]{2,1,0:T(1,128)}), f32[16,1,4096]{2,1,0:T(1,128)S(1)}, u32[]{:S(2)}, u32[]{:S(2)}) async-start(f32[16,1,4096]{2,1,0:T(1,128)} %reshape.615), calls=%async_computation.6 | async-start | bytes 524288 | tf_op jit(solution)/shard_map/all_to_all | solution.py:116
  166.8 5.3 reshape.618
  177.0 5.3 reshape.616
  188.0 3.7 subtract_multiply_fusion
  204.6 6.3 %all-to-all-start.9 = ((f32[1,16,16,256]{3,1,0,2:T(8,128)}), f32[1,16,16,256]{3,1,0,2:T(8,128)S(1)}, u32[]{:S(2)}, u32[]{:S(2)}) async-start(f32[1,16,16,256]{3,1,0,2:T(8,128)} %copy.145), calls=%async_computation.9 | async-start | bytes 524288 | tf_op jit(solution)/shard_map/all_to_all | solution.py:70
  218.9 3.5 all-to-all-done.9
  222.5 3.7 all-to-all-start.8
  226.9 97.4 %all-reduce = (f32[16,16]{1,0:T(8,128)S(1)}, f32[16]{0:T(128)S(1)}, f32[16,16]{1,0:T(8,128)}, f32[16,16]{1,0:T(8,128)}) all-reduce(f32[16,16]{1,0:T(8,128)S(1)} %convolution_bitcast_fusion.12, f32[16]{0:T(128)S(1)} %get-tuple-element.46, ...), channel_id=1, replica_groups=mesh['batch'=8,'px'=4,'py'=16] {'batch','px','py'}, use_global_device_ids=true, to_apply=%region_1.2 | all-reduce | flops 784 | bytes 6272 | tf_op jit(solution)/shard_map/psum | solution.py:150
  340.2 4.3 all-to-all-start.10
  382.4 20.4 %reduce.30 = f32[4096,16]{1,0:T(8,128)} reduce(f32[4096,1,1,16]{3,2,1,0:T(1,128)} %bitcast.602, f32[]{:T(128)} %broadcast.652), dimensions={1,2}, to_apply=%bitcast.539.reduce_sub_computation | reduce | bytes 524292
  405.8 10.5 %all-to-all-start.15 = ((f32[16,1,4096]{2,1,0:T(1,128)}), f32[16,1,4096]{2,1,0:T(1,128)}, u32[]{:S(2)}, u32[]{:S(2)}) async-start(f32[16,1,4096]{2,1,0:T(1,128)} %reshape.629), calls=%async_computation.15 | async-start | bytes 524288 | tf_op jit(solution)/shard_map/all_to_all | solution.py:117
  422.2 20.4 %reduce.28 = f32[4096,16]{1,0:T(8,128)} reduce(f32[4096,1,1,16]{3,2,1,0:T(1,128)} %bitcast.603, f32[]{:T(128)} %broadcast.652), dimensions={1,2}, to_apply=%bitcast.537.reduce_sub_computation | reduce | bytes 524292
  445.7 7.4 %all-to-all-start.14 = ((f32[16,1,4096]{2,1,0:T(1,128)}), f32[16,1,4096]{2,1,0:T(1,128)S(1)}, u32[]{:S(2)}, u32[]{:S(2)}) async-start(f32[16,1,4096]{2,1,0:T(1,128)} %reshape.627), calls=%async_computation.14 | async-start | bytes 524288 | tf_op jit(solution)/shard_map/all_to_all | solution.py:116
  455.6 91.3 %reduce-scatter.2.cloned.1.call-done = f32[2,16,16,1,4,2]{2,1,4,3,0,5:T(8,128)} async-done(((f32[2,16,16,1,4,16]{2,1,4,3,0,5:T(8,128)}), f32[2,16,16,1,4,2]{2,1,4,3,0,5:T(8,128)}) %reduce-scatter.2.cloned.1.call-update) | async-done | bytes 16400 | tf_op jit(solution)/shard_map/reduce_scatter | solution.py:160
  550.8 5.3 reshape.630
  559.6 5.3 reshape.628
  570.6 3.8 multiply_bitcast_fusion
  (195 shorter events, 184.6 us)
Async XLA Ops:
  9.7 23.5 %all-to-all-start.1 = ((f32[1,16,16,256]{3,1,0,2:T(8,128)}), f32[1,16,16,256]{3,1,0,2:T(8,128)S(1)}, u32[]{:S(2)}, u32[]{:S(2)}) async-start(f32[1,16,16,256]{3,1,0,2:T(8,128)} %copy.115), calls=%async_computation.1 | async-start | bytes 524288 | tf_op jit(solution)/shard_map/all_to_all | solution.py:70
  33.2 14.6 %all-to-all-start = ((f32[1,16,16,256]{3,1,0,2:T(8,128)}), f32[1,16,16,256]{3,1,0,2:T(8,128)S(1)}, u32[]{:S(2)}, u32[]{:S(2)}) async-start(f32[1,16,16,256]{3,1,0,2:T(8,128)} %copy.111), calls=%async_computation | async-start | bytes 524288 | tf_op jit(solution)/shard_map/all_to_all | solution.py:69
  54.7 19.6 %copy-start.1 = (f32[2,16,16,1,4,16]{5,4,3,2,1,0:T(4,128)S(1)}, f32[2,16,16,1,4,16]{5,4,3,2,1,0:T(4,128)}, u32[]{:S(2)}) copy-start(f32[2,16,16,1,4,16]{5,4,3,2,1,0:T(4,128)} %param.9) | copy-start | bytes 393220
  55.5 9.1 %all-to-all-start.2 = ((f32[4,1,2048]{2,1,0:T(1,128)}), f32[4,1,2048]{2,1,0:T(1,128)S(1)}, u32[]{:S(2)}, u32[]{:S(2)}) async-start(f32[4,1,2048]{2,1,0:T(1,128)} %reshape.609), calls=%async_computation.2 | async-start | bytes 65536 | tf_op jit(solution)/shard_map/all_to_all | solution.py:82
  64.6 7.8 %all-to-all-start.3 = ((f32[4,1,2048]{2,1,0:T(1,128)}), f32[4,1,2048]{2,1,0:T(1,128)S(1)}, u32[]{:S(2)}, u32[]{:S(2)}) async-start(f32[4,1,2048]{2,1,0:T(1,128)} %reshape.607), calls=%async_computation.3 | async-start | bytes 65536 | tf_op jit(solution)/shard_map/all_to_all | solution.py:83
  76.8 7.7 %all-to-all-start.5 = ((f32[4,1,2048]{2,1,0:T(1,128)}), f32[4,1,2048]{2,1,0:T(1,128)S(1)}, u32[]{:S(2)}, u32[]{:S(2)}) async-start(f32[4,1,2048]{2,1,0:T(1,128)} %reshape.613), calls=%async_computation.5 | async-start | bytes 65536 | tf_op jit(solution)/shard_map/all_to_all | solution.py:104
  84.6 7.9 %all-to-all-start.4 = ((f32[4,1,2048]{2,1,0:T(1,128)}), f32[4,1,2048]{2,1,0:T(1,128)S(1)}, u32[]{:S(2)}, u32[]{:S(2)}) async-start(f32[4,1,2048]{2,1,0:T(1,128)} %reshape.611), calls=%async_computation.4 | async-start | bytes 65536 | tf_op jit(solution)/shard_map/all_to_all | solution.py:103
  120.3 36.5 %all-to-all-start.7 = ((f32[16,1,4096]{2,1,0:T(1,128)}), f32[16,1,4096]{2,1,0:T(1,128)S(1)}, u32[]{:S(2)}, u32[]{:S(2)}) async-start(f32[16,1,4096]{2,1,0:T(1,128)} %reshape.617), calls=%async_computation.7 | async-start | bytes 524288 | tf_op jit(solution)/shard_map/all_to_all | solution.py:117
  156.8 19.0 %all-to-all-start.6 = ((f32[16,1,4096]{2,1,0:T(1,128)}), f32[16,1,4096]{2,1,0:T(1,128)S(1)}, u32[]{:S(2)}, u32[]{:S(2)}) async-start(f32[16,1,4096]{2,1,0:T(1,128)} %reshape.615), calls=%async_computation.6 | async-start | bytes 524288 | tf_op jit(solution)/shard_map/all_to_all | solution.py:116
  204.6 17.9 %all-to-all-start.9 = ((f32[1,16,16,256]{3,1,0,2:T(8,128)}), f32[1,16,16,256]{3,1,0,2:T(8,128)S(1)}, u32[]{:S(2)}, u32[]{:S(2)}) async-start(f32[1,16,16,256]{3,1,0,2:T(8,128)} %copy.145), calls=%async_computation.9 | async-start | bytes 524288 | tf_op jit(solution)/shard_map/all_to_all | solution.py:70
  222.5 107.5 %all-to-all-start.8 = ((f32[1,16,16,256]{3,1,0,2:T(8,128)}), f32[1,16,16,256]{3,1,0,2:T(8,128)S(1)}, u32[]{:S(2)}, u32[]{:S(2)}) async-start(f32[1,16,16,256]{3,1,0,2:T(8,128)} %copy.141), calls=%async_computation.8 | async-start | bytes 524288 | tf_op jit(solution)/shard_map/all_to_all | solution.py:69
  340.2 8.8 %all-to-all-start.10 = ((f32[4,1,2048]{2,1,0:T(1,128)}), f32[4,1,2048]{2,1,0:T(1,128)S(1)}, u32[]{:S(2)}, u32[]{:S(2)}) async-start(f32[4,1,2048]{2,1,0:T(1,128)} %reshape.621), calls=%async_computation.10 | async-start | bytes 65536 | tf_op jit(solution)/shard_map/all_to_all | solution.py:82
  345.4 13.5 %copy-start.2 = (f32[2,16,16,1,4,16]{5,4,3,2,1,0:T(4,128)S(1)}, f32[2,16,16,1,4,16]{5,4,3,2,1,0:T(4,128)}, u32[]{:S(2)}) copy-start(f32[2,16,16,1,4,16]{5,4,3,2,1,0:T(4,128)} %param.9) | copy-start | bytes 393220
  349.0 7.9 %all-to-all-start.11 = ((f32[4,1,2048]{2,1,0:T(1,128)}), f32[4,1,2048]{2,1,0:T(1,128)S(1)}, u32[]{:S(2)}, u32[]{:S(2)}) async-start(f32[4,1,2048]{2,1,0:T(1,128)} %reshape.619), calls=%async_computation.11 | async-start | bytes 65536 | tf_op jit(solution)/shard_map/all_to_all | solution.py:83
  361.3 7.7 %all-to-all-start.13 = ((f32[4,1,2048]{2,1,0:T(1,128)}), f32[4,1,2048]{2,1,0:T(1,128)S(1)}, u32[]{:S(2)}, u32[]{:S(2)}) async-start(f32[4,1,2048]{2,1,0:T(1,128)} %reshape.625), calls=%async_computation.13 | async-start | bytes 65536 | tf_op jit(solution)/shard_map/all_to_all | solution.py:104
  369.1 7.7 %all-to-all-start.12 = ((f32[4,1,2048]{2,1,0:T(1,128)}), f32[4,1,2048]{2,1,0:T(1,128)S(1)}, u32[]{:S(2)}, u32[]{:S(2)}) async-start(f32[4,1,2048]{2,1,0:T(1,128)} %reshape.623), calls=%async_computation.12 | async-start | bytes 65536 | tf_op jit(solution)/shard_map/all_to_all | solution.py:103
  402.8 13.5 %copy-start.5 = (f32[4,16,16]{2,0,1:T(4,128)S(1)}, f32[4,16,16]{2,0,1:T(4,128)}, u32[]{:S(2)}) copy-start(f32[4,16,16]{2,0,1:T(4,128)} %copy.169) | copy-start | bytes 12292
  402.8 13.5 %copy-start.6 = (f32[4,16,16]{2,0,1:T(4,128)S(1)}, f32[4,16,16]{2,0,1:T(4,128)}, u32[]{:S(2)}) copy-start(f32[4,16,16]{2,0,1:T(4,128)} %copy.171) | copy-start | bytes 12292
  405.8 39.9 %all-to-all-start.15 = ((f32[16,1,4096]{2,1,0:T(1,128)}), f32[16,1,4096]{2,1,0:T(1,128)}, u32[]{:S(2)}, u32[]{:S(2)}) async-start(f32[16,1,4096]{2,1,0:T(1,128)} %reshape.629), calls=%async_computation.15 | async-start | bytes 524288 | tf_op jit(solution)/shard_map/all_to_all | solution.py:117
  442.6 10.8 %copy-start.3 = (f32[1,16,16,1,4,16]{2,1,4,3,0,5:T(8,128)S(1)}, f32[1,16,16,1,4,16]{2,1,4,3,0,5:T(8,128)}, u32[]{:S(2)}) copy-start(f32[1,16,16,1,4,16]{2,1,4,3,0,5:T(8,128)} %get-tuple-element.40) | copy-start | bytes 196612
  442.6 10.8 %copy-start.4 = (f32[1,16,16,1,4,16]{2,1,4,3,0,5:T(8,128)S(1)}, f32[1,16,16,1,4,16]{2,1,4,3,0,5:T(8,128)}, u32[]{:S(2)}) copy-start(f32[1,16,16,1,4,16]{2,1,4,3,0,5:T(8,128)} %get-tuple-element.41) | copy-start | bytes 196612
  445.7 9.3 %copy-start.9 = (f32[16,16]{1,0:T(8,128)S(1)}, f32[16,16]{1,0:T(8,128)}, u32[]{:S(2)}) copy-start(f32[16,16]{1,0:T(8,128)} %get-tuple-element.39) | copy-start | bytes 3076
  445.7 112.6 %all-to-all-start.14 = ((f32[16,1,4096]{2,1,0:T(1,128)}), f32[16,1,4096]{2,1,0:T(1,128)S(1)}, u32[]{:S(2)}, u32[]{:S(2)}) async-start(f32[16,1,4096]{2,1,0:T(1,128)} %reshape.627), calls=%async_computation.14 | async-start | bytes 524288 | tf_op jit(solution)/shard_map/all_to_all | solution.py:116
  453.1 93.9 %reduce-scatter.2.cloned.1.call-start = ((), (), s32[]{:S(2)}) async-start(), calls=%async_computation.17 | async-start | bytes 1179648 | tf_op jit(solution)/shard_map/reduce_scatter | solution.py:160
  (8 other events, 18.7 us)
Sparse Core Ops, SparseCore 0:
  459.0 87.8 reduce-scatter.1
where the time goes:
time: 594 us; the launch traced here: 584 us
  waiting for transfers between devices  135 us (23%)
  other arithmetic  98.6 us (17%)
  blocking collectives  97.4 us (16%)
  local copies, waits for them, and re-layouts  93.8 us (16%)
  starting transfers between devices  88.2 us (15%)
  matrix products  56.4 us (9%)
  between operations  15.4 us (3%)
    psum x1, blocking collectives, shards(): lax.psum((skip_grad, bias_grad, inner_grad, outer_grad), ('batch', 'px',...  97.4 us
    reduce_scatter x1, waiting for transfers between devices, shards(): lax.psum_scatter(jnp.stack([part_real, part_imaginary]), 'batch', scatter...  91.3 us
    unnamed x6, other arithmetic  82.8 us
    unnamed x62, local copies, waits for them, and re-layouts  45.4 us
    dot_general x36, matrix products, exact(): return jnp.einsum(pattern, left_operand, right_operand, precision=precise)  40.8 us
    another operation x16, local copies, waits for them, and re-layouts  20.5 us
    all_to_all x2, starting transfers between devices, inverse(): lax.all_to_all(second_imaginary, 'py', split_axis=3, concat_axis=2, tiled...  19 us
    all_to_all x2, starting transfers between devices, forward(): lax.all_to_all(depth_imaginary, 'py', split_axis=2, concat_axis=3, tiled=...  18.1 us
  transfers between devices with their start and end apart: 17, of which 13 were waited for; matrix products, arithmetic and copies ran while one was open for 20% of the time, Pallas kernels for 0%

commit v1 on v0

v1 whole, which is shorter than its diff:
```python
import math

import jax
import jax.numpy as jnp
import ml_dtypes
import numpy as np
from jax import lax
from jax.experimental import pallas as pl
from jax.experimental.pallas import tpu as pltpu
from jax.sharding import PartitionSpec as P

f32 = jnp.float32
bf16 = jnp.bfloat16
C = 16
N = 128
PX, PY, NB = 4, 16, 8
XL, YL = N // PX, N // PY
XY = XL * YL
ML = C // PX
PEERS = PX * PY
LANES = 128
SIGMA = 1.0 / math.sqrt(N**3)
RHO = 1.0 / math.sqrt(NB * N**3)
NT = (((1,), (1,)), ((), ()))


def tables():
    turn = lambda r, n: 2.0 * np.pi * (np.mod(r, n) / n)
    freq = np.where(np.arange(C) < C // 2, np.arange(C), np.arange(C) - C)
    depth = turn(np.arange(C)[:, None] * np.arange(N)[None, :], N)
    cos_z, sin_z = np.cos(depth), np.sin(depth)
    low = np.concatenate([cos_z, -sin_z]).astype(ml_dtypes.bfloat16)
    ax = turn(np.arange(XL)[:, None] * freq[None, :], N)
    ay = turn(np.arange(YL)[:, None] * freq[None, :], N)
    phase = ax[:, None, None, :] + ay[None, :, :, None]
    phase = phase.reshape(XY, PX, ML * C)
    co, si = np.cos(phase), np.sin(phase)
    upper = np.stack([co, -si], axis=2)
    lower = np.stack([si, co], axis=2)
    plane = np.concatenate([upper, lower]).reshape(2 * XY, PX * 2 * ML * C)
    plane_hi = plane.astype(ml_dtypes.bfloat16)
    plane_lo = (plane - plane_hi.astype(np.float64)).astype(ml_dtypes.bfloat16)
    ox = turn(np.arange(PX)[:, None] * XL * freq[None, :], N)
    oy = turn(np.arange(PY)[:, None] * YL * freq[None, :], N)
    off = ox[:, None, None, :] + oy[None, :, :, None]
    off = off.reshape(PEERS, PX, ML * C)
    cs = np.concatenate([np.cos(off), np.cos(off)], axis=2)
    sn = np.concatenate([np.sin(off), -np.sin(off)], axis=2)
    offset = (np.concatenate([cs, sn], axis=1) * SIGMA).astype(np.float32)
    eye = np.eye(8)
    synth = np.concatenate(
        [
            np.einsum("ab,kz->akbz", eye, cos_z).reshape(8 * C, 8 * N),
            np.einsum("ab,kz->akbz", eye, -sin_z).reshape(8 * C, 8 * N),
        ]
    ).astype(ml_dtypes.bfloat16)
    return low, plane_hi, plane_lo, offset, synth


def dot(a, b):
    return jnp.dot(a, b, preferred_element_type=f32)


def dot_nt(a, b):
    return lax.dot_general(a, b, NT, preferred_element_type=f32)


def split(a):
    hi = a.astype(bf16)
    return hi, (a - hi.astype(f32)).astype(bf16)


def my_offset(offset_ref):
    me = lax.axis_index("px") * PY + lax.axis_index("py")
    return offset_ref[me]


def forward_part(get, low_ref, hi_ref, lo_ref, offset_ref, turn_ref, out_ref):
    low = low_ref[...]
    rows = []
    for c in range(C):
        z = dot_nt(low, get(c))
        rows.append(jnp.concatenate([z[:C], z[C:]], axis=1))
    x_hi, x_lo = split(jnp.concatenate(rows, axis=0))
    off = my_offset(offset_ref)
    for mb in range(PX):
        cols = slice(mb * LANES, (mb + 1) * LANES)
        hi = hi_ref[:, cols]
        part = dot(x_hi, hi) + dot(x_lo, hi) + dot(x_hi, lo_ref[:, cols])
        turned = part * off[mb] + pltpu.roll(part, LANES // 2, 1) * off[PX + mb]
        turn_ref[mb] = turned
    for mb in range(PX):
        for k in range(C):
            out_ref[mb * PY + k, 0:C, :] = turn_ref[mb, pl.ds(k, C, stride=C), :]


def inverse_part(recv_ref, hi_ref, lo_ref, offset_ref, synth_ref, turn_ref, g_ref):
    off = my_offset(offset_ref)
    for mb in range(PX):
        v = recv_ref[mb * PY : (mb + 1) * PY].reshape(PY * C, LANES)
        turn_ref[mb] = v * off[mb] - pltpu.roll(v, LANES // 2, 1) * off[PX + mb]
    rows = []
    for o in range(C):
        rows.append(
            jnp.concatenate(
                [turn_ref[mb, pl.ds(o, C, stride=C), :] for mb in range(PX)], axis=1
            )
        )
    v_hi, v_lo = split(jnp.concatenate(rows, axis=0))
    hi = hi_ref[...]
    z = dot_nt(hi, v_hi) + dot_nt(hi, v_lo) + dot_nt(lo_ref[...], v_hi)
    z = z.astype(bf16)
    for ob in range(2):
        cols = slice(ob * LANES, (ob + 1) * LANES)
        zb = jnp.concatenate([z[:XY, cols], z[XY:, cols]], axis=1)
        g = dot(zb, synth_ref[...])
        for o in range(8):
            g_ref[ob * 8 + o] = g[:, o * N : (o + 1) * N]


def k_forward(field_ref, low_ref, hi_ref, lo_ref, offset_ref, out_ref, turn_ref):
    forward_part(
        lambda c: field_ref[c], low_ref, hi_ref, lo_ref, offset_ref, turn_ref, out_ref
    )


def k_mix(recv_ref, wa_ref, wb_ref, u_ref, out_ref):
    u = jnp.sum(recv_ref[...], axis=0)
    us = pltpu.roll(u, LANES // 2, 1)
    u_ref[...] = u
    v = jnp.zeros((C, LANES), f32)
    for c in range(C):
        v = v + wa_ref[c] * u[c : c + 1, :] + wb_ref[c] * us[c : c + 1, :]
    out_ref[...] = jnp.broadcast_to(v[None], (PEERS, C, LANES))


def gelu_parts(x):
    a = math.sqrt(2.0 / math.pi)
    b = a * 0.044715
    x2 = x * x
    h = 0.5 * jnp.tanh(x * (a + b * x2)) + 0.5
    g = x * h
    d = h + g * (1.0 - h) * (2.0 * a + (6.0 * b) * x2)
    return g, d


def tile(ref, p):
    left = ref[:, pl.ds(p * 32, 16), :].reshape(C * 16, N)
    right = ref[:, pl.ds(p * 32 + 16, 16), :].reshape(C * 16, N)
    return jnp.concatenate([left, right], axis=1)


def untile(ref, p, value):
    ref[:, pl.ds(p * 32, 16), :] = value[:, :N].reshape(C, 16, N)
    ref[:, pl.ds(p * 32 + 16, 16), :] = value[:, N:].reshape(C, 16, N)


def pack_rows(acc):
    r = lax.broadcasted_iota(jnp.int32, (256, 256), 0)
    l = lax.broadcasted_iota(jnp.int32, (256, 256), 1)
    kept = jnp.where(r % 16 == l % 16, acc, 0.0).reshape(C, 16, 256).sum(axis=1)
    r = lax.broadcasted_iota(jnp.int32, (256, LANES), 0)
    l = lax.broadcasted_iota(jnp.int32, (256, LANES), 1)
    pick = jnp.where(r // 16 == l % 16, 1.0, 0.0)
    spread = jnp.dot(kept, pick, precision=lax.Precision.HIGHEST, preferred_element_type=f32)
    r = lax.broadcasted_iota(jnp.int32, (C, LANES), 0)
    l = lax.broadcasted_iota(jnp.int32, (C, LANES), 1)
    spread = jnp.where(r % 8 == l // 16, spread, 0.0)
    return spread.reshape(2, 8, LANES).sum(axis=1)


def k_middle(
    recv_ref, field_ref, cot_ref, kron_ref, bias_ref, low_ref, hi_ref, lo_ref, offset_ref, synth_ref,
    out_ref, dpre_ref,
    turn_ref, g_ref, skip_acc, bias_acc, in_acc, out_acc,
):
    inverse_part(recv_ref, hi_ref, lo_ref, offset_ref, synth_ref, turn_ref, g_ref)
    skip_acc[...] = jnp.zeros_like(skip_acc)
    in_acc[...] = jnp.zeros_like(in_acc)
    out_acc[...] = jnp.zeros_like(out_acc)
    bias_acc[...] = jnp.zeros_like(bias_acc)

    def step(p, carry):
        f = tile(field_ref, p)
        cot = tile(cot_ref, p)
        pre = tile(g_ref, p) + dot(kron_ref[0], f) + bias_ref[...]
        hid, d_hid = gelu_parts(pre)
        hid = hid.astype(bf16)
        act, d_act = gelu_parts(dot(kron_ref[1], hid))
        act = act.astype(bf16)
        d_inner = (dot(kron_ref[2], cot) * d_act).astype(bf16)
        dpre = dot(kron_ref[3], d_inner) * d_hid
        dpre = dpre.astype(bf16)
        untile(dpre_ref, p, dpre)
        skip_acc[...] += dot_nt(dpre, f)
        in_acc[...] += dot_nt(d_inner, hid)
        out_acc[...] += dot_nt(cot, act)
        bias_acc[...] += dpre.astype(f32)
        return carry

    lax.fori_loop(0, XY // 32, step, 0)
    forward_part(
        lambda c: dpre_ref[c], low_ref, hi_ref, lo_ref, offset_ref, turn_ref, out_ref
    )
    bias = bias_acc[...].reshape(C, 16, 256).sum(axis=1)
    total = jnp.sum(bias, axis=1, keepdims=True)
    r = lax.broadcasted_iota(jnp.int32, (C, LANES), 0)
    l = lax.broadcasted_iota(jnp.int32, (C, LANES), 1)
    bias_row = jnp.sum(jnp.where(r == l, total, 0.0), axis=0, keepdims=True)
    small = jnp.concatenate(
        [pack_rows(skip_acc[...]), pack_rows(in_acc[...]), pack_rows(out_acc[...]),
         bias_row, jnp.zeros((1, LANES), f32)], axis=0
    )
    out_ref[:, C : C + 8, :] = jnp.broadcast_to(small[None], (PEERS, 8, LANES))


def k_mix_back(recv_ref, u_ref, wa_ref, wb_ref, out_ref, share_ref):
    got = jnp.sum(recv_ref[...], axis=0)
    g = got[:C]
    gs = pltpu.roll(g, LANES // 2, 1)
    rows = []
    for c in range(C):
        rows.append(jnp.sum(wa_ref[c] * g - wb_ref[c] * gs, axis=0, keepdims=True))
    du = jnp.concatenate(rows, axis=0)
    out_ref[...] = jnp.broadcast_to(du[None], (PEERS, C, LANES))
    share = jnp.concatenate([u_ref[...], got], axis=0)
    share_ref[...] = jnp.broadcast_to(share[None], (NB, 2 * C + 8, LANES))


def k_input(recv_ref, dpre_ref, kron_ref, hi_ref, lo_ref, offset_ref, synth_ref, out_ref, turn_ref, g_ref):
    inverse_part(recv_ref, hi_ref, lo_ref, offset_ref, synth_ref, turn_ref, g_ref)

    def step(p, carry):
        untile(out_ref, p, (dot(kron_ref[4], tile(dpre_ref, p)) + tile(g_ref, p)).astype(bf16))
        return carry

    lax.fori_loop(0, XY // 32, step, 0)


def k_shared(recv_ref, spec_ref, skip_ref, bias_ref, in_ref, outer_ref, pa_ref, pb_ref):
    for c in range(C):
        pa = jnp.zeros((C, LANES), f32)
        pb = jnp.zeros((C, LANES), f32)
        for s in range(NB):
            u = recv_ref[s, c : c + 1, :]
            g = recv_ref[s, C : 2 * C, :]
            pa = pa + u * g
            pb = pb + u * pltpu.roll(g, LANES // 2, 1)
        pa_ref[c * C : (c + 1) * C, :] = pa
        pb_ref[c * C : (c + 1) * C, :] = pb
    b = lax.axis_index("batch")
    r = lax.broadcasted_iota(jnp.int32, (8, LANES), 0)
    l = lax.broadcasted_iota(jnp.int32, (8, LANES), 1)
    mine = ((l % 64) // C == r // 2) & (l % C == 2 * b + r % 2)
    sel_a = jnp.where(mine, 1.0, 0.0)
    sel_b = jnp.where(l < 64, sel_a, -sel_a)
    full = lambda x, y: lax.dot_general(
        x, y, NT, precision=lax.Precision.HIGHEST, preferred_element_type=f32
    )
    spec_ref[0] = full(sel_a, pa_ref[...])
    spec_ref[1] = full(sel_b, pb_ref[...])
    small = jnp.sum(recv_ref[:, 2 * C :, :], axis=0) * RHO
    r = lax.broadcasted_iota(jnp.int32, (C, LANES), 0)
    l = lax.broadcasted_iota(jnp.int32, (C, LANES), 1)
    pr = lax.broadcasted_iota(jnp.int32, (LANES, C), 0)
    pc = lax.broadcasted_iota(jnp.int32, (LANES, C), 1)
    pick = jnp.where(pr % C == pc, 1.0, 0.0)
    for i, ref in enumerate((skip_ref, in_ref, outer_ref)):
        two = jnp.concatenate(
            [jnp.broadcast_to(small[2 * i + h : 2 * i + h + 1], (8, LANES)) for h in range(2)], axis=0
        )
        two = jnp.where(l // C == r % 8, two, 0.0)
        ref[...] = jnp.dot(two, pick, precision=lax.Precision.HIGHEST, preferred_element_type=f32)
    bias_ref[...] = jnp.broadcast_to(small[6:7], (8, LANES))


def call(body, name, outs, scratch, *args):
    vm = pl.BlockSpec(memory_space=pltpu.VMEM)
    many = isinstance(outs, (list, tuple))
    return pl.pallas_call(
        body,
        out_shape=outs,
        in_specs=[vm] * len(args),
        out_specs=[vm] * len(outs) if many else vm,
        scratch_shapes=scratch,
        compiler_params=pltpu.CompilerParams(vmem_limit_bytes=48 * 2**20),
        name=name,
    )(*args)


def shape(*dims, dtype=f32):
    return jax.ShapeDtypeStruct(dims, dtype)


def shards(field, cotangent, spec_weight, skip_weight, skip_bias, mlp_in, mlp_out):
    low, hi, lo, offset, synth = [jnp.asarray(t) for t in tables()]
    field = field.reshape(C, XY, N)
    cotangent = cotangent.reshape(C, XY, N)
    weight = spec_weight.reshape(2, C, C, ML * C)
    wa = jnp.concatenate([weight[0], weight[0]], axis=2)
    wb = jnp.concatenate([-weight[1], weight[1]], axis=2)
    maps = jnp.stack([skip_weight, mlp_in, mlp_out.T, mlp_in.T, skip_weight.T])
    same = jnp.eye(16, dtype=bf16)
    kron = (maps[:, :, None, :, None] * same[None, None, :, None, :]).reshape(5, 256, 256)
    bias = jnp.broadcast_to(skip_bias[:, None, None], (C, 16, 2 * N)).reshape(256, 2 * N)
    turn = pltpu.VMEM((PX, PY * C, LANES), f32)
    cells = pltpu.VMEM((C, XY, N), f32)
    square = pltpu.VMEM((256, 256), f32)

    def exchange(block):
        return lax.all_to_all(block, ("px", "py"), 0, 0, tiled=True)

    sent = call(k_forward, "forward", shape(PEERS, C, LANES), [turn], field, low, hi, lo, offset)
    u, sent = call(
        k_mix, "mix", [shape(C, LANES), shape(PEERS, C, LANES)], [], exchange(sent), wa, wb
    )
    sent, dpre = call(
        k_middle, "middle",
        [shape(PEERS, C + 8, LANES), shape(C, XY, N, dtype=bf16)],
        [turn, cells, square, square, square, square],
        exchange(sent), field, cotangent, kron, bias, low, hi, lo, offset, synth,
    )
    sent, share = call(
        k_mix_back, "mix_back",
        [shape(PEERS, C, LANES), shape(NB, 2 * C + 8, LANES)],
        [], exchange(sent), u, wa, wb,
    )
    back = exchange(sent)
    share = lax.all_to_all(share, "batch", 0, 0, tiled=True)
    grad_input = call(
        k_input, "input_grad", shape(C, XY, N, dtype=bf16), [turn, cells],
        back, dpre, kron, hi, lo, offset, synth,
    )
    spec, skip, b, inner, outer = call(
        k_shared, "shared",
        [shape(2, 8, 256), shape(C, C), shape(8, LANES), shape(C, C), shape(C, C)],
        [pltpu.VMEM((256, LANES), f32)] * 2, share,
    )
    spec = spec.reshape(2, ML, 2, C, C).transpose(0, 3, 4, 1, 2).reshape(2, C, C, 1, ML, 2)
    return (grad_input.reshape(1, C, XL, YL, N), spec, skip, b[0, :C], inner, outer)


def solution(mesh):
    placed = (
        P("batch", None, "px", "py", None),
        P("batch", None, "px", "py", None),
        P(None, None, None, "py", "px", None),
        P(),
        P(),
        P(),
        P(),
    )
    return jax.shard_map(
        shards,
        mesh=mesh,
        in_specs=placed,
        out_specs=(
            P("batch", None, "px", "py", None),
            P(None, None, None, "py", "px", "batch"),
            P(),
            P(),
            P(),
            P(),
        ),
        check_vma=False,
    )
```

time: 594 us -> 161 us (0.27); the launches traced: 584 us -> 160 us
  waiting for transfers between devices: 135 us -> 29.8 us
  other arithmetic: 98.6 us -> 1.31 us
  local copies, waits for them, and re-layouts: 93.8 us -> 27.6 us
  starting transfers between devices: 88.2 us -> 29.9 us
  matrix products: 56.4 us -> 0 us
  blocking collectives: 97.4 us -> 49.2 us
  Pallas kernels: 0 us -> 21.2 us
  between operations: 15.4 us -> 0.89 us
    psum x1 -> x0, blocking collectives: 97.4 us -> none  [shards(): lax.psum((skip_grad, bias_grad, inner_grad, outer_grad), ('batch', 'px',...]
    reduce_scatter x1 -> x0, waiting for transfers between devices: 91.3 us -> none  [shards(): lax.psum_scatter(jnp.stack([part_real, part_imaginary]), 'batch', scatter...]
    unnamed x6 -> x0, other arithmetic: 82.8 us -> none
    all_to_all x16 -> x3, starting transfers between devices: 87.9 us -> 29.9 us  [exchange(): return lax.all_to_all(block, ('px', 'py'), 0, 0, tiled=True)]
    dot_general x48 -> x0, matrix products: 56.4 us -> none  [the longest x36 40.8 us: exact(): return jnp.einsum(pattern, left_operand, right_operand, precision=precise)]
    all_to_all x0 -> x2, blocking collectives: none -> 49.2 us  [the longest x1 33.2 us: exchange(): return lax.all_to_all(block, ('px', 'py'), 0, 0, tiled=True)]
    unnamed x62 -> x50, local copies, waits for them, and re-layouts: 45.4 us -> 8.17 us
    pallas_call x0 -> x6, Pallas kernels: none -> 21.2 us  [call(): pl.pallas_call(body, out_shape=outs, in_specs=[vm] * len(args), out_specs...]
  transfers between devices with their start and end apart: 17 -> 3, of which waited for: 13 -> 3; matrix products, arithmetic and copies ran while one was open for 20% -> 13% of each run, Pallas kernels for 0% -> 1%
where the time goes in v1:
time: 161 us; the launch traced here: 160 us
  blocking collectives  49.2 us (31%)
  starting transfers between devices  29.9 us (19%)
  waiting for transfers between devices  29.8 us (19%)
  local copies, waits for them, and re-layouts  27.6 us (17%)
  Pallas kernels  21.2 us (13%)
    all_to_all x1, blocking collectives, exchange(): return lax.all_to_all(block, ('px', 'py'), 0, 0, tiled=True)  33.2 us
    all_to_all x3, starting transfers between devices, exchange(): return lax.all_to_all(block, ('px', 'py'), 0, 0, tiled=True)  29.9 us
    all_to_all x3, waiting for transfers between devices, exchange(): return lax.all_to_all(block, ('px', 'py'), 0, 0, tiled=True)  29.8 us
    pallas_call x6, Pallas kernels, call(): pl.pallas_call(body, out_shape=outs, in_specs=[vm] * len(args), out_specs...  21.2 us
    all_to_all x1, blocking collectives, shards(): share = lax.all_to_all(share, 'batch', 0, 0, tiled=True)  16.1 us
    mul x4, local copies, waits for them, and re-layouts, shards(): maps[:, :, None, :, None] * same[None, None, :, None, :]  14.6 us
    unnamed x50, local copies, waits for them, and re-layouts  8.17 us
  transfers between devices with their start and end apart: 3, of which 3 were waited for; matrix products, arithmetic and copies ran while one was open for 13% of the time, Pallas kernels for 1%

profile of v1, /device:TPU:1, one launch (start us, length us, event | category | flops | bytes accessed | tf_op | source)
XLA Modules:
  0.0 159.8 jit_solution(3358098140524254595)
XLA Ops:
  0.6 1.0 copy-done
  1.7 1.0 copy-done.2
  2.7 1.2 copy-done.4
  3.9 0.9 copy-done.6
  5.6 2.3 %forward.1 = f32[64,16,128]{2,1,0:T(8,128)} custom-call(bf16[16,256,128]{2,1,0:T(8,128)(2,1)S(1)} %bitcast.30, bf16[32,128]{1,0:T(8,128)(2,1)S(1)} %copy-done.16, bf16[512,512]{1,0:T(8,128)(2,1)S(1)} %copy-done, bf16[512,512]{1,0:T(8,128)(2,1)S(1)} %copy-done.2, f32[64,8,128]{2,1,0:T(8,128)S(1)} %copy-done.6), custom_call_target="tpu_custom_call" | custom-call | tf_op jit(solution)/shard_map/forward/pallas_call | solution.py:280
  7.9 15.4 %all-to-all-start = ((f32[64,16,128]{2,1,0:T(8,128)}), f32[64,16,128]{2,1,0:T(8,128)S(1)}, u32[]{:S(2)}, u32[]{:S(2)}) async-start(f32[64,16,128]{2,1,0:T(8,128)} %forward.1), calls=%async_computation | async-start | bytes 1048576 | tf_op jit(solution)/shard_map/all_to_all | solution.py:311
  23.3 1.3 fusion.1
  25.5 15.0 %all-to-all-done.recv_ref = f32[64,16,128]{2,1,0:T(8,128)S(1)} async-done(((f32[64,16,128]{2,1,0:T(8,128)}), f32[64,16,128]{2,1,0:T(8,128)S(1)}, u32[]{:S(2)}, u32[]{:S(2)}) %all-to-all-start) | async-done | bytes 524320 | tf_op jit(solution)/shard_map/all_to_all | solution.py:311
  40.5 1.0 mix.1
  41.5 6.3 %all-to-all-start.1 = ((f32[64,16,128]{2,1,0:T(8,128)}), f32[64,16,128]{2,1,0:T(8,128)}, u32[]{:S(2)}, u32[]{:S(2)}) async-start(f32[64,16,128]{2,1,0:T(8,128)} %get-tuple-element.17), calls=%async_computation.1 | async-start | bytes 1048576 | tf_op jit(solution)/shard_map/all_to_all | solution.py:311
  47.9 3.1 %mul.20 = bf16[5,16,16,16,16]{4,3,2,1,0:T(8,128)(2,1)} broadcast(bf16[5,16,16]{2,1,0:T(8,128)(2,1)S(1)} %copy.20), dimensions={0,1,3} | broadcast | bytes 657920 | tf_op jit(solution)/shard_map/mul | solution.py:304
  51.0 7.6 %mul.21 = bf16[5,256,256]{2,1,0:T(8,128)(2,1)} reshape(bf16[5,16,16,16,16]{4,3,2,1,0:T(8,128)(2,1)} %mul.20) | data formatting | bytes 1310720 | tf_op jit(solution)/shard_map/mul | solution.py:304
  58.6 1.2 mul.22
  59.8 2.8 %mul.23 = bf16[256,256]{1,0:T(8,128)(2,1)} reshape(bf16[16,16,16,16]{3,2,1,0:T(8,128)(2,1)} %mul.22) | data formatting | bytes 262144 | tf_op jit(solution)/shard_map/mul | solution.py:304
  63.3 1.2 broadcast_multiply_fusion.kron_ref
  65.7 12.1 %middle.1 = (f32[64,24,128]{2,1,0:T(8,128)S(1)}, bf16[16,256,128]{2,1,0:T(8,128)(2,1)S(1)}) custom-call(f32[64,16,128]{2,1,0:T(8,128)} %all-to-all-done.1.recv_ref, bf16[16,256,128]{2,1,0:T(8,128)(2,1)S(1)} %bitcast.31, bf16[16,256,128]{2,1,0:T(8,128)(2,1)} %bitcast.33, bf16[5,256,256]{2,1,0:T(8,128)(2,1)S(1)} %broadcast_multiply_fusion.kron_ref, ...), custom_call_target="tpu_custom_call" | custom-call | tf_op jit(solution)/shard_map/middle/pallas_call | solution.py:280
  77.9 1.0 copy-done.13
  78.9 33.2 %all_to_all.25.recv_ref = f32[64,24,128]{2,1,0:T(8,128)S(1)} all-to-all(f32[64,24,128]{2,1,0:T(8,128)S(1)} %get-tuple-element.18), channel_id=1, replica_groups=mesh['batch'=8,'px'=4,'py'=16] {'px','py'}, dimensions={0} | all-to-all | bytes 1572864 | tf_op jit(solution)/shard_map/all_to_all | solution.py:311
  113.0 16.1 %all_to_all.26.recv_ref = f32[8,40,128]{2,1,0:T(8,128)S(1)} all-to-all(f32[8,40,128]{2,1,0:T(8,128)S(1)} %get-tuple-element.22), channel_id=1, replica_groups=mesh['batch'=8,'px'=4,'py'=16] {'batch'}, dimensions={0} | all-to-all | bytes 327680 | tf_op jit(solution)/shard_map/all_to_all | solution.py:329
  129.1 8.2 %all-to-all-start.3 = ((f32[64,16,128]{2,1,0:T(8,128)}), f32[64,16,128]{2,1,0:T(8,128)S(1)}, u32[]{:S(2)}, u32[]{:S(2)}) async-start(f32[64,16,128]{2,1,0:T(8,128)} %copy-done.15), calls=%async_computation.3 | async-start | bytes 1048576 | tf_op jit(solution)/shard_map/all_to_all | solution.py:311
  137.2 1.4 shared.1
  139.9 14.5 %all-to-all-done.3.recv_ref = f32[64,16,128]{2,1,0:T(8,128)S(1)} async-done(((f32[64,16,128]{2,1,0:T(8,128)}), f32[64,16,128]{2,1,0:T(8,128)S(1)}, u32[]{:S(2)}, u32[]{:S(2)}) %all-to-all-start.3) | async-done | bytes 524320 | tf_op jit(solution)/shard_map/all_to_all | solution.py:311
  154.4 1.2 copy-done.14
  155.6 4.2 %input_grad.1 = bf16[16,256,128]{2,1,0:T(8,128)(2,1)} custom-call(f32[64,16,128]{2,1,0:T(8,128)S(1)} %all-to-all-done.3.recv_ref, bf16[16,256,128]{2,1,0:T(8,128)(2,1)S(1)} %copy-done.14, bf16[5,256,256]{2,1,0:T(8,128)(2,1)S(1)} %broadcast_multiply_fusion.kron_ref, bf16[512,512]{1,0:T(8,128)(2,1)S(1)} %copy-done.1, bf16[512,512]{1,0:T(8,128)(2,1)S(1)} %copy-done.3, ...), custom_call_target="tpu_custom_call" | custom-call | tf_op jit(solution)/shard_map/input_grad/pallas_call | solution.py:280
  (59 shorter events, 5.9 us)
Async XLA Ops:
  0.6 1.0 copy-start
  1.7 1.0 copy-start.2
  2.7 1.2 copy-start.4
  3.9 0.9 copy-start.6
  5.6 19.5 %copy-start.19 = (bf16[16,16]{1,0:T(8,128)(2,1)S(1)}, bf16[16,16]{1,0:T(8,128)(2,1)}, u32[]{:S(2)}) copy-start(bf16[16,16]{1,0:T(8,128)(2,1)} %param.15) | copy-start | bytes 1540
  5.6 19.6 %copy-start.18 = (bf16[16,16]{1,0:T(8,128)(2,1)S(1)}, bf16[16,16]{1,0:T(8,128)(2,1)}, u32[]{:S(2)}) copy-start(bf16[16,16]{1,0:T(8,128)(2,1)} %param.17) | copy-start | bytes 1540
  5.6 42.2 %copy-start.20 = (bf16[16,16]{1,0:T(8,128)(2,1)S(1)}, bf16[16,16]{1,0:T(8,128)(2,1)}, u32[]{:S(2)}) copy-start(bf16[16,16]{1,0:T(8,128)(2,1)} %param.18) | copy-start | bytes 1540
  7.9 32.6 %all-to-all-start = ((f32[64,16,128]{2,1,0:T(8,128)}), f32[64,16,128]{2,1,0:T(8,128)S(1)}, u32[]{:S(2)}, u32[]{:S(2)}) async-start(f32[64,16,128]{2,1,0:T(8,128)} %forward.1), calls=%async_computation | async-start | bytes 1048576 | tf_op jit(solution)/shard_map/all_to_all | solution.py:311
  25.5 22.4 %copy-start.11 = (f32[16,16,128]{2,1,0:T(8,128)}, f32[16,16,128]{2,1,0:T(8,128)S(1)}, u32[]{:S(2)}) copy-start(f32[16,16,128]{2,1,0:T(8,128)S(1)} %get-tuple-element.31.wb_ref) | copy-start | bytes 393220
  25.5 33.1 %copy-start.9 = (f32[16,16,128]{2,1,0:T(8,128)}, f32[16,16,128]{2,1,0:T(8,128)S(1)}, u32[]{:S(2)}) copy-start(f32[16,16,128]{2,1,0:T(8,128)S(1)} %get-tuple-element.30.wa_ref) | copy-start | bytes 393220
  41.5 23.4 %all-to-all-start.1 = ((f32[64,16,128]{2,1,0:T(8,128)}), f32[64,16,128]{2,1,0:T(8,128)}, u32[]{:S(2)}, u32[]{:S(2)}) async-start(f32[64,16,128]{2,1,0:T(8,128)} %get-tuple-element.17), calls=%async_computation.1 | async-start | bytes 1048576 | tf_op jit(solution)/shard_map/all_to_all | solution.py:311
  51.0 11.6 %copy-start.21 = (f32[16]{0:T(128)S(1)}, f32[16]{0:T(128)}, u32[]{:S(2)}) copy-start(f32[16]{0:T(128)} %param.16) | copy-start | bytes 196
  51.0 14.7 %copy-start.1 = (bf16[512,512]{1,0:T(8,128)(2,1)S(1)}, bf16[512,512]{1,0:T(8,128)(2,1)}, u32[]{:S(2)}) copy-start(bf16[512,512]{1,0:T(8,128)(2,1)} %constant.11.clone.hi_ref) | copy-start | bytes 1572868
  51.0 14.7 %copy-start.3 = (bf16[512,512]{1,0:T(8,128)(2,1)S(1)}, bf16[512,512]{1,0:T(8,128)(2,1)}, u32[]{:S(2)}) copy-start(bf16[512,512]{1,0:T(8,128)(2,1)} %constant.12.clone.lo_ref) | copy-start | bytes 1572868
  51.0 14.7 %copy-start.5 = (bf16[1,16,32,8,128]{4,3,2,1,0:T(8,128)(2,1)S(1)}, bf16[1,16,32,8,128]{4,3,2,1,0:T(8,128)(2,1)}, u32[]{:S(2)}) copy-start(bf16[1,16,32,8,128]{4,3,2,1,0:T(8,128)(2,1)} %param.12) | copy-start | bytes 3145732
  51.0 14.7 %copy-start.7 = (f32[64,8,128]{2,1,0:T(8,128)S(1)}, f32[64,8,128]{2,1,0:T(8,128)}, u32[]{:S(2)}) copy-start(f32[64,8,128]{2,1,0:T(8,128)} %constant.13.clone.offset_ref) | copy-start | bytes 786436
  51.0 14.7 %copy-start.8 = (bf16[256,1024]{1,0:T(8,128)(2,1)S(1)}, bf16[256,1024]{1,0:T(8,128)(2,1)}, u32[]{:S(2)}) copy-start(bf16[256,1024]{1,0:T(8,128)(2,1)} %constant.14.clone.synth_ref) | copy-start | bytes 1572868
  51.0 14.7 %copy-start.17 = (bf16[32,128]{1,0:T(8,128)(2,1)S(1)}, bf16[32,128]{1,0:T(8,128)(2,1)}, u32[]{:S(2)}) copy-start(bf16[32,128]{1,0:T(8,128)(2,1)} %constant.10.clone.low_ref) | copy-start | bytes 24580
  64.8 47.2 %copy-start.10 = (f32[16,16,128]{2,1,0:T(8,128)S(1)}, f32[16,16,128]{2,1,0:T(8,128)}, u32[]{:S(2)}) copy-start(f32[16,16,128]{2,1,0:T(8,128)} %copy-done.9) | copy-start | bytes 393220
  64.8 47.2 %copy-start.12 = (f32[16,16,128]{2,1,0:T(8,128)S(1)}, f32[16,16,128]{2,1,0:T(8,128)}, u32[]{:S(2)}) copy-start(f32[16,16,128]{2,1,0:T(8,128)} %copy-done.11) | copy-start | bytes 393220
  77.9 1.0 copy-start.13
  112.2 0.8 copy-start.15
  129.1 25.3 %all-to-all-start.3 = ((f32[64,16,128]{2,1,0:T(8,128)}), f32[64,16,128]{2,1,0:T(8,128)S(1)}, u32[]{:S(2)}, u32[]{:S(2)}) async-start(f32[64,16,128]{2,1,0:T(8,128)} %copy-done.15), calls=%async_computation.3 | async-start | bytes 1048576 | tf_op jit(solution)/shard_map/all_to_all | solution.py:311
  154.4 1.2 copy-start.14
  (1 other events, 0.7 us)

commit v2 on v1

--- a/solution.py
+++ b/solution.py
@@ -18,6 +18,8 @@
 XY = XL * YL
 ML = C // PX
 PEERS = PX * PY
+SMALL = 7
+ROWS = C + SMALL
 LANES = 128
 SIGMA = 1.0 / math.sqrt(N**3)
 RHO = 1.0 / math.sqrt(NB * N**3)
@@ -35,9 +37,7 @@
     phase = ax[:, None, None, :] + ay[None, :, :, None]
     phase = phase.reshape(XY, PX, ML * C)
     co, si = np.cos(phase), np.sin(phase)
-    upper = np.stack([co, -si], axis=2)
-    lower = np.stack([si, co], axis=2)
-    plane = np.concatenate([upper, lower]).reshape(2 * XY, PX * 2 * ML * C)
+    plane = np.stack([co, -si], axis=2).reshape(XY, PX * LANES)
     plane_hi = plane.astype(ml_dtypes.bfloat16)
     plane_lo = (plane - plane_hi.astype(np.float64)).astype(ml_dtypes.bfloat16)
     ox = turn(np.arange(PX)[:, None] * XL * freq[None, :], N)
@@ -45,7 +45,7 @@
     off = ox[:, None, None, :] + oy[None, :, :, None]
     off = off.reshape(PEERS, PX, ML * C)
     cs = np.concatenate([np.cos(off), np.cos(off)], axis=2)
-    sn = np.concatenate([np.sin(off), -np.sin(off)], axis=2)
+    sn = np.concatenate([np.sin(off), np.sin(off)], axis=2)
     offset = (np.concatenate([cs, sn], axis=1) * SIGMA).astype(np.float32)
     eye = np.eye(8)
     synth = np.concatenate(
@@ -70,58 +70,114 @@
     return hi, (a - hi.astype(f32)).astype(bf16)
 
 
-def my_offset(offset_ref):
-    me = lax.axis_index("px") * PY + lax.axis_index("py")
-    return offset_ref[me]
-
-
-def forward_part(get, low_ref, hi_ref, lo_ref, offset_ref, turn_ref, out_ref):
+def halves():
+    lane = lax.broadcasted_iota(jnp.int32, (1, LANES), 1)
+    return jnp.where(lane < LANES // 2, -1.0, 1.0)
+
+
+def turned(v):
+    return halves() * pltpu.roll(v, LANES // 2, 1)
+
+
+def my_place():
+    return lax.axis_index("px") * PY + lax.axis_index("py")
+
+
+def forward_part(get, low_ref, hi_ref, lo_ref, off_ref, turn_ref, put):
     low = low_ref[...]
-    rows = []
-    for c in range(C):
-        z = dot_nt(low, get(c))
-        rows.append(jnp.concatenate([z[:C], z[C:]], axis=1))
-    x_hi, x_lo = split(jnp.concatenate(rows, axis=0))
-    off = my_offset(offset_ref)
+    rows = [dot_nt(low, get(c)) for c in range(C)]
+    both = jnp.concatenate([r[:C] for r in rows] + [r[C:] for r in rows], axis=0)
+    x_hi, x_lo = split(both)
+    hi = hi_ref[...]
+    part = dot(x_hi, hi) + dot(x_lo, hi) + dot(x_hi, lo_ref[...])
     for mb in range(PX):
-        cols = slice(mb * LANES, (mb + 1) * LANES)
-        hi = hi_ref[:, cols]
-        part = dot(x_hi, hi) + dot(x_lo, hi) + dot(x_hi, lo_ref[:, cols])
-        turned = part * off[mb] + pltpu.roll(part, LANES // 2, 1) * off[PX + mb]
-        turn_ref[mb] = turned
+        pa = part[: C * C, mb * LANES : (mb + 1) * LANES]
+        pb = part[C * C :, mb * LANES : (mb + 1) * LANES]
+        co, si = off_ref[mb : mb + 1, :], off_ref[PX + mb : PX + mb + 1, :]
+        turn_ref[mb] = (pa * co + pb * si) + turned(pb * co - pa * si)
     for mb in range(PX):
         for k in range(C):
-            out_ref[mb * PY + k, 0:C, :] = turn_ref[mb, pl.ds(k, C, stride=C), :]
-
-
-def inverse_part(recv_ref, hi_ref, lo_ref, offset_ref, synth_ref, turn_ref, g_ref):
-    off = my_offset(offset_ref)
+            put(mb * PY + k, turn_ref[mb, pl.ds(k, C, stride=C), :])
+
+
+def inverse_part(recv_ref, hi_ref, lo_ref, off_ref, synth_ref, turn_ref, g_ref):
     for mb in range(PX):
         v = recv_ref[mb * PY : (mb + 1) * PY].reshape(PY * C, LANES)
-        turn_ref[mb] = v * off[mb] - pltpu.roll(v, LANES // 2, 1) * off[PX + mb]
+        r = turned(v)
+        co, si = off_ref[mb : mb + 1, :], off_ref[PX + mb : PX + mb + 1, :]
+        turn_ref[mb] = v * co + r * si
+        turn_ref[PX + mb] = v * si - r * co
     rows = []
-    for o in range(C):
-        rows.append(
-            jnp.concatenate(
-                [turn_ref[mb, pl.ds(o, C, stride=C), :] for mb in range(PX)], axis=1
+    for half in range(2):
+        for o in range(C):
+            rows.append(
+                jnp.concatenate(
+                    [turn_ref[half * PX + mb, pl.ds(o, C, stride=C), :] for mb in range(PX)], axis=1
+                )
             )
-        )
     v_hi, v_lo = split(jnp.concatenate(rows, axis=0))
     hi = hi_ref[...]
     z = dot_nt(hi, v_hi) + dot_nt(hi, v_lo) + dot_nt(lo_ref[...], v_hi)
     z = z.astype(bf16)
     for ob in range(2):
-        cols = slice(ob * LANES, (ob + 1) * LANES)
-        zb = jnp.concatenate([z[:XY, cols], z[XY:, cols]], axis=1)
-        g = dot(zb, synth_ref[...])
+        re = z[:, ob * LANES : (ob + 1) * LANES]
+        im = z[:, C * C + ob * LANES : C * C + (ob + 1) * LANES]
+        g = dot(jnp.concatenate([re, im], axis=1), synth_ref[...])
         for o in range(8):
             g_ref[ob * 8 + o] = g[:, o * N : (o + 1) * N]
 
 
-def k_forward(field_ref, low_ref, hi_ref, lo_ref, offset_ref, out_ref, turn_ref):
-    forward_part(
-        lambda c: field_ref[c], low_ref, hi_ref, lo_ref, offset_ref, turn_ref, out_ref
-    )
+def k_forward(
+    field_hbm, low_hbm, hi_hbm, lo_hbm, offset_hbm, out_ref,
+    field_ref, low_ref, hi_ref, lo_ref, off_ref, turn_ref, sems,
+):
+    copies = [
+        pltpu.make_async_copy(a, b, sems.at[i])
+        for i, (a, b) in enumerate(
+            (
+                (low_hbm, low_ref),
+                (field_hbm, field_ref),
+                (hi_hbm, hi_ref),
+                (lo_hbm, lo_ref),
+                (offset_hbm.at[my_place()], off_ref),
+            )
+        )
+    ]
+    for copy in copies:
+        copy.start()
+    for copy in copies:
+        copy.wait()
+
+    def put(d, value):
+        out_ref[d] = value
+
+    forward_part(lambda c: field_ref[c], low_ref, hi_ref, lo_ref, off_ref, turn_ref, put)
+
+
+def spread_map(w, transpose):
+    r = lax.broadcasted_iota(jnp.int32, (256, C), 0)
+    l = lax.broadcasted_iota(jnp.int32, (256, C), 1)
+    rep = jnp.where(r // 16 == l, 1.0, 0.0).astype(bf16)
+    if transpose:
+        wide = lax.dot_general(w, rep, (((0,), (1,)), ((), ())), preferred_element_type=f32)
+    else:
+        wide = dot_nt(w, rep)
+    full = dot(rep, wide.astype(bf16))
+    r = lax.broadcasted_iota(jnp.int32, (256, 256), 0)
+    l = lax.broadcasted_iota(jnp.int32, (256, 256), 1)
+    return jnp.where(r % 16 == l % 16, full, 0.0).astype(bf16)
+
+
+def k_maps(skip_ref, in_ref, outer_ref, bias_in_ref, kron_ref, bias_ref):
+    kron_ref[0] = spread_map(skip_ref[...], False)
+    kron_ref[1] = spread_map(in_ref[...], False)
+    kron_ref[2] = spread_map(outer_ref[...], True)
+    kron_ref[3] = spread_map(in_ref[...], True)
+    kron_ref[4] = spread_map(skip_ref[...], True)
+    r = lax.broadcasted_iota(jnp.int32, (256, C), 0)
+    l = lax.broadcasted_iota(jnp.int32, (256, C), 1)
+    column = jnp.sum(jnp.where(r // 16 == l, bias_in_ref[...], 0.0), axis=1, keepdims=True)
+    bias_ref[...] = jnp.broadcast_to(column, (256, N))
 
 
 def k_mix(recv_ref, wa_ref, wb_ref, u_ref, out_ref):
@@ -171,10 +227,12 @@
 
 def k_middle(
     recv_ref, field_ref, cot_ref, kron_ref, bias_ref, low_ref, hi_ref, lo_ref, offset_ref, synth_ref,
-    out_ref, dpre_ref,
-    turn_ref, g_ref, skip_acc, bias_acc, in_acc, out_acc,
+    out_ref, dpre_hbm,
+    dpre_ref, sem, turn_ref, g_ref, skip_acc, bias_acc, in_acc, out_acc,
 ):
-    inverse_part(recv_ref, hi_ref, lo_ref, offset_ref, synth_ref, turn_ref, g_ref)
+    off_ref = offset_ref.at[my_place()]
+    inverse_part(recv_ref, hi_ref, lo_ref, off_ref, synth_ref, turn_ref, g_ref)
+    bias = jnp.concatenate([bias_ref[...], bias_ref[...]], axis=1)
     skip_acc[...] = jnp.zeros_like(skip_acc)
     in_acc[...] = jnp.zeros_like(in_acc)
     out_acc[...] = jnp.zeros_like(out_acc)
@@ -183,7 +241,7 @@
     def step(p, carry):
         f = tile(field_ref, p)
         cot = tile(cot_ref, p)
-        pre = tile(g_ref, p) + dot(kron_ref[0], f) + bias_ref[...]
+        pre = tile(g_ref, p) + dot(kron_ref[0], f) + bias
         hid, d_hid = gelu_parts(pre)
         hid = hid.astype(bf16)
         act, d_act = gelu_parts(dot(kron_ref[1], hid))
@@ -199,9 +257,8 @@
         return carry
 
     lax.fori_loop(0, XY // 32, step, 0)
-    forward_part(
-        lambda c: dpre_ref[c], low_ref, hi_ref, lo_ref, offset_ref, turn_ref, out_ref
-    )
+    copy = pltpu.make_async_copy(dpre_ref, dpre_hbm, sem)
+    copy.start()
     bias = bias_acc[...].reshape(C, 16, 256).sum(axis=1)
     total = jnp.sum(bias, axis=1, keepdims=True)
     r = lax.broadcasted_iota(jnp.int32, (C, LANES), 0)
@@ -211,11 +268,20 @@
         [pack_rows(skip_acc[...]), pack_rows(in_acc[...]), pack_rows(out_acc[...]),
          bias_row, jnp.zeros((1, LANES), f32)], axis=0
     )
-    out_ref[:, C : C + 8, :] = jnp.broadcast_to(small[None], (PEERS, 8, LANES))
+    small = small[:SMALL]
+
+    def put(d, value):
+        out_ref[d * ROWS : (d + 1) * ROWS, :] = jnp.concatenate([value, small], axis=0)
+
+    forward_part(lambda c: dpre_ref[c], low_ref, hi_ref, lo_ref, off_ref, turn_ref, put)
+    copy.wait()
 
 
 def k_mix_back(recv_ref, u_ref, wa_ref, wb_ref, out_ref, share_ref):
-    got = jnp.sum(recv_ref[...], axis=0)
+    slabs = recv_ref[...].reshape(8, 8 * ROWS, LANES).sum(axis=0)
+    got = slabs[:ROWS]
+    for i in range(1, 8):
+        got = got + slabs[i * ROWS : (i + 1) * ROWS]
     g = got[:C]
     gs = pltpu.roll(g, LANES // 2, 1)
     rows = []
@@ -223,18 +289,25 @@
         rows.append(jnp.sum(wa_ref[c] * g - wb_ref[c] * gs, axis=0, keepdims=True))
     du = jnp.concatenate(rows, axis=0)
     out_ref[...] = jnp.broadcast_to(du[None], (PEERS, C, LANES))
-    share = jnp.concatenate([u_ref[...], got], axis=0)
+    share = jnp.concatenate([u_ref[...], got, jnp.zeros((8 - SMALL, LANES), f32)], axis=0)
     share_ref[...] = jnp.broadcast_to(share[None], (NB, 2 * C + 8, LANES))
 
 
-def k_input(recv_ref, dpre_ref, kron_ref, hi_ref, lo_ref, offset_ref, synth_ref, out_ref, turn_ref, g_ref):
-    inverse_part(recv_ref, hi_ref, lo_ref, offset_ref, synth_ref, turn_ref, g_ref)
-
-    def step(p, carry):
+def k_input(
+    recv_ref, dpre_ref, kron_ref, hi_ref, lo_ref, offset_ref, synth_ref, out_hbm,
+    out_ref, turn_ref, g_ref, sems,
+):
+    off_ref = offset_ref.at[my_place()]
+    inverse_part(recv_ref, hi_ref, lo_ref, off_ref, synth_ref, turn_ref, g_ref)
+    steps = XY // 32
+    copies = []
+    for p in range(steps):
         untile(out_ref, p, (dot(kron_ref[4], tile(dpre_ref, p)) + tile(g_ref, p)).astype(bf16))
-        return carry
-
-    lax.fori_loop(0, XY // 32, step, 0)
+        part = pl.ds(p * 32, 32)
+        copies.append(pltpu.make_async_copy(out_ref.at[:, part], out_hbm.at[:, part], sems.at[p]))
+        copies[-1].start()
+    for copy in copies:
+        copy.wait()
 
 
 def k_shared(recv_ref, spec_ref, skip_ref, bias_ref, in_ref, outer_ref, pa_ref, pb_ref):
@@ -257,8 +330,10 @@
     full = lambda x, y: lax.dot_general(
         x, y, NT, precision=lax.Precision.HIGHEST, preferred_element_type=f32
     )
-    spec_ref[0] = full(sel_a, pa_ref[...])
-    spec_ref[1] = full(sel_b, pb_ref[...])
+    for i, part in enumerate((full(sel_a, pa_ref[...]), full(sel_b, pb_ref[...]))):
+        for c in range(C):
+            for m in range(ML):
+                spec_ref[i, c, m] = part[2 * m : 2 * m + 2, c * C : (c + 1) * C]
     small = jnp.sum(recv_ref[:, 2 * C :, :], axis=0) * RHO
     r = lax.broadcasted_iota(jnp.int32, (C, LANES), 0)
     l = lax.broadcasted_iota(jnp.int32, (C, LANES), 1)
@@ -274,16 +349,18 @@
     bias_ref[...] = jnp.broadcast_to(small[6:7], (8, LANES))
 
 
-def call(body, name, outs, scratch, *args):
+def call(body, name, outs, scratch, *args, hbm_in=(), hbm_out=()):
     vm = pl.BlockSpec(memory_space=pltpu.VMEM)
+    hbm = pl.BlockSpec(memory_space=pltpu.HBM)
     many = isinstance(outs, (list, tuple))
+    out_specs = [hbm if i in hbm_out else vm for i in range(len(outs) if many else 1)]
     return pl.pallas_call(
         body,
         out_shape=outs,
-        in_specs=[vm] * len(args),
-        out_specs=[vm] * len(outs) if many else vm,
+        in_specs=[hbm if i in hbm_in else vm for i in range(len(args))],
+        out_specs=out_specs if many else out_specs[0],
         scratch_shapes=scratch,
-        compiler_params=pltpu.CompilerParams(vmem_limit_bytes=48 * 2**20),
+        compiler_params=pltpu.CompilerParams(vmem_limit_bytes=40 * 2**20),
         name=name,
     )(*args)
 
@@ -299,44 +376,54 @@
     weight = spec_weight.reshape(2, C, C, ML * C)
     wa = jnp.concatenate([weight[0], weight[0]], axis=2)
     wb = jnp.concatenate([-weight[1], weight[1]], axis=2)
-    maps = jnp.stack([skip_weight, mlp_in, mlp_out.T, mlp_in.T, skip_weight.T])
-    same = jnp.eye(16, dtype=bf16)
-    kron = (maps[:, :, None, :, None] * same[None, None, :, None, :]).reshape(5, 256, 256)
-    bias = jnp.broadcast_to(skip_bias[:, None, None], (C, 16, 2 * N)).reshape(256, 2 * N)
     turn = pltpu.VMEM((PX, PY * C, LANES), f32)
+    twice = pltpu.VMEM((2 * PX, PY * C, LANES), f32)
     cells = pltpu.VMEM((C, XY, N), f32)
+    cells_low = pltpu.VMEM((C, XY, N), bf16)
     square = pltpu.VMEM((256, 256), f32)
+    own = pltpu.VMEM((8, LANES), f32)
+    plane = pltpu.VMEM((XY, PX * LANES), bf16)
 
     def exchange(block):
         return lax.all_to_all(block, ("px", "py"), 0, 0, tiled=True)
 
-    sent = call(k_forward, "forward", shape(PEERS, C, LANES), [turn], field, low, hi, lo, offset)
+    sent = call(
+        k_forward, "forward", shape(PEERS, C, LANES),
+        [cells_low, pltpu.VMEM((2 * C, N), bf16), plane, plane, own, turn, pltpu.SemaphoreType.DMA((5,))],
+        field, low, hi, lo, offset, hbm_in=range(5),
+    )
+    kron, bias = call(
+        k_maps, "maps", [shape(5, 256, 256, dtype=bf16), shape(256, N)], [],
+        skip_weight, mlp_in, mlp_out, skip_bias.reshape(1, C),
+    )
     u, sent = call(
         k_mix, "mix", [shape(C, LANES), shape(PEERS, C, LANES)], [], exchange(sent), wa, wb
     )
     sent, dpre = call(
         k_middle, "middle",
-        [shape(PEERS, C + 8, LANES), shape(C, XY, N, dtype=bf16)],
-        [turn, cells, square, square, square, square],
-        exchange(sent), field, cotangent, kron, bias, low, hi, lo, offset, synth,
-    )
+        [shape(PEERS * ROWS, LANES), shape(C, XY, N, dtype=bf16)],
+        [cells_low, pltpu.SemaphoreType.DMA, twice, cells, square, square, square, square],
+        exchange(sent), field, cotangent, kron, bias, low, hi, lo, offset, synth, hbm_out=(1,),
+    )
+    sent = exchange(sent.reshape(PEERS, 1, ROWS * LANES)).reshape(PEERS * ROWS, LANES)
     sent, share = call(
         k_mix_back, "mix_back",
         [shape(PEERS, C, LANES), shape(NB, 2 * C + 8, LANES)],
-        [], exchange(sent), u, wa, wb,
-    )
-    back = exchange(sent)
+        [], sent, u, wa, wb,
+    )
+    back, share = lax.optimization_barrier((exchange(sent), share))
     share = lax.all_to_all(share, "batch", 0, 0, tiled=True)
     grad_input = call(
-        k_input, "input_grad", shape(C, XY, N, dtype=bf16), [turn, cells],
-        back, dpre, kron, hi, lo, offset, synth,
+        k_input, "input_grad", shape(C, XY, N, dtype=bf16),
+        [cells_low, twice, cells, pltpu.SemaphoreType.DMA((XY // 32,))],
+        back, dpre, kron, hi, lo, offset, synth, hbm_out=(0,),
     )
     spec, skip, b, inner, outer = call(
         k_shared, "shared",
-        [shape(2, 8, 256), shape(C, C), shape(8, LANES), shape(C, C), shape(C, C)],
+        [shape(2, C, ML, 2, C), shape(C, C), shape(8, LANES), shape(C, C), shape(C, C)],
         [pltpu.VMEM((256, LANES), f32)] * 2, share,
     )
-    spec = spec.reshape(2, ML, 2, C, C).transpose(0, 3, 4, 1, 2).reshape(2, C, C, 1, ML, 2)
+    spec = spec.transpose(0, 1, 4, 2, 3).reshape(2, C, C, 1, ML, 2)
     return (grad_input.reshape(1, C, XL, YL, N), spec, skip, b[0, :C], inner, outer)
 
 

time: 161 us -> 151 us (0.938)
  local copies, waits for them, and re-layouts: 27.6 us -> 13.6 us
  waiting for transfers between devices: 29.8 us -> 35.3 us
  Pallas kernels: 21.2 us -> 18.8 us
  blocking collectives: 49.2 us -> 51.1 us
    all_to_all x1 -> x2, blocking collectives: 33.2 us -> 51.1 us  [exchange(): return lax.all_to_all(block, ('px', 'py'), 0, 0, tiled=True)]
    all_to_all x1 -> x0, blocking collectives: 16.1 us -> none  [shards(): share = lax.all_to_all(share, 'batch', 0, 0, tiled=True)]
    mul x4 -> x0, local copies, waits for them, and re-layouts: 14.6 us -> none  [shards(): maps[:, :, None, :, None] * same[None, None, :, None, :]]
    all_to_all x3 -> x2, starting transfers between devices: 29.9 us -> 21.8 us  [exchange(): return lax.all_to_all(block, ('px', 'py'), 0, 0, tiled=True)]
    all_to_all x0 -> x1, starting transfers between devices: none -> 6.6 us  [shards(): share = lax.all_to_all(share, 'batch', 0, 0, tiled=True)]
    all_to_all x0 -> x1, waiting for transfers between devices: none -> 6 us  [shards(): share = lax.all_to_all(share, 'batch', 0, 0, tiled=True)]
    unnamed x50, local copies, waits for them, and re-layouts: 8.17 us -> 12.5 us
    pallas_call x6 -> x7, Pallas kernels: 21.2 us -> 18.8 us  [call(): pl.pallas_call(body, out_shape=outs, in_specs=[hbm if i in hbm_in else vm...]
  transfers between devices with their start and end apart: 3 -> 3, of which waited for: 3 -> 3; matrix products, arithmetic and copies ran while one was open for 13% -> 1% of each run, Pallas kernels for 1% -> 2%
where the time goes in v2:
time: 151 us; the launch traced here: 148 us
  blocking collectives  51.1 us (34%)
  waiting for transfers between devices  35.3 us (23%)
  starting transfers between devices  28.4 us (19%)
  Pallas kernels  18.8 us (12%)
  local copies, waits for them, and re-layouts  13.6 us (9%)
    all_to_all x2, blocking collectives, exchange(): return lax.all_to_all(block, ('px', 'py'), 0, 0, tiled=True)  51.1 us
    all_to_all x2, waiting for transfers between devices, exchange(): return lax.all_to_all(block, ('px', 'py'), 0, 0, tiled=True)  29.3 us
    all_to_all x2, starting transfers between devices, exchange(): return lax.all_to_all(block, ('px', 'py'), 0, 0, tiled=True)  21.8 us
    pallas_call x7, Pallas kernels, call(): pl.pallas_call(body, out_shape=outs, in_specs=[hbm if i in hbm_in else vm...  18.8 us
    unnamed x50, local copies, waits for them, and re-layouts  12.5 us
    all_to_all x1, starting transfers between devices, shards(): share = lax.all_to_all(share, 'batch', 0, 0, tiled=True)  6.6 us
    all_to_all x1, waiting for transfers between devices, shards(): share = lax.all_to_all(share, 'batch', 0, 0, tiled=True)  6 us
  transfers between devices with their start and end apart: 3, of which 3 were waited for; matrix products, arithmetic and copies ran while one was open for 1% of the time, Pallas kernels for 2%

profile of v2, /device:TPU:1, one launch (start us, length us, event | category | flops | bytes accessed | tf_op | source)
XLA Modules:
  0.0 148.2 jit_solution(13935704610574629715)
XLA Ops:
  0.6 1.2 copy-done
  1.9 0.9 copy-done.2
  2.8 0.9 copy-done.4
  3.8 0.9 copy-done.6
  4.7 0.7 copy-done.18
  5.4 2.2 %forward.1 = f32[64,16,128]{2,1,0:T(8,128)} custom-call(bf16[16,256,128]{2,1,0:T(8,128)(2,1)S(1)} %bitcast.13, bf16[32,128]{1,0:T(8,128)(2,1)S(1)} %copy-done.18, bf16[256,512]{1,0:T(8,128)(2,1)S(1)} %copy-done.6, bf16[256,512]{1,0:T(8,128)(2,1)S(1)} %copy-done.4, f32[64,8,128]{2,1,0:T(8,128)S(1)} %copy-done.2), custom_call_target="tpu_custom_call" | custom-call | tf_op jit(solution)/shard_map/forward/pallas_call | solution.py:357
  7.7 15.6 %all-to-all-start = ((f32[64,16,128]{2,1,0:T(8,128)}), f32[64,16,128]{2,1,0:T(8,128)S(1)}, u32[]{:S(2)}, u32[]{:S(2)}) async-start(f32[64,16,128]{2,1,0:T(8,128)} %forward.1), calls=%async_computation | async-start | bytes 1048576 | tf_op jit(solution)/shard_map/all_to_all | solution.py:388
  24.1 16.3 %all-to-all-done.recv_ref = f32[64,16,128]{2,1,0:T(8,128)S(1)} async-done(((f32[64,16,128]{2,1,0:T(8,128)}), f32[64,16,128]{2,1,0:T(8,128)S(1)}, u32[]{:S(2)}, u32[]{:S(2)}) %all-to-all-start) | async-done | bytes 524320 | tf_op jit(solution)/shard_map/all_to_all | solution.py:388
  40.4 1.0 mix.1
  41.4 6.2 %all-to-all-start.1 = ((f32[64,16,128]{2,1,0:T(8,128)}), f32[64,16,128]{2,1,0:T(8,128)S(1)}, u32[]{:S(2)}, u32[]{:S(2)}) async-start(f32[64,16,128]{2,1,0:T(8,128)} %get-tuple-element.21), calls=%async_computation.1 | async-start | bytes 1048576 | tf_op jit(solution)/shard_map/all_to_all | solution.py:388
  50.4 0.7 maps.1
  51.7 13.0 %all-to-all-done.1.recv_ref = f32[64,16,128]{2,1,0:T(8,128)S(1)} async-done(((f32[64,16,128]{2,1,0:T(8,128)}), f32[64,16,128]{2,1,0:T(8,128)S(1)}, u32[]{:S(2)}, u32[]{:S(2)}) %all-to-all-start.1) | async-done | bytes 524320 | tf_op jit(solution)/shard_map/all_to_all | solution.py:388
  64.8 1.2 copy-done.13
  66.1 0.9 copy-done.17
  67.0 10.3 %middle.1 = (f32[1472,128]{1,0:T(8,128)S(1)}, bf16[16,256,128]{2,1,0:T(8,128)(2,1)S(1)}) custom-call(f32[64,16,128]{2,1,0:T(8,128)S(1)} %all-to-all-done.1.recv_ref, bf16[16,256,128]{2,1,0:T(8,128)(2,1)S(1)} %bitcast.14, bf16[16,256,128]{2,1,0:T(8,128)(2,1)S(1)} %bitcast.16, bf16[5,256,256]{2,1,0:T(8,128)(2,1)S(1)} %get-tuple-element.22.kron_ref, ...), custom_call_target="tpu_custom_call" | custom-call | tf_op jit(solution)/shard_map/middle/pallas_call | solution.py:357
  77.3 1.0 copy-done.14
  78.3 28.3 %all_to_all.25 = f32[64,1,2944]{2,1,0:T(1,128)S(1)} all-to-all(f32[64,1,2944]{2,1,0:T(1,128)S(1)} %bitcast.17), channel_id=1, replica_groups=mesh['batch'=8,'px'=4,'py'=16] {'px','py'}, dimensions={0} | all-to-all | bytes 1507328 | tf_op jit(solution)/shard_map/all_to_all | solution.py:388
  106.6 0.7 mix_back.1
  107.3 22.8 %all_to_all.26.recv_ref = f32[64,16,128]{2,1,0:T(8,128)S(1)} all-to-all(f32[64,16,128]{2,1,0:T(8,128)S(1)} %get-tuple-element.26), channel_id=1, replica_groups=mesh['batch'=8,'px'=4,'py'=16] {'px','py'}, dimensions={0} | all-to-all | bytes 1048576 | tf_op jit(solution)/shard_map/all_to_all | solution.py:388
  130.1 6.6 %all-to-all-start.4 = ((f32[8,40,128]{2,1,0:T(8,128)}), f32[8,40,128]{2,1,0:T(8,128)S(1)}, u32[]{:S(2)}, u32[]{:S(2)}) async-start(f32[8,40,128]{2,1,0:T(8,128)} %get-tuple-element.30), calls=%async_computation.4 | async-start | bytes 327680 | tf_op jit(solution)/shard_map/all_to_all | solution.py:415
  136.7 1.2 copy-done.15
  137.9 2.5 %input_grad.1 = bf16[16,256,128]{2,1,0:T(8,128)(2,1)} custom-call(f32[64,16,128]{2,1,0:T(8,128)S(1)} %all_to_all.26.recv_ref, bf16[16,256,128]{2,1,0:T(8,128)(2,1)S(1)} %copy-done.15, bf16[5,256,256]{2,1,0:T(8,128)(2,1)S(1)} %get-tuple-element.22.kron_ref, bf16[256,512]{1,0:T(8,128)(2,1)S(1)} %copy-done.7, bf16[256,512]{1,0:T(8,128)(2,1)S(1)} %copy-done.5, ...), custom_call_target="tpu_custom_call" | custom-call | tf_op jit(solution)/shard_map/input_grad/pallas_call | solution.py:357
  140.3 6.0 %all-to-all-done.4.recv_ref = f32[8,40,128]{2,1,0:T(8,128)S(1)} async-done(((f32[8,40,128]{2,1,0:T(8,128)}), f32[8,40,128]{2,1,0:T(8,128)S(1)}, u32[]{:S(2)}, u32[]{:S(2)}) %all-to-all-start.4) | async-done | bytes 163872 | tf_op jit(solution)/shard_map/all_to_all | solution.py:415
  146.4 1.4 shared.1
  (47 shorter events, 4.7 us)
Async XLA Ops:
  0.6 1.2 copy-start
  1.9 0.9 copy-start.2
  2.8 0.9 copy-start.4
  3.8 0.9 copy-start.6
  4.7 0.7 copy-start.18
  7.7 15.6 %copy-start.24 = (f32[2,16,16,1,4,16]{5,4,3,2,1,0:T(4,128)S(1)}, f32[2,16,16,1,4,16]{5,4,3,2,1,0:T(4,128)}, u32[]{:S(2)}) copy-start(f32[2,16,16,1,4,16]{5,4,3,2,1,0:T(4,128)} %param.14) | copy-start | bytes 393220
  7.7 32.7 %all-to-all-start = ((f32[64,16,128]{2,1,0:T(8,128)}), f32[64,16,128]{2,1,0:T(8,128)S(1)}, u32[]{:S(2)}, u32[]{:S(2)}) async-start(f32[64,16,128]{2,1,0:T(8,128)} %forward.1), calls=%async_computation | async-start | bytes 1048576 | tf_op jit(solution)/shard_map/all_to_all | solution.py:388
  23.9 40.9 %copy-start.8 = (bf16[256,1024]{1,0:T(8,128)(2,1)S(1)}, bf16[256,1024]{1,0:T(8,128)(2,1)}, u32[]{:S(2)}) copy-start(bf16[256,1024]{1,0:T(8,128)(2,1)} %constant.14.clone.synth_ref) | copy-start | bytes 1572868
  24.1 17.3 %copy-start.9 = (f32[16,16,128]{2,1,0:T(8,128)}, f32[16,16,128]{2,1,0:T(8,128)S(1)}, u32[]{:S(2)}) copy-start(f32[16,16,128]{2,1,0:T(8,128)S(1)} %get-tuple-element.50.wa_ref) | copy-start | bytes 393220
  24.1 17.3 %copy-start.11 = (f32[16,16,128]{2,1,0:T(8,128)}, f32[16,16,128]{2,1,0:T(8,128)S(1)}, u32[]{:S(2)}) copy-start(f32[16,16,128]{2,1,0:T(8,128)S(1)} %get-tuple-element.51.wb_ref) | copy-start | bytes 393220
  24.1 40.7 %copy-start.1 = (bf16[1,16,32,8,128]{4,3,2,1,0:T(8,128)(2,1)S(1)}, bf16[1,16,32,8,128]{4,3,2,1,0:T(8,128)(2,1)}, u32[]{:S(2)}) copy-start(bf16[1,16,32,8,128]{4,3,2,1,0:T(8,128)(2,1)} %param.12) | copy-start | bytes 3145732
  41.4 23.4 %copy-start.3 = (f32[64,8,128]{2,1,0:T(8,128)S(1)}, f32[64,8,128]{2,1,0:T(8,128)}, u32[]{:S(2)}) copy-start(f32[64,8,128]{2,1,0:T(8,128)} %constant.13.clone.offset_hbm.offset_ref) | copy-start | bytes 786436
  41.4 23.4 %copy-start.5 = (bf16[256,512]{1,0:T(8,128)(2,1)S(1)}, bf16[256,512]{1,0:T(8,128)(2,1)}, u32[]{:S(2)}) copy-start(bf16[256,512]{1,0:T(8,128)(2,1)} %constant.12.clone.lo_hbm.lo_ref) | copy-start | bytes 786436
  41.4 23.4 %copy-start.7 = (bf16[256,512]{1,0:T(8,128)(2,1)S(1)}, bf16[256,512]{1,0:T(8,128)(2,1)}, u32[]{:S(2)}) copy-start(bf16[256,512]{1,0:T(8,128)(2,1)} %constant.11.clone.hi_hbm.hi_ref) | copy-start | bytes 786436
  41.4 23.4 %all-to-all-start.1 = ((f32[64,16,128]{2,1,0:T(8,128)}), f32[64,16,128]{2,1,0:T(8,128)S(1)}, u32[]{:S(2)}, u32[]{:S(2)}) async-start(f32[64,16,128]{2,1,0:T(8,128)} %get-tuple-element.21), calls=%async_computation.1 | async-start | bytes 1048576 | tf_op jit(solution)/shard_map/all_to_all | solution.py:388
  48.3 0.7 copy-start.20
  50.4 14.5 %copy-start.19 = (bf16[32,128]{1,0:T(8,128)(2,1)S(1)}, bf16[32,128]{1,0:T(8,128)(2,1)}, u32[]{:S(2)}) copy-start(bf16[32,128]{1,0:T(8,128)(2,1)} %constant.10.clone.low_hbm.low_ref) | copy-start | bytes 24580
  64.8 1.2 copy-start.13
  66.1 0.9 copy-start.17
  77.3 1.0 copy-start.14
  78.3 28.3 %copy-start.10 = (f32[16,16,128]{2,1,0:T(8,128)S(1)}, f32[16,16,128]{2,1,0:T(8,128)}, u32[]{:S(2)}) copy-start(f32[16,16,128]{2,1,0:T(8,128)} %copy-done.9) | copy-start | bytes 393220
  78.3 28.3 %copy-start.12 = (f32[16,16,128]{2,1,0:T(8,128)S(1)}, f32[16,16,128]{2,1,0:T(8,128)}, u32[]{:S(2)}) copy-start(f32[16,16,128]{2,1,0:T(8,128)} %copy-done.11) | copy-start | bytes 393220
  130.1 16.3 %all-to-all-start.4 = ((f32[8,40,128]{2,1,0:T(8,128)}), f32[8,40,128]{2,1,0:T(8,128)S(1)}, u32[]{:S(2)}, u32[]{:S(2)}) async-start(f32[8,40,128]{2,1,0:T(8,128)} %get-tuple-element.30), calls=%async_computation.4 | async-start | bytes 327680 | tf_op jit(solution)/shard_map/all_to_all | solution.py:415
  136.7 1.2 copy-start.15
  (4 other events, 2.7 us)

commit v3 on v2

--- a/solution.py
+++ b/solution.py
@@ -18,8 +18,7 @@
 XY = XL * YL
 ML = C // PX
 PEERS = PX * PY
-SMALL = 7
-ROWS = C + SMALL
+ROWS = C + 1
 LANES = 128
 SIGMA = 1.0 / math.sqrt(N**3)
 RHO = 1.0 / math.sqrt(NB * N**3)
@@ -100,9 +99,9 @@
             put(mb * PY + k, turn_ref[mb, pl.ds(k, C, stride=C), :])
 
 
-def inverse_part(recv_ref, hi_ref, lo_ref, off_ref, synth_ref, turn_ref, g_ref):
+def inverse_part(block, hi_ref, lo_ref, off_ref, synth_ref, turn_ref, g_ref):
     for mb in range(PX):
-        v = recv_ref[mb * PY : (mb + 1) * PY].reshape(PY * C, LANES)
+        v = jnp.concatenate([block(mb * PY + k) for k in range(PY)], axis=0)
         r = turned(v)
         co, si = off_ref[mb : mb + 1, :], off_ref[PX + mb : PX + mb + 1, :]
         turn_ref[mb] = v * co + r * si
@@ -221,17 +220,26 @@
     spread = jnp.dot(kept, pick, precision=lax.Precision.HIGHEST, preferred_element_type=f32)
     r = lax.broadcasted_iota(jnp.int32, (C, LANES), 0)
     l = lax.broadcasted_iota(jnp.int32, (C, LANES), 1)
-    spread = jnp.where(r % 8 == l // 16, spread, 0.0)
-    return spread.reshape(2, 8, LANES).sum(axis=1)
+    return jnp.where(r % 8 == l // 16, spread, 0.0)
 
 
 def k_middle(
-    recv_ref, field_ref, cot_ref, kron_ref, bias_ref, low_ref, hi_ref, lo_ref, offset_ref, synth_ref,
+    recv_ref, field_hbm, cot_hbm, bias_hbm, kron_ref, low_ref, hi_ref, lo_ref, offset_ref, synth_ref,
     out_ref, dpre_hbm,
-    dpre_ref, sem, turn_ref, g_ref, skip_acc, bias_acc, in_acc, out_acc,
+    field_ref, cot_ref, bias_ref, dpre_ref, sems, turn_ref, g_ref, skip_acc, bias_acc, in_acc, out_acc,
 ):
+    copies = [
+        pltpu.make_async_copy(a, b, sems.at[i])
+        for i, (a, b) in enumerate(
+            ((field_hbm, field_ref), (cot_hbm, cot_ref), (bias_hbm, bias_ref))
+        )
+    ]
+    for copy in copies:
+        copy.start()
     off_ref = offset_ref.at[my_place()]
-    inverse_part(recv_ref, hi_ref, lo_ref, off_ref, synth_ref, turn_ref, g_ref)
+    inverse_part(lambda d: recv_ref[d], hi_ref, lo_ref, off_ref, synth_ref, turn_ref, g_ref)
+    for copy in copies:
+        copy.wait()
     bias = jnp.concatenate([bias_ref[...], bias_ref[...]], axis=1)
     skip_acc[...] = jnp.zeros_like(skip_acc)
     in_acc[...] = jnp.zeros_like(in_acc)
@@ -257,7 +265,7 @@
         return carry
 
     lax.fori_loop(0, XY // 32, step, 0)
-    copy = pltpu.make_async_copy(dpre_ref, dpre_hbm, sem)
+    copy = pltpu.make_async_copy(dpre_ref, dpre_hbm, sems.at[3])
     copy.start()
     bias = bias_acc[...].reshape(C, 16, 256).sum(axis=1)
     total = jnp.sum(bias, axis=1, keepdims=True)
@@ -266,30 +274,36 @@
     bias_row = jnp.sum(jnp.where(r == l, total, 0.0), axis=0, keepdims=True)
     small = jnp.concatenate(
         [pack_rows(skip_acc[...]), pack_rows(in_acc[...]), pack_rows(out_acc[...]),
-         bias_row, jnp.zeros((1, LANES), f32)], axis=0
-    )
-    small = small[:SMALL]
+         bias_row, jnp.zeros((C - 1, LANES), f32)], axis=0
+    )
 
     def put(d, value):
-        out_ref[d * ROWS : (d + 1) * ROWS, :] = jnp.concatenate([value, small], axis=0)
+        out_ref[d * ROWS : (d + 1) * ROWS, :] = jnp.concatenate([value, small[d : d + 1]], axis=0)
 
     forward_part(lambda c: dpre_ref[c], low_ref, hi_ref, lo_ref, off_ref, turn_ref, put)
     copy.wait()
 
 
-def k_mix_back(recv_ref, u_ref, wa_ref, wb_ref, out_ref, share_ref):
+def k_mix_back(recv_ref, wa_ref, wb_ref, out_ref, g_ref):
     slabs = recv_ref[...].reshape(8, 8 * ROWS, LANES).sum(axis=0)
     got = slabs[:ROWS]
     for i in range(1, 8):
         got = got + slabs[i * ROWS : (i + 1) * ROWS]
     g = got[:C]
+    g_ref[...] = g
     gs = pltpu.roll(g, LANES // 2, 1)
     rows = []
     for c in range(C):
         rows.append(jnp.sum(wa_ref[c] * g - wb_ref[c] * gs, axis=0, keepdims=True))
-    du = jnp.concatenate(rows, axis=0)
-    out_ref[...] = jnp.broadcast_to(du[None], (PEERS, C, LANES))
-    share = jnp.concatenate([u_ref[...], got, jnp.zeros((8 - SMALL, LANES), f32)], axis=0)
+    block = jnp.concatenate(rows + [got[C:]], axis=0)
+    slab = jnp.concatenate([block] * 8, axis=0)
+    for i in range(8):
+        out_ref[i * 8 * ROWS : (i + 1) * 8 * ROWS, :] = slab
+
+
+def k_share(back_ref, u_ref, g_ref, share_ref):
+    small = back_ref[pl.ds(C, PEERS, stride=ROWS), :].reshape(8, 8, LANES).sum(axis=1)
+    share = jnp.concatenate([u_ref[...], g_ref[...], small], axis=0)
     share_ref[...] = jnp.broadcast_to(share[None], (NB, 2 * C + 8, LANES))
 
 
@@ -298,7 +312,10 @@
     out_ref, turn_ref, g_ref, sems,
 ):
     off_ref = offset_ref.at[my_place()]
-    inverse_part(recv_ref, hi_ref, lo_ref, off_ref, synth_ref, turn_ref, g_ref)
+    inverse_part(
+        lambda d: recv_ref[d * ROWS : d * ROWS + C, :],
+        hi_ref, lo_ref, off_ref, synth_ref, turn_ref, g_ref,
+    )
     steps = XY // 32
     copies = []
     for p in range(steps):
@@ -354,13 +371,17 @@
     hbm = pl.BlockSpec(memory_space=pltpu.HBM)
     many = isinstance(outs, (list, tuple))
     out_specs = [hbm if i in hbm_out else vm for i in range(len(outs) if many else 1)]
+    args = [
+        pltpu.with_memory_space_constraint(a, pltpu.HBM) if i in hbm_in else a
+        for i, a in enumerate(args)
+    ]
     return pl.pallas_call(
         body,
         out_shape=outs,
         in_specs=[hbm if i in hbm_in else vm for i in range(len(args))],
         out_specs=out_specs if many else out_specs[0],
         scratch_shapes=scratch,
-        compiler_params=pltpu.CompilerParams(vmem_limit_bytes=40 * 2**20),
+        compiler_params=pltpu.CompilerParams(vmem_limit_bytes=32 * 2**20),
         name=name,
     )(*args)
 
@@ -387,6 +408,9 @@
     def exchange(block):
         return lax.all_to_all(block, ("px", "py"), 0, 0, tiled=True)
 
+    def exchange_rows(block):
+        return exchange(block.reshape(PEERS, 1, ROWS * LANES)).reshape(PEERS * ROWS, LANES)
+
     sent = call(
         k_forward, "forward", shape(PEERS, C, LANES),
         [cells_low, pltpu.VMEM((2 * C, N), bf16), plane, plane, own, turn, pltpu.SemaphoreType.DMA((5,))],
@@ -401,17 +425,18 @@
     )
     sent, dpre = call(
         k_middle, "middle",
-        [shape(PEERS * ROWS, LANES), shape(C, XY, N, dtype=bf16)],
-        [cells_low, pltpu.SemaphoreType.DMA, twice, cells, square, square, square, square],
-        exchange(sent), field, cotangent, kron, bias, low, hi, lo, offset, synth, hbm_out=(1,),
-    )
-    sent = exchange(sent.reshape(PEERS, 1, ROWS * LANES)).reshape(PEERS * ROWS, LANES)
-    sent, share = call(
-        k_mix_back, "mix_back",
-        [shape(PEERS, C, LANES), shape(NB, 2 * C + 8, LANES)],
-        [], sent, u, wa, wb,
-    )
-    back, share = lax.optimization_barrier((exchange(sent), share))
+        [shape(PEERS * ROWS, LANES), pltpu.HBM((C, XY, N), bf16)],
+        [cells_low, cells_low, pltpu.VMEM((256, N), f32), cells_low, pltpu.SemaphoreType.DMA((4,)),
+         twice, cells, square, square, square, square],
+        exchange(sent), field, cotangent, bias, kron, low, hi, lo, offset, synth,
+        hbm_in=(1, 2, 3), hbm_out=(1,),
+    )
+    sent, g = call(
+        k_mix_back, "mix_back", [shape(PEERS * ROWS, LANES), shape(C, LANES)], [],
+        exchange_rows(sent), wa, wb,
+    )
+    back = exchange_rows(sent)
+    share = call(k_share, "share", shape(NB, 2 * C + 8, LANES), [], back, u, g)
     share = lax.all_to_all(share, "batch", 0, 0, tiled=True)
     grad_input = call(
         k_input, "input_grad", shape(C, XY, N, dtype=bf16),

time: 151 us -> 141 us (0.934)
  local copies, waits for them, and re-layouts: 13.6 us -> 3.66 us
  blocking collectives: 51.1 us -> 47.6 us
  Pallas kernels: 18.8 us -> 21.5 us
  waiting for transfers between devices: 35.3 us -> 37.5 us
    unnamed x50 -> x24, local copies, waits for them, and re-layouts: 12.5 us -> 2.53 us
    all_to_all x2, blocking collectives: 51.1 us -> 47.6 us  [exchange(): return lax.all_to_all(block, ('px', 'py'), 0, 0, tiled=True)]
    pallas_call x7 -> x8, Pallas kernels: 18.8 us -> 21.5 us  [call(): pl.pallas_call(body, out_shape=outs, in_specs=[hbm if i in hbm_in else vm...]
    all_to_all x2, waiting for transfers between devices: 29.3 us -> 31.4 us  [exchange(): return lax.all_to_all(block, ('px', 'py'), 0, 0, tiled=True)]
where the time goes in v3:
time: 141 us; the launch traced here: 139 us
  blocking collectives  47.6 us (34%)
  waiting for transfers between devices  37.5 us (27%)
  starting transfers between devices  28.4 us (20%)
  Pallas kernels  21.5 us (15%)
  local copies, waits for them, and re-layouts  3.66 us (3%)
    all_to_all x2, blocking collectives, exchange(): return lax.all_to_all(block, ('px', 'py'), 0, 0, tiled=True)  47.6 us
    all_to_all x2, waiting for transfers between devices, exchange(): return lax.all_to_all(block, ('px', 'py'), 0, 0, tiled=True)  31.4 us
    all_to_all x2, starting transfers between devices, exchange(): return lax.all_to_all(block, ('px', 'py'), 0, 0, tiled=True)  21.8 us
    pallas_call x8, Pallas kernels, call(): pl.pallas_call(body, out_shape=outs, in_specs=[hbm if i in hbm_in else vm...  21.5 us
    all_to_all x1, starting transfers between devices, shards(): share = lax.all_to_all(share, 'batch', 0, 0, tiled=True)  6.6 us
    all_to_all x1, waiting for transfers between devices, shards(): share = lax.all_to_all(share, 'batch', 0, 0, tiled=True)  6 us
  transfers between devices with their start and end apart: 3, of which 3 were waited for; matrix products, arithmetic and copies ran while one was open for 1% of the time, Pallas kernels for 2%

profile of v3, /device:TPU:1, one launch (start us, length us, event | category | flops | bytes accessed | tf_op | source)
XLA Modules:
  0.0 139.5 jit_solution(10125658154229282455)
XLA Ops:
  0.6 3.5 %forward.1 = f32[64,16,128]{2,1,0:T(8,128)} custom-call(bf16[16,256,128]{2,1,0:T(8,128)(2,1)} %bitcast.21, bf16[32,128]{1,0:T(8,128)(2,1)} %constant.10.clone.low_hbm.low_ref, bf16[256,512]{1,0:T(8,128)(2,1)} %constant.11.clone.hi_hbm.hi_ref, bf16[256,512]{1,0:T(8,128)(2,1)} %constant.12.clone.lo_hbm.lo_ref, f32[64,8,128]{2,1,0:T(8,128)} %constant.13.clone.offset_hbm.offset_ref), custom_call_target="tpu_custom_call" | custom-call | tf_op jit(solution)/shard_map/forward/pallas_call | solution.py:378
  4.1 15.6 %all-to-all-start = ((f32[64,16,128]{2,1,0:T(8,128)}), f32[64,16,128]{2,1,0:T(8,128)S(1)}, u32[]{:S(2)}, u32[]{:S(2)}) async-start(f32[64,16,128]{2,1,0:T(8,128)} %forward.1), calls=%async_computation | async-start | bytes 1048576 | tf_op jit(solution)/shard_map/all_to_all | solution.py:409
  19.7 0.1 fusion
  19.8 0.3 squeeze.12
  20.1 0.3 squeeze.11
  20.4 0.1 pad_maximum_fusion
  20.5 16.3 %all-to-all-done.recv_ref = f32[64,16,128]{2,1,0:T(8,128)S(1)} async-done(((f32[64,16,128]{2,1,0:T(8,128)}), f32[64,16,128]{2,1,0:T(8,128)S(1)}, u32[]{:S(2)}, u32[]{:S(2)}) %all-to-all-start) | async-done | bytes 524320 | tf_op jit(solution)/shard_map/all_to_all | solution.py:409
  36.9 1.0 mix.1
  37.9 6.2 %all-to-all-start.1 = ((f32[64,16,128]{2,1,0:T(8,128)}), f32[64,16,128]{2,1,0:T(8,128)S(1)}, u32[]{:S(2)}, u32[]{:S(2)}) async-start(f32[64,16,128]{2,1,0:T(8,128)} %get-tuple-element.19), calls=%async_computation.1 | async-start | bytes 1048576 | tf_op jit(solution)/shard_map/all_to_all | solution.py:409
  44.2 0.6 copy-done.10
  44.8 0.7 maps.1
  45.5 0.6 copy-done.5
  46.2 15.1 %all-to-all-done.1.recv_ref = f32[64,16,128]{2,1,0:T(8,128)S(1)} async-done(((f32[64,16,128]{2,1,0:T(8,128)}), f32[64,16,128]{2,1,0:T(8,128)S(1)}, u32[]{:S(2)}, u32[]{:S(2)}) %all-to-all-start.1) | async-done | bytes 524320 | tf_op jit(solution)/shard_map/all_to_all | solution.py:409
  61.3 11.6 %middle.1 = (f32[1088,128]{1,0:T(8,128)S(1)}, bf16[16,256,128]{2,1,0:T(8,128)(2,1)}) custom-call(f32[64,16,128]{2,1,0:T(8,128)S(1)} %all-to-all-done.1.recv_ref, bf16[16,256,128]{2,1,0:T(8,128)(2,1)} %bitcast.22, bf16[16,256,128]{2,1,0:T(8,128)(2,1)} %bitcast.23, f32[256,128]{1,0:T(8,128)} %copy-done.5, bf16[5,256,256]{2,1,0:T(8,128)(2,1)S(1)} %get-tuple-element.21.kron_ref, ...), custom_call_target="tpu_custom_call" | custom-call | tf_op jit(solution)/shard_map/middle/pallas_call | solution.py:378
  72.9 23.8 %all_to_all.25 = f32[64,1,2176]{2,1,0:T(1,128)S(1)} all-to-all(f32[64,1,2176]{2,1,0:T(1,128)S(1)} %bitcast.18), channel_id=1, replica_groups=mesh['batch'=8,'px'=4,'py'=16] {'px','py'}, dimensions={0} | all-to-all | bytes 1114112 | tf_op jit(solution)/shard_map/all_to_all | solution.py:409
  96.7 0.2 mix_back.1
  96.9 23.7 %all_to_all.26 = f32[64,1,2176]{2,1,0:T(1,128)S(1)} all-to-all(f32[64,1,2176]{2,1,0:T(1,128)S(1)} %bitcast.19), channel_id=1, replica_groups=mesh['batch'=8,'px'=4,'py'=16] {'px','py'}, dimensions={0} | all-to-all | bytes 1114112 | tf_op jit(solution)/shard_map/all_to_all | solution.py:409
  120.6 0.7 share.1
  121.3 6.6 %all-to-all-start.4 = ((f32[8,40,128]{2,1,0:T(8,128)}), f32[8,40,128]{2,1,0:T(8,128)S(1)}, u32[]{:S(2)}, u32[]{:S(2)}) async-start(f32[8,40,128]{2,1,0:T(8,128)} %share.1), calls=%async_computation.4 | async-start | bytes 327680 | tf_op jit(solution)/shard_map/all_to_all | solution.py:440
  127.9 1.2 copy-done.4
  129.2 2.5 %input_grad.1 = bf16[16,256,128]{2,1,0:T(8,128)(2,1)} custom-call(f32[1088,128]{1,0:T(8,128)S(1)} %bitcast.16, bf16[16,256,128]{2,1,0:T(8,128)(2,1)S(1)} %copy-done.4, bf16[5,256,256]{2,1,0:T(8,128)(2,1)S(1)} %get-tuple-element.21.kron_ref, bf16[256,512]{1,0:T(8,128)(2,1)S(1)} %copy-done.2, bf16[256,512]{1,0:T(8,128)(2,1)S(1)} %copy-done.1, ...), custom_call_target="tpu_custom_call" | custom-call | tf_op jit(solution)/shard_map/input_grad/pallas_call | solution.py:378
  131.6 6.0 %all-to-all-done.4.recv_ref = f32[8,40,128]{2,1,0:T(8,128)S(1)} async-done(((f32[8,40,128]{2,1,0:T(8,128)}), f32[8,40,128]{2,1,0:T(8,128)S(1)}, u32[]{:S(2)}, u32[]{:S(2)}) %all-to-all-start.4) | async-done | bytes 163872 | tf_op jit(solution)/shard_map/all_to_all | solution.py:440
  137.6 1.4 shared.1
  139.0 0.5 slice_bitcast_fusion
  (22 shorter events, 0.1 us)
Async XLA Ops:
  4.1 15.6 %copy-start.11 = (f32[2,16,16,1,4,16]{5,4,3,2,1,0:T(4,128)S(1)}, f32[2,16,16,1,4,16]{5,4,3,2,1,0:T(4,128)}, u32[]{:S(2)}) copy-start(f32[2,16,16,1,4,16]{5,4,3,2,1,0:T(4,128)} %param.14) | copy-start | bytes 393220
  4.1 32.7 %all-to-all-start = ((f32[64,16,128]{2,1,0:T(8,128)}), f32[64,16,128]{2,1,0:T(8,128)S(1)}, u32[]{:S(2)}, u32[]{:S(2)}) async-start(f32[64,16,128]{2,1,0:T(8,128)} %forward.1), calls=%async_computation | async-start | bytes 1048576 | tf_op jit(solution)/shard_map/all_to_all | solution.py:409
  36.9 24.4 %copy-start.3 = (bf16[256,1024]{1,0:T(8,128)(2,1)S(1)}, bf16[256,1024]{1,0:T(8,128)(2,1)}, u32[]{:S(2)}) copy-start(bf16[256,1024]{1,0:T(8,128)(2,1)} %constant.14.clone.synth_ref) | copy-start | bytes 1572868
  37.8 6.3 %copy-start.7 = (bf16[16,16]{1,0:T(8,128)(2,1)S(1)}, bf16[16,16]{1,0:T(8,128)(2,1)}, u32[]{:S(2)}) copy-start(bf16[16,16]{1,0:T(8,128)(2,1)} %skip_ref.1) | copy-start | bytes 1540
  37.9 6.3 %copy-start.8 = (bf16[16,16]{1,0:T(8,128)(2,1)S(1)}, bf16[16,16]{1,0:T(8,128)(2,1)}, u32[]{:S(2)}) copy-start(bf16[16,16]{1,0:T(8,128)(2,1)} %in_ref.1) | copy-start | bytes 1540
  37.9 6.3 %copy-start.9 = (bf16[16,16]{1,0:T(8,128)(2,1)S(1)}, bf16[16,16]{1,0:T(8,128)(2,1)}, u32[]{:S(2)}) copy-start(bf16[16,16]{1,0:T(8,128)(2,1)} %outer_ref.1) | copy-start | bytes 1540
  37.9 23.4 %copy-start = (f32[64,8,128]{2,1,0:T(8,128)S(1)}, f32[64,8,128]{2,1,0:T(8,128)}, u32[]{:S(2)}) copy-start(f32[64,8,128]{2,1,0:T(8,128)} %constant.13.clone.offset_hbm.offset_ref) | copy-start | bytes 786436
  37.9 23.4 %copy-start.1 = (bf16[256,512]{1,0:T(8,128)(2,1)S(1)}, bf16[256,512]{1,0:T(8,128)(2,1)}, u32[]{:S(2)}) copy-start(bf16[256,512]{1,0:T(8,128)(2,1)} %constant.12.clone.lo_hbm.lo_ref) | copy-start | bytes 786436
  37.9 23.4 %copy-start.2 = (bf16[256,512]{1,0:T(8,128)(2,1)S(1)}, bf16[256,512]{1,0:T(8,128)(2,1)}, u32[]{:S(2)}) copy-start(bf16[256,512]{1,0:T(8,128)(2,1)} %constant.11.clone.hi_hbm.hi_ref) | copy-start | bytes 786436
  37.9 23.4 %all-to-all-start.1 = ((f32[64,16,128]{2,1,0:T(8,128)}), f32[64,16,128]{2,1,0:T(8,128)S(1)}, u32[]{:S(2)}, u32[]{:S(2)}) async-start(f32[64,16,128]{2,1,0:T(8,128)} %get-tuple-element.19), calls=%async_computation.1 | async-start | bytes 1048576 | tf_op jit(solution)/shard_map/all_to_all | solution.py:409
  44.1 0.7 copy-start.10
  44.8 16.5 %copy-start.6 = (bf16[32,128]{1,0:T(8,128)(2,1)S(1)}, bf16[32,128]{1,0:T(8,128)(2,1)}, u32[]{:S(2)}) copy-start(bf16[32,128]{1,0:T(8,128)(2,1)} %constant.10.clone.low_hbm.low_ref) | copy-start | bytes 24580
  45.5 0.7 copy-start.5
  121.3 16.3 %all-to-all-start.4 = ((f32[8,40,128]{2,1,0:T(8,128)}), f32[8,40,128]{2,1,0:T(8,128)S(1)}, u32[]{:S(2)}, u32[]{:S(2)}) async-start(f32[8,40,128]{2,1,0:T(8,128)} %share.1), calls=%async_computation.4 | async-start | bytes 327680 | tf_op jit(solution)/shard_map/all_to_all | solution.py:440
  127.9 1.2 copy-start.4

commit v4 on v3

--- a/solution.py
+++ b/solution.py
@@ -82,11 +82,13 @@
     return lax.axis_index("px") * PY + lax.axis_index("py")
 
 
-def forward_part(get, low_ref, hi_ref, lo_ref, off_ref, turn_ref, put):
+def forward_part(get, low_ref, hi_ref, lo_ref, off_ref, turn_ref, put, ready=None):
     low = low_ref[...]
     rows = [dot_nt(low, get(c)) for c in range(C)]
     both = jnp.concatenate([r[:C] for r in rows] + [r[C:] for r in rows], axis=0)
     x_hi, x_lo = split(both)
+    if ready is not None:
+        ready()
     hi = hi_ref[...]
     part = dot(x_hi, hi) + dot(x_lo, hi) + dot(x_hi, lo_ref[...])
     for mb in range(PX):
@@ -130,27 +132,29 @@
     field_hbm, low_hbm, hi_hbm, lo_hbm, offset_hbm, out_ref,
     field_ref, low_ref, hi_ref, lo_ref, off_ref, turn_ref, sems,
 ):
-    copies = [
-        pltpu.make_async_copy(a, b, sems.at[i])
-        for i, (a, b) in enumerate(
-            (
-                (low_hbm, low_ref),
-                (field_hbm, field_ref),
-                (hi_hbm, hi_ref),
-                (lo_hbm, lo_ref),
-                (offset_hbm.at[my_place()], off_ref),
-            )
-        )
-    ]
+    pairs = [(low_hbm, low_ref)]
+    for i in range(4):
+        part = pl.ds(4 * i, 4)
+        pairs.append((field_hbm.at[part], field_ref.at[part]))
+    pairs += [(hi_hbm, hi_ref), (lo_hbm, lo_ref), (offset_hbm.at[my_place()], off_ref)]
+    copies = [pltpu.make_async_copy(a, b, sems.at[i]) for i, (a, b) in enumerate(pairs)]
     for copy in copies:
         copy.start()
-    for copy in copies:
-        copy.wait()
+    copies[0].wait()
+
+    def get(c):
+        if c % 4 == 0:
+            copies[1 + c // 4].wait()
+        return field_ref[c]
+
+    def ready():
+        for copy in copies[5:]:
+            copy.wait()
 
     def put(d, value):
         out_ref[d] = value
 
-    forward_part(lambda c: field_ref[c], low_ref, hi_ref, lo_ref, off_ref, turn_ref, put)
+    forward_part(get, low_ref, hi_ref, lo_ref, off_ref, turn_ref, put, ready)
 
 
 def spread_map(w, transpose):
@@ -167,16 +171,33 @@
     return jnp.where(r % 16 == l % 16, full, 0.0).astype(bf16)
 
 
-def k_maps(skip_ref, in_ref, outer_ref, bias_in_ref, kron_ref, bias_ref):
-    kron_ref[0] = spread_map(skip_ref[...], False)
-    kron_ref[1] = spread_map(in_ref[...], False)
-    kron_ref[2] = spread_map(outer_ref[...], True)
-    kron_ref[3] = spread_map(in_ref[...], True)
-    kron_ref[4] = spread_map(skip_ref[...], True)
+def k_prepare(
+    skip_ref, in_ref, outer_ref, bias_in_ref, field_hbm, cot_hbm,
+    kron_ref, pre_ref, dact_ref, field_ref, cot_ref, sems,
+):
+    copies = [
+        pltpu.make_async_copy(field_hbm, field_ref, sems.at[0]),
+        pltpu.make_async_copy(cot_hbm, cot_ref, sems.at[1]),
+    ]
+    for copy in copies:
+        copy.start()
+    skip = spread_map(skip_ref[...], False)
+    outer = spread_map(outer_ref[...], True)
+    kron_ref[0] = spread_map(in_ref[...], False)
+    kron_ref[1] = spread_map(in_ref[...], True)
+    kron_ref[2] = spread_map(skip_ref[...], True)
     r = lax.broadcasted_iota(jnp.int32, (256, C), 0)
     l = lax.broadcasted_iota(jnp.int32, (256, C), 1)
-    column = jnp.sum(jnp.where(r // 16 == l, bias_in_ref[...], 0.0), axis=1, keepdims=True)
-    bias_ref[...] = jnp.broadcast_to(column, (256, N))
+    bias = jnp.sum(jnp.where(r // 16 == l, bias_in_ref[...], 0.0), axis=1, keepdims=True)
+    for copy in copies:
+        copy.wait()
+
+    def step(p, carry):
+        untile(pre_ref, p, dot(skip, tile(field_ref, p)) + bias)
+        untile(dact_ref, p, dot(outer, tile(cot_ref, p)))
+        return carry
+
+    lax.fori_loop(0, XY // 32, step, 0, unroll=2)
 
 
 def k_mix(recv_ref, wa_ref, wb_ref, u_ref, out_ref):
@@ -224,23 +245,12 @@
 
 
 def k_middle(
-    recv_ref, field_hbm, cot_hbm, bias_hbm, kron_ref, low_ref, hi_ref, lo_ref, offset_ref, synth_ref,
+    recv_ref, field_ref, cot_ref, pre_ref, dact_ref, kron_ref, low_ref, hi_ref, lo_ref, offset_ref, synth_ref,
     out_ref, dpre_hbm,
-    field_ref, cot_ref, bias_ref, dpre_ref, sems, turn_ref, g_ref, skip_acc, bias_acc, in_acc, out_acc,
+    dpre_ref, sems, turn_ref, g_ref, skip_acc, bias_acc, in_acc, out_acc,
 ):
-    copies = [
-        pltpu.make_async_copy(a, b, sems.at[i])
-        for i, (a, b) in enumerate(
-            ((field_hbm, field_ref), (cot_hbm, cot_ref), (bias_hbm, bias_ref))
-        )
-    ]
-    for copy in copies:
-        copy.start()
     off_ref = offset_ref.at[my_place()]
     inverse_part(lambda d: recv_ref[d], hi_ref, lo_ref, off_ref, synth_ref, turn_ref, g_ref)
-    for copy in copies:
-        copy.wait()
-    bias = jnp.concatenate([bias_ref[...], bias_ref[...]], axis=1)
     skip_acc[...] = jnp.zeros_like(skip_acc)
     in_acc[...] = jnp.zeros_like(in_acc)
     out_acc[...] = jnp.zeros_like(out_acc)
@@ -249,13 +259,13 @@
     def step(p, carry):
         f = tile(field_ref, p)
         cot = tile(cot_ref, p)
-        pre = tile(g_ref, p) + dot(kron_ref[0], f) + bias
+        pre = tile(g_ref, p) + tile(pre_ref, p)
         hid, d_hid = gelu_parts(pre)
         hid = hid.astype(bf16)
-        act, d_act = gelu_parts(dot(kron_ref[1], hid))
+        act, d_act = gelu_parts(dot(kron_ref[0], hid))
         act = act.astype(bf16)
-        d_inner = (dot(kron_ref[2], cot) * d_act).astype(bf16)
-        dpre = dot(kron_ref[3], d_inner) * d_hid
+        d_inner = (tile(dact_ref, p) * d_act).astype(bf16)
+        dpre = dot(kron_ref[1], d_inner) * d_hid
         dpre = dpre.astype(bf16)
         untile(dpre_ref, p, dpre)
         skip_acc[...] += dot_nt(dpre, f)
@@ -264,8 +274,8 @@
         bias_acc[...] += dpre.astype(f32)
         return carry
 
-    lax.fori_loop(0, XY // 32, step, 0)
-    copy = pltpu.make_async_copy(dpre_ref, dpre_hbm, sems.at[3])
+    lax.fori_loop(0, XY // 32, step, 0, unroll=XY // 32)
+    copy = pltpu.make_async_copy(dpre_ref, dpre_hbm, sems.at[0])
     copy.start()
     bias = bias_acc[...].reshape(C, 16, 256).sum(axis=1)
     total = jnp.sum(bias, axis=1, keepdims=True)
@@ -319,7 +329,7 @@
     steps = XY // 32
     copies = []
     for p in range(steps):
-        untile(out_ref, p, (dot(kron_ref[4], tile(dpre_ref, p)) + tile(g_ref, p)).astype(bf16))
+        untile(out_ref, p, (dot(kron_ref[2], tile(dpre_ref, p)) + tile(g_ref, p)).astype(bf16))
         part = pl.ds(p * 32, 32)
         copies.append(pltpu.make_async_copy(out_ref.at[:, part], out_hbm.at[:, part], sems.at[p]))
         copies[-1].start()
@@ -363,16 +373,18 @@
         )
         two = jnp.where(l // C == r % 8, two, 0.0)
         ref[...] = jnp.dot(two, pick, precision=lax.Precision.HIGHEST, preferred_element_type=f32)
-    bias_ref[...] = jnp.broadcast_to(small[6:7], (8, LANES))
-
-
-def call(body, name, outs, scratch, *args, hbm_in=(), hbm_out=()):
+    bias_ref[...] = small[6, :C]
+
+
+def call(body, name, outs, scratch, *args, hbm_in=(), vmem_in=(), hbm_out=()):
     vm = pl.BlockSpec(memory_space=pltpu.VMEM)
     hbm = pl.BlockSpec(memory_space=pltpu.HBM)
     many = isinstance(outs, (list, tuple))
     out_specs = [hbm if i in hbm_out else vm for i in range(len(outs) if many else 1)]
     args = [
-        pltpu.with_memory_space_constraint(a, pltpu.HBM) if i in hbm_in else a
+        pltpu.with_memory_space_constraint(a, pltpu.HBM) if i in hbm_in
+        else pltpu.with_memory_space_constraint(a, pltpu.VMEM) if i in vmem_in
+        else a
         for i, a in enumerate(args)
     ]
     return pl.pallas_call(
@@ -390,6 +402,30 @@
     return jax.ShapeDtypeStruct(dims, dtype)
 
 
+def run_prepare(skip_weight, mlp_in, mlp_out, skip_bias, field, cotangent):
+    return call(
+        k_prepare, "prepare",
+        [pltpu.VMEM((3, 256, 256), bf16), pltpu.VMEM((C, XY, N), f32), pltpu.VMEM((C, XY, N), f32),
+         pltpu.VMEM((C, XY, N), bf16), pltpu.VMEM((C, XY, N), bf16)],
+        [pltpu.SemaphoreType.DMA((2,))],
+        skip_weight, mlp_in, mlp_out, skip_bias.reshape(1, C), field, cotangent, hbm_in=(4, 5),
+    )
+
+
+def run_middle(recv, field, cotangent, pre, dact, kron, low, hi, lo, offset, synth):
+    turn = pltpu.VMEM((2 * PX, PY * C, LANES), f32)
+    cells = pltpu.VMEM((C, XY, N), f32)
+    square = pltpu.VMEM((256, 256), f32)
+    return call(
+        k_middle, "middle",
+        [pltpu.VMEM((PEERS * ROWS, LANES), f32), pltpu.HBM((C, XY, N), bf16)],
+        [pltpu.VMEM((C, XY, N), bf16), pltpu.SemaphoreType.DMA((1,)),
+         turn, cells, square, square, square, square],
+        recv, field, cotangent, pre, dact, kron, low, hi, lo, offset, synth,
+        hbm_out=(1,), vmem_in=(1, 2, 3, 4, 5),
+    )
+
+
 def shards(field, cotangent, spec_weight, skip_weight, skip_bias, mlp_in, mlp_out):
     low, hi, lo, offset, synth = [jnp.asarray(t) for t in tables()]
     field = field.reshape(C, XY, N)
@@ -401,7 +437,6 @@
     twice = pltpu.VMEM((2 * PX, PY * C, LANES), f32)
     cells = pltpu.VMEM((C, XY, N), f32)
     cells_low = pltpu.VMEM((C, XY, N), bf16)
-    square = pltpu.VMEM((256, 256), f32)
     own = pltpu.VMEM((8, LANES), f32)
     plane = pltpu.VMEM((XY, PX * LANES), bf16)
 
@@ -412,28 +447,23 @@
         return exchange(block.reshape(PEERS, 1, ROWS * LANES)).reshape(PEERS * ROWS, LANES)
 
     sent = call(
-        k_forward, "forward", shape(PEERS, C, LANES),
-        [cells_low, pltpu.VMEM((2 * C, N), bf16), plane, plane, own, turn, pltpu.SemaphoreType.DMA((5,))],
+        k_forward, "forward", pltpu.VMEM((PEERS, C, LANES), f32),
+        [cells_low, pltpu.VMEM((2 * C, N), bf16), plane, plane, own, turn, pltpu.SemaphoreType.DMA((8,))],
         field, low, hi, lo, offset, hbm_in=range(5),
     )
-    kron, bias = call(
-        k_maps, "maps", [shape(5, 256, 256, dtype=bf16), shape(256, N)], [],
-        skip_weight, mlp_in, mlp_out, skip_bias.reshape(1, C),
+    kron, pre, dact, field, cotangent = run_prepare(
+        skip_weight, mlp_in, mlp_out, skip_bias, field, cotangent
     )
     u, sent = call(
-        k_mix, "mix", [shape(C, LANES), shape(PEERS, C, LANES)], [], exchange(sent), wa, wb
-    )
-    sent, dpre = call(
-        k_middle, "middle",
-        [shape(PEERS * ROWS, LANES), pltpu.HBM((C, XY, N), bf16)],
-        [cells_low, cells_low, pltpu.VMEM((256, N), f32), cells_low, pltpu.SemaphoreType.DMA((4,)),
-         twice, cells, square, square, square, square],
-        exchange(sent), field, cotangent, bias, kron, low, hi, lo, offset, synth,
-        hbm_in=(1, 2, 3), hbm_out=(1,),
+        k_mix, "mix", [shape(C, LANES), pltpu.VMEM((PEERS, C, LANES), f32)], [],
+        exchange(sent), wa, wb, vmem_in=(1, 2),
+    )
+    sent, dpre = run_middle(
+        exchange(sent), field, cotangent, pre, dact, kron, low, hi, lo, offset, synth
     )
     sent, g = call(
-        k_mix_back, "mix_back", [shape(PEERS * ROWS, LANES), shape(C, LANES)], [],
-        exchange_rows(sent), wa, wb,
+        k_mix_back, "mix_back", [pltpu.VMEM((PEERS * ROWS, LANES), f32), shape(C, LANES)], [],
+        exchange_rows(sent), wa, wb, vmem_in=(1, 2),
     )
     back = exchange_rows(sent)
     share = call(k_share, "share", shape(NB, 2 * C + 8, LANES), [], back, u, g)
@@ -445,11 +475,11 @@
     )
     spec, skip, b, inner, outer = call(
         k_shared, "shared",
-        [shape(2, C, ML, 2, C), shape(C, C), shape(8, LANES), shape(C, C), shape(C, C)],
+        [shape(2, C, ML, 2, C), shape(C, C), shape(C), shape(C, C), shape(C, C)],
         [pltpu.VMEM((256, LANES), f32)] * 2, share,
     )
     spec = spec.transpose(0, 1, 4, 2, 3).reshape(2, C, C, 1, ML, 2)
-    return (grad_input.reshape(1, C, XL, YL, N), spec, skip, b[0, :C], inner, outer)
+    return (grad_input.reshape(1, C, XL, YL, N), spec, skip, b, inner, outer)
 
 
 def solution(mesh):

time: 141 us -> 142 us (level)
  local copies, waits for them, and re-layouts: 3.66 us -> 10.5 us
  waiting for transfers between devices: 37.5 us -> 33.5 us
  Pallas kernels: 21.5 us -> 18.6 us
    unnamed x24 -> x52, local copies, waits for them, and re-layouts: 2.53 us -> 9.88 us
    all_to_all x2, waiting for transfers between devices: 31.4 us -> 26.3 us  [exchange(): return lax.all_to_all(block, ('px', 'py'), 0, 0, tiled=True)]
    pallas_call x8, Pallas kernels: 21.5 us -> 18.6 us  [call(): pl.pallas_call(body, out_shape=outs, in_specs=[hbm if i in hbm_in else vm...]
  transfers between devices with their start and end apart: 3 -> 3, of which waited for: 3 -> 3; matrix products, arithmetic and copies ran while one was open for 1% -> 1% of each run, Pallas kernels for 2% -> 4%
where the time goes in v4:
time: 142 us; the launch traced here: 140 us
  blocking collectives  47.7 us (34%)
  waiting for transfers between devices  33.5 us (24%)
  starting transfers between devices  28.3 us (20%)
  Pallas kernels  18.6 us (13%)
  local copies, waits for them, and re-layouts  10.5 us (7%)
    all_to_all x2, blocking collectives, exchange(): return lax.all_to_all(block, ('px', 'py'), 0, 0, tiled=True)  47.7 us
    all_to_all x2, waiting for transfers between devices, exchange(): return lax.all_to_all(block, ('px', 'py'), 0, 0, tiled=True)  26.3 us
    all_to_all x2, starting transfers between devices, exchange(): return lax.all_to_all(block, ('px', 'py'), 0, 0, tiled=True)  21.7 us
    pallas_call x8, Pallas kernels, call(): pl.pallas_call(body, out_shape=outs, in_specs=[hbm if i in hbm_in else vm...  18.6 us
    unnamed x52, local copies, waits for them, and re-layouts  9.88 us
    all_to_all x1, waiting for transfers between devices, shards(): share = lax.all_to_all(share, 'batch', 0, 0, tiled=True)  7.19 us
    all_to_all x1, starting transfers between devices, shards(): share = lax.all_to_all(share, 'batch', 0, 0, tiled=True)  6.6 us
  transfers between devices with their start and end apart: 3, of which 3 were waited for; matrix products, arithmetic and copies ran while one was open for 1% of the time, Pallas kernels for 4%

profile of v4, /device:TPU:1, one launch (start us, length us, event | category | flops | bytes accessed | tf_op | source)
XLA Modules:
  0.0 139.7 jit_solution(3023369793162467954)
XLA Ops:
  0.6 3.6 %forward.1 = f32[64,16,128]{2,1,0:T(8,128)} custom-call(bf16[16,256,128]{2,1,0:T(8,128)(2,1)} %bitcast.19, bf16[32,128]{1,0:T(8,128)(2,1)} %constant.10.clone.low_hbm.low_ref, bf16[256,512]{1,0:T(8,128)(2,1)} %constant.11.clone.hi_hbm.hi_ref, bf16[256,512]{1,0:T(8,128)(2,1)} %constant.12.clone.lo_hbm.lo_ref, f32[64,8,128]{2,1,0:T(8,128)} %constant.13.clone.offset_hbm.offset_ref), custom_call_target="tpu_custom_call" | custom-call | tf_op jit(solution)/shard_map/forward/pallas_call | solution.py:390
  4.3 15.4 %all-to-all-start = ((f32[64,16,128]{2,1,0:T(8,128)}), f32[64,16,128]{2,1,0:T(8,128)S(1)}, u32[]{:S(2)}, u32[]{:S(2)}) async-start(f32[64,16,128]{2,1,0:T(8,128)} %forward.1), calls=%async_computation | async-start | bytes 1048576 | tf_op jit(solution)/shard_map/all_to_all | solution.py:444
  19.9 0.3 squeeze.9
  20.6 16.2 %all-to-all-done.recv_ref = f32[64,16,128]{2,1,0:T(8,128)S(1)} async-done(((f32[64,16,128]{2,1,0:T(8,128)}), f32[64,16,128]{2,1,0:T(8,128)S(1)}, u32[]{:S(2)}, u32[]{:S(2)}) %all-to-all-start) | async-done | bytes 524320 | tf_op jit(solution)/shard_map/all_to_all | solution.py:444
  36.9 1.0 mix.1
  37.9 6.3 %all-to-all-start.1 = ((f32[64,16,128]{2,1,0:T(8,128)}), f32[64,16,128]{2,1,0:T(8,128)}, u32[]{:S(2)}, u32[]{:S(2)}) async-start(f32[64,16,128]{2,1,0:T(8,128)} %get-tuple-element.22), calls=%async_computation.1 | async-start | bytes 1048576 | tf_op jit(solution)/shard_map/all_to_all | solution.py:444
  44.2 2.8 %prepare.1 = (bf16[3,256,256]{2,1,0:T(8,128)(2,1)S(1)}, f32[16,256,128]{2,1,0:T(8,128)S(1)}, f32[16,256,128]{2,1,0:T(8,128)S(1)}, bf16[16,256,128]{2,1,0:T(8,128)(2,1)S(1)}, bf16[16,256,128]{2,1,0:T(8,128)(2,1)S(1)}) custom-call(bf16[16,16]{1,0:T(8,128)(2,1)S(1)} %copy-done.21, bf16[16,16]{1,0:T(8,128)(2,1)S(1)} %copy-done.22, ...), custom_call_target="tpu_custom_call" | custom-call | tf_op jit(solution)/shard_map/prepare/pallas_call | solution.py:390
  47.1 1.4 copy-done.3
  48.5 0.8 copy-done.7
  49.2 1.0 copy-done.14
  50.2 1.0 copy-done.16
  51.2 10.1 %all-to-all-done.1.recv_ref = f32[64,16,128]{2,1,0:T(8,128)} async-done(((f32[64,16,128]{2,1,0:T(8,128)}), f32[64,16,128]{2,1,0:T(8,128)}, u32[]{:S(2)}, u32[]{:S(2)}) %all-to-all-start.1) | async-done | bytes 524320 | tf_op jit(solution)/shard_map/all_to_all | solution.py:444
  61.3 1.6 %copy-done.4 = f32[16,256,128]{2,1,0:T(8,128)S(1)} copy-done((f32[16,256,128]{2,1,0:T(8,128)S(1)}, f32[16,256,128]{2,1,0:T(8,128)}, u32[]{:S(2)}) %copy-start.4) | copy-done | bytes 2097176
  62.9 1.0 copy-done.8
  63.9 1.2 copy-done.15
  65.1 1.2 copy-done.17
  66.3 7.1 %middle.1 = (f32[1088,128]{1,0:T(8,128)S(1)}, bf16[16,256,128]{2,1,0:T(8,128)(2,1)}) custom-call(f32[64,16,128]{2,1,0:T(8,128)} %all-to-all-done.1.recv_ref, bf16[16,256,128]{2,1,0:T(8,128)(2,1)S(1)} %copy-done.15, bf16[16,256,128]{2,1,0:T(8,128)(2,1)S(1)} %copy-done.17, f32[16,256,128]{2,1,0:T(8,128)S(1)} %get-tuple-element.25.pre_ref, ...), custom_call_target="tpu_custom_call" | custom-call | tf_op jit(solution)/shard_map/middle/pallas_call | solution.py:390
  73.5 23.9 %all_to_all.25 = f32[64,1,2176]{2,1,0:T(1,128)S(1)} all-to-all(f32[64,1,2176]{2,1,0:T(1,128)S(1)} %bitcast.16), channel_id=1, replica_groups=mesh['batch'=8,'px'=4,'py'=16] {'px','py'}, dimensions={0} | all-to-all | bytes 1114112 | tf_op jit(solution)/shard_map/all_to_all | solution.py:444
  97.6 23.7 %all_to_all.26 = f32[64,1,2176]{2,1,0:T(1,128)S(1)} all-to-all(f32[64,1,2176]{2,1,0:T(1,128)S(1)} %bitcast.17), channel_id=1, replica_groups=mesh['batch'=8,'px'=4,'py'=16] {'px','py'}, dimensions={0} | all-to-all | bytes 1114112 | tf_op jit(solution)/shard_map/all_to_all | solution.py:444
  121.3 0.7 copy-done.19
  122.0 6.6 %all-to-all-start.4 = ((f32[8,40,128]{2,1,0:T(8,128)}), f32[8,40,128]{2,1,0:T(8,128)S(1)}, u32[]{:S(2)}, u32[]{:S(2)}) async-start(f32[8,40,128]{2,1,0:T(8,128)} %copy-done.19), calls=%async_computation.4 | async-start | bytes 327680 | tf_op jit(solution)/shard_map/all_to_all | solution.py:470
  128.6 2.5 %input_grad.1 = bf16[16,256,128]{2,1,0:T(8,128)(2,1)} custom-call(f32[1088,128]{1,0:T(8,128)S(1)} %bitcast.14, bf16[16,256,128]{2,1,0:T(8,128)(2,1)S(1)} %copy-done.18, bf16[3,256,256]{2,1,0:T(8,128)(2,1)S(1)} %copy-done.9, bf16[256,512]{1,0:T(8,128)(2,1)S(1)} %copy-done.2, bf16[256,512]{1,0:T(8,128)(2,1)S(1)} %copy-done.1, f32[64,8,128]{2,1,0:T(8,128)S(1)} %copy-done, ...), custom_call_target="tpu_custom_call" | custom-call | tf_op jit(solution)/shard_map/input_grad/pallas_call | solution.py:390
  131.1 7.2 %all-to-all-done.4.recv_ref = f32[8,40,128]{2,1,0:T(8,128)S(1)} async-done(((f32[8,40,128]{2,1,0:T(8,128)}), f32[8,40,128]{2,1,0:T(8,128)S(1)}, u32[]{:S(2)}, u32[]{:S(2)}) %all-to-all-start.4) | async-done | bytes 163872 | tf_op jit(solution)/shard_map/all_to_all | solution.py:470
  138.3 1.4 shared.1
  (49 shorter events, 0.8 us)
Async XLA Ops:
  0.6 19.1 %copy-start.25 = (f32[2,16,16,1,4,16]{5,4,3,2,1,0:T(4,128)S(1)}, f32[2,16,16,1,4,16]{5,4,3,2,1,0:T(4,128)}, u32[]{:S(2)}) copy-start(f32[2,16,16,1,4,16]{5,4,3,2,1,0:T(4,128)} %param.14) | copy-start | bytes 393220
  4.3 32.6 %all-to-all-start = ((f32[64,16,128]{2,1,0:T(8,128)}), f32[64,16,128]{2,1,0:T(8,128)S(1)}, u32[]{:S(2)}, u32[]{:S(2)}) async-start(f32[64,16,128]{2,1,0:T(8,128)} %forward.1), calls=%async_computation | async-start | bytes 1048576 | tf_op jit(solution)/shard_map/all_to_all | solution.py:444
  19.8 24.4 %copy-start.21 = (bf16[16,16]{1,0:T(8,128)(2,1)S(1)}, bf16[16,16]{1,0:T(8,128)(2,1)}, u32[]{:S(2)}) copy-start(bf16[16,16]{1,0:T(8,128)(2,1)} %skip_ref.1) | copy-start | bytes 1540
  19.8 24.4 %copy-start.22 = (bf16[16,16]{1,0:T(8,128)(2,1)S(1)}, bf16[16,16]{1,0:T(8,128)(2,1)}, u32[]{:S(2)}) copy-start(bf16[16,16]{1,0:T(8,128)(2,1)} %in_ref.1) | copy-start | bytes 1540
  19.9 24.4 %copy-start.23 = (bf16[16,16]{1,0:T(8,128)(2,1)S(1)}, bf16[16,16]{1,0:T(8,128)(2,1)}, u32[]{:S(2)}) copy-start(bf16[16,16]{1,0:T(8,128)(2,1)} %outer_ref.1) | copy-start | bytes 1540
  19.9 24.3 %copy-start.24 = (f32[16]{0:T(128)S(1)}, f32[16]{0:T(128)}, u32[]{:S(2)}) copy-start(f32[16]{0:T(128)} %param.16) | copy-start | bytes 196
  20.6 23.6 %copy-start.10 = (f32[16,16,128]{2,1,0:T(8,128)}, f32[16,16,128]{2,1,0:T(8,128)S(1)}, u32[]{:S(2)}) copy-start(f32[16,16,128]{2,1,0:T(8,128)S(1)} %get-tuple-element.52.wa_ref) | copy-start | bytes 393220
  20.6 23.6 %copy-start.12 = (f32[16,16,128]{2,1,0:T(8,128)}, f32[16,16,128]{2,1,0:T(8,128)S(1)}, u32[]{:S(2)}) copy-start(f32[16,16,128]{2,1,0:T(8,128)S(1)} %get-tuple-element.53.wb_ref) | copy-start | bytes 393220
  20.6 40.7 %copy-start = (f32[64,8,128]{2,1,0:T(8,128)S(1)}, f32[64,8,128]{2,1,0:T(8,128)}, u32[]{:S(2)}) copy-start(f32[64,8,128]{2,1,0:T(8,128)} %constant.13.clone.offset_hbm.offset_ref) | copy-start | bytes 786436
  20.6 40.7 %copy-start.1 = (bf16[256,512]{1,0:T(8,128)(2,1)S(1)}, bf16[256,512]{1,0:T(8,128)(2,1)}, u32[]{:S(2)}) copy-start(bf16[256,512]{1,0:T(8,128)(2,1)} %constant.12.clone.lo_hbm.lo_ref) | copy-start | bytes 786436
  20.6 40.7 %copy-start.2 = (bf16[256,512]{1,0:T(8,128)(2,1)S(1)}, bf16[256,512]{1,0:T(8,128)(2,1)}, u32[]{:S(2)}) copy-start(bf16[256,512]{1,0:T(8,128)(2,1)} %constant.11.clone.hi_hbm.hi_ref) | copy-start | bytes 786436
  20.6 40.6 %copy-start.5 = (bf16[256,1024]{1,0:T(8,128)(2,1)S(1)}, bf16[256,1024]{1,0:T(8,128)(2,1)}, u32[]{:S(2)}) copy-start(bf16[256,1024]{1,0:T(8,128)(2,1)} %constant.14.clone.synth_ref) | copy-start | bytes 1572868
  20.6 40.6 %copy-start.20 = (bf16[32,128]{1,0:T(8,128)(2,1)S(1)}, bf16[32,128]{1,0:T(8,128)(2,1)}, u32[]{:S(2)}) copy-start(bf16[32,128]{1,0:T(8,128)(2,1)} %constant.10.clone.low_hbm.low_ref) | copy-start | bytes 24580
  37.9 23.4 %all-to-all-start.1 = ((f32[64,16,128]{2,1,0:T(8,128)}), f32[64,16,128]{2,1,0:T(8,128)}, u32[]{:S(2)}, u32[]{:S(2)}) async-start(f32[64,16,128]{2,1,0:T(8,128)} %get-tuple-element.22), calls=%async_computation.1 | async-start | bytes 1048576 | tf_op jit(solution)/shard_map/all_to_all | solution.py:444
  47.1 1.4 copy-start.3
  61.3 1.6 %copy-start.4 = (f32[16,256,128]{2,1,0:T(8,128)S(1)}, f32[16,256,128]{2,1,0:T(8,128)}, u32[]{:S(2)}) copy-start(f32[16,256,128]{2,1,0:T(8,128)} %copy-done.3) | copy-start | bytes 6291460
  63.9 1.2 copy-start.15
  65.1 1.2 copy-start.17
  66.3 31.1 %copy-start.11 = (f32[16,16,128]{2,1,0:T(8,128)S(1)}, f32[16,16,128]{2,1,0:T(8,128)}, u32[]{:S(2)}) copy-start(f32[16,16,128]{2,1,0:T(8,128)} %copy-done.10) | copy-start | bytes 393220
  66.3 31.1 %copy-start.13 = (f32[16,16,128]{2,1,0:T(8,128)S(1)}, f32[16,16,128]{2,1,0:T(8,128)}, u32[]{:S(2)}) copy-start(f32[16,16,128]{2,1,0:T(8,128)} %copy-done.12) | copy-start | bytes 393220
  73.4 55.2 %copy-start.6 = (bf16[256,1024]{1,0:T(8,128)(2,1)S(1)}, bf16[256,1024]{1,0:T(8,128)(2,1)}, u32[]{:S(2)}) copy-start(bf16[256,1024]{1,0:T(8,128)(2,1)} %constant.14.clone.synth_ref) | copy-start | bytes 1572868
  73.5 55.2 %copy-start.9 = (bf16[3,256,256]{2,1,0:T(8,128)(2,1)S(1)}, bf16[3,256,256]{2,1,0:T(8,128)(2,1)}, u32[]{:S(2)}) copy-start(bf16[3,256,256]{2,1,0:T(8,128)(2,1)} %copy-done.7) | copy-start | bytes 1179652
  73.5 55.2 %copy-start.18 = (bf16[16,256,128]{2,1,0:T(8,128)(2,1)S(1)}, bf16[16,256,128]{2,1,0:T(8,128)(2,1)}, u32[]{:S(2)}) copy-start(bf16[16,256,128]{2,1,0:T(8,128)(2,1)} %get-tuple-element.30.dpre_ref) | copy-start | bytes 3145732
  122.0 16.3 %all-to-all-start.4 = ((f32[8,40,128]{2,1,0:T(8,128)}), f32[8,40,128]{2,1,0:T(8,128)S(1)}, u32[]{:S(2)}, u32[]{:S(2)}) async-start(f32[8,40,128]{2,1,0:T(8,128)} %copy-done.19), calls=%async_computation.4 | async-start | bytes 327680 | tf_op jit(solution)/shard_map/all_to_all | solution.py:470
  (5 other events, 4.4 us)

commit v5 on v4

--- a/solution.py
+++ b/solution.py
@@ -18,10 +18,13 @@
 XY = XL * YL
 ML = C // PX
 PEERS = PX * PY
+STEPS = XY // 32
+HALF = XY // 2
 ROWS = C + 1
 LANES = 128
 SIGMA = 1.0 / math.sqrt(N**3)
 RHO = 1.0 / math.sqrt(NB * N**3)
+KEPT = f32
 NT = (((1,), (1,)), ((), ()))
 
 
@@ -53,7 +56,17 @@
             np.einsum("ab,kz->akbz", eye, -sin_z).reshape(8 * C, 8 * N),
         ]
     ).astype(ml_dtypes.bfloat16)
-    return low, plane_hi, plane_lo, offset, synth
+    low = np.pad(low.astype(np.float32), ((0, 0), (0, PX * LANES - N))).astype(ml_dtypes.bfloat16)
+    table = np.concatenate([plane_hi, plane_lo, synth[:, : 4 * N], synth[:, 4 * N :], low])
+    return table, offset
+
+
+class Table:
+    def __init__(self, ref):
+        self.hi = ref.at[0:XY, :]
+        self.lo = ref.at[XY : 2 * XY, :]
+        self.synth = [ref.at[2 * XY : 3 * XY, :], ref.at[3 * XY : 4 * XY, :]]
+        self.low = ref.at[4 * XY : 4 * XY + 2 * C, 0:N]
 
 
 def dot(a, b):
@@ -82,15 +95,15 @@
     return lax.axis_index("px") * PY + lax.axis_index("py")
 
 
-def forward_part(get, low_ref, hi_ref, lo_ref, off_ref, turn_ref, put, ready=None):
-    low = low_ref[...]
+def forward_part(get, table, off_ref, turn_ref, put, ready=None):
+    low = table.low[...]
     rows = [dot_nt(low, get(c)) for c in range(C)]
     both = jnp.concatenate([r[:C] for r in rows] + [r[C:] for r in rows], axis=0)
     x_hi, x_lo = split(both)
     if ready is not None:
         ready()
-    hi = hi_ref[...]
-    part = dot(x_hi, hi) + dot(x_lo, hi) + dot(x_hi, lo_ref[...])
+    hi = table.hi[...]
+    part = dot(x_hi, hi) + dot(x_lo, hi) + dot(x_hi, table.lo[...])
     for mb in range(PX):
         pa = part[: C * C, mb * LANES : (mb + 1) * LANES]
         pb = part[C * C :, mb * LANES : (mb + 1) * LANES]
@@ -101,7 +114,7 @@
             put(mb * PY + k, turn_ref[mb, pl.ds(k, C, stride=C), :])
 
 
-def inverse_part(block, hi_ref, lo_ref, off_ref, synth_ref, turn_ref, g_ref):
+def inverse_part(block, table, off_ref, turn_ref, g_ref):
     for mb in range(PX):
         v = jnp.concatenate([block(mb * PY + k) for k in range(PY)], axis=0)
         r = turned(v)
@@ -117,26 +130,27 @@
                 )
             )
     v_hi, v_lo = split(jnp.concatenate(rows, axis=0))
-    hi = hi_ref[...]
-    z = dot_nt(hi, v_hi) + dot_nt(hi, v_lo) + dot_nt(lo_ref[...], v_hi)
+    hi = table.hi[...]
+    z = dot_nt(hi, v_hi) + dot_nt(hi, v_lo) + dot_nt(table.lo[...], v_hi)
     z = z.astype(bf16)
     for ob in range(2):
         re = z[:, ob * LANES : (ob + 1) * LANES]
         im = z[:, C * C + ob * LANES : C * C + (ob + 1) * LANES]
-        g = dot(jnp.concatenate([re, im], axis=1), synth_ref[...])
-        for o in range(8):
-            g_ref[ob * 8 + o] = g[:, o * N : (o + 1) * N]
-
-
-def k_forward(
-    field_hbm, low_hbm, hi_hbm, lo_hbm, offset_hbm, out_ref,
-    field_ref, low_ref, hi_ref, lo_ref, off_ref, turn_ref, sems,
-):
-    pairs = [(low_hbm, low_ref)]
+        both = jnp.concatenate([re, im], axis=1)
+        for half in range(2):
+            g = dot(both, table.synth[half][...])
+            for o in range(4):
+                g_ref[ob * 8 + half * 4 + o] = g[:, o * N : (o + 1) * N]
+
+
+def k_forward(field_hbm, table_hbm, offset_hbm, out_ref, field_ref, table_ref, off_ref, turn_ref, sems):
+    low_rows, plane_rows = pl.ds(4 * XY, 2 * C), pl.ds(0, 2 * XY)
+    pairs = [(table_hbm.at[low_rows], table_ref.at[low_rows])]
     for i in range(4):
         part = pl.ds(4 * i, 4)
         pairs.append((field_hbm.at[part], field_ref.at[part]))
-    pairs += [(hi_hbm, hi_ref), (lo_hbm, lo_ref), (offset_hbm.at[my_place()], off_ref)]
+    pairs.append((table_hbm.at[plane_rows], table_ref.at[plane_rows]))
+    pairs.append((offset_hbm.at[my_place()], off_ref))
     copies = [pltpu.make_async_copy(a, b, sems.at[i]) for i, (a, b) in enumerate(pairs)]
     for copy in copies:
         copy.start()
@@ -154,7 +168,7 @@
     def put(d, value):
         out_ref[d] = value
 
-    forward_part(get, low_ref, hi_ref, lo_ref, off_ref, turn_ref, put, ready)
+    forward_part(get, Table(table_ref), off_ref, turn_ref, put, ready)
 
 
 def spread_map(w, transpose):
@@ -173,7 +187,7 @@
 
 def k_prepare(
     skip_ref, in_ref, outer_ref, bias_in_ref, field_hbm, cot_hbm,
-    kron_ref, pre_ref, dact_ref, field_ref, cot_ref, sems,
+    kron_ref, pre_hbm, dact_hbm, field_ref, cot_ref, pre_ref, dact_ref, sems,
 ):
     copies = [
         pltpu.make_async_copy(field_hbm, field_ref, sems.at[0]),
@@ -193,21 +207,37 @@
         copy.wait()
 
     def step(p, carry):
-        untile(pre_ref, p, dot(skip, tile(field_ref, p)) + bias)
-        untile(dact_ref, p, dot(outer, tile(cot_ref, p)))
+        untile(pre_ref, p, (dot(skip, tile(field_ref, p)) + bias).astype(KEPT))
+        untile(dact_ref, p, dot(outer, tile(cot_ref, p)).astype(KEPT))
         return carry
 
-    lax.fori_loop(0, XY // 32, step, 0, unroll=2)
-
-
-def k_mix(recv_ref, wa_ref, wb_ref, u_ref, out_ref):
+    lax.fori_loop(0, STEPS, step, 0, unroll=2)
+    copies = [
+        pltpu.make_async_copy(pre_ref, pre_hbm, sems.at[0]),
+        pltpu.make_async_copy(dact_ref, dact_hbm, sems.at[1]),
+    ]
+    for copy in copies:
+        copy.start()
+    for copy in copies:
+        copy.wait()
+
+
+def k_mix(recv_ref, wa_ref, wb_ref, u_ref, out_hbm, eight_ref, sems):
     u = jnp.sum(recv_ref[...], axis=0)
     us = pltpu.roll(u, LANES // 2, 1)
     u_ref[...] = u
     v = jnp.zeros((C, LANES), f32)
     for c in range(C):
         v = v + wa_ref[c] * u[c : c + 1, :] + wb_ref[c] * us[c : c + 1, :]
-    out_ref[...] = jnp.broadcast_to(v[None], (PEERS, C, LANES))
+    eight_ref[...] = jnp.broadcast_to(v[None], (8, C, LANES))
+    copies = [
+        pltpu.make_async_copy(eight_ref, out_hbm.at[pl.ds(8 * i, 8)], sems.at[i])
+        for i in range(PEERS // 8)
+    ]
+    for copy in copies:
+        copy.start()
+    for copy in copies:
+        copy.wait()
 
 
 def gelu_parts(x):
@@ -245,18 +275,27 @@
 
 
 def k_middle(
-    recv_ref, field_ref, cot_ref, pre_ref, dact_ref, kron_ref, low_ref, hi_ref, lo_ref, offset_ref, synth_ref,
+    recv_ref, field_ref, cot_ref, pre_hbm, dact_hbm, kron_hbm, table_ref, offset_ref,
     out_ref, dpre_hbm,
-    dpre_ref, sems, turn_ref, g_ref, skip_acc, bias_acc, in_acc, out_acc,
+    pre_ref, dact_ref, kron_ref, dpre_ref, sems, turn_ref, g_ref, skip_acc, bias_acc, in_acc, out_acc,
 ):
+    pairs = [(kron_hbm.at[0:2], kron_ref)]
+    for i in range(2):
+        part = pl.ds(i * HALF, HALF)
+        pairs.append((pre_hbm.at[:, part], pre_ref.at[:, part]))
+        pairs.append((dact_hbm.at[:, part], dact_ref.at[:, part]))
+    copies = [pltpu.make_async_copy(a, b, sems.at[i]) for i, (a, b) in enumerate(pairs)]
+    for copy in copies:
+        copy.start()
     off_ref = offset_ref.at[my_place()]
-    inverse_part(lambda d: recv_ref[d], hi_ref, lo_ref, off_ref, synth_ref, turn_ref, g_ref)
+    table = Table(table_ref)
+    inverse_part(lambda d: recv_ref[d], table, off_ref, turn_ref, g_ref)
     skip_acc[...] = jnp.zeros_like(skip_acc)
     in_acc[...] = jnp.zeros_like(in_acc)
     out_acc[...] = jnp.zeros_like(out_acc)
     bias_acc[...] = jnp.zeros_like(bias_acc)
 
-    def step(p, carry):
+    def step(p):
         f = tile(field_ref, p)
         cot = tile(cot_ref, p)
         pre = tile(g_ref, p) + tile(pre_ref, p)
@@ -272,10 +311,14 @@
         in_acc[...] += dot_nt(d_inner, hid)
         out_acc[...] += dot_nt(cot, act)
         bias_acc[...] += dpre.astype(f32)
-        return carry
-
-    lax.fori_loop(0, XY // 32, step, 0, unroll=XY // 32)
-    copy = pltpu.make_async_copy(dpre_ref, dpre_hbm, sems.at[0])
+
+    copies[0].wait()
+    for p in range(STEPS):
+        if p % (STEPS // 2) == 0:
+            copies[1 + 2 * (p // (STEPS // 2))].wait()
+            copies[2 + 2 * (p // (STEPS // 2))].wait()
+        step(p)
+    copy = pltpu.make_async_copy(dpre_ref, dpre_hbm, sems.at[5])
     copy.start()
     bias = bias_acc[...].reshape(C, 16, 256).sum(axis=1)
     total = jnp.sum(bias, axis=1, keepdims=True)
@@ -290,7 +333,7 @@
     def put(d, value):
         out_ref[d * ROWS : (d + 1) * ROWS, :] = jnp.concatenate([value, small[d : d + 1]], axis=0)
 
-    forward_part(lambda c: dpre_ref[c], low_ref, hi_ref, lo_ref, off_ref, turn_ref, put)
+    forward_part(lambda c: dpre_ref[c], table, off_ref, turn_ref, put)
     copy.wait()
 
 
@@ -311,22 +354,25 @@
         out_ref[i * 8 * ROWS : (i + 1) * 8 * ROWS, :] = slab
 
 
-def k_share(back_ref, u_ref, g_ref, share_ref):
+def k_share(back_ref, u_ref, g_ref, share_hbm, block_ref, sems):
     small = back_ref[pl.ds(C, PEERS, stride=ROWS), :].reshape(8, 8, LANES).sum(axis=1)
-    share = jnp.concatenate([u_ref[...], g_ref[...], small], axis=0)
-    share_ref[...] = jnp.broadcast_to(share[None], (NB, 2 * C + 8, LANES))
+    block_ref[...] = jnp.concatenate([u_ref[...], g_ref[...], small], axis=0)
+    copies = [pltpu.make_async_copy(block_ref, share_hbm.at[i], sems.at[i]) for i in range(NB)]
+    for copy in copies:
+        copy.start()
+    for copy in copies:
+        copy.wait()
 
 
 def k_input(
-    recv_ref, dpre_ref, kron_ref, hi_ref, lo_ref, offset_ref, synth_ref, out_hbm,
+    recv_ref, dpre_ref, kron_ref, table_ref, offset_ref, out_hbm,
     out_ref, turn_ref, g_ref, sems,
 ):
+    steps = XY // 32
     off_ref = offset_ref.at[my_place()]
     inverse_part(
-        lambda d: recv_ref[d * ROWS : d * ROWS + C, :],
-        hi_ref, lo_ref, off_ref, synth_ref, turn_ref, g_ref,
-    )
-    steps = XY // 32
+        lambda d: recv_ref[d * ROWS : d * ROWS + C, :], Table(table_ref), off_ref, turn_ref, g_ref
+    )
     copies = []
     for p in range(steps):
         untile(out_ref, p, (dot(kron_ref[2], tile(dpre_ref, p)) + tile(g_ref, p)).astype(bf16))
@@ -402,32 +448,35 @@
     return jax.ShapeDtypeStruct(dims, dtype)
 
 
+CELLS = pltpu.VMEM((C, XY, N), f32)
+CELLS_LOW = pltpu.VMEM((C, XY, N), bf16)
+CELLS_KEPT = pltpu.VMEM((C, XY, N), KEPT)
+OWN = pltpu.VMEM((8, LANES), f32)
+
+
 def run_prepare(skip_weight, mlp_in, mlp_out, skip_bias, field, cotangent):
     return call(
         k_prepare, "prepare",
-        [pltpu.VMEM((3, 256, 256), bf16), pltpu.VMEM((C, XY, N), f32), pltpu.VMEM((C, XY, N), f32),
-         pltpu.VMEM((C, XY, N), bf16), pltpu.VMEM((C, XY, N), bf16)],
-        [pltpu.SemaphoreType.DMA((2,))],
-        skip_weight, mlp_in, mlp_out, skip_bias.reshape(1, C), field, cotangent, hbm_in=(4, 5),
-    )
-
-
-def run_middle(recv, field, cotangent, pre, dact, kron, low, hi, lo, offset, synth):
+        [shape(3, 256, 256, dtype=bf16), pltpu.HBM((C, XY, N), KEPT), pltpu.HBM((C, XY, N), KEPT)],
+        [CELLS_LOW, CELLS_LOW, CELLS_KEPT, CELLS_KEPT, pltpu.SemaphoreType.DMA((2,))],
+        skip_weight, mlp_in, mlp_out, skip_bias.reshape(1, C), field, cotangent, hbm_in=(4, 5), hbm_out=(1, 2),
+    )
+
+
+def run_middle(recv, field, cotangent, pre, dact, kron, table, offset):
     turn = pltpu.VMEM((2 * PX, PY * C, LANES), f32)
-    cells = pltpu.VMEM((C, XY, N), f32)
     square = pltpu.VMEM((256, 256), f32)
     return call(
         k_middle, "middle",
-        [pltpu.VMEM((PEERS * ROWS, LANES), f32), pltpu.HBM((C, XY, N), bf16)],
-        [pltpu.VMEM((C, XY, N), bf16), pltpu.SemaphoreType.DMA((1,)),
-         turn, cells, square, square, square, square],
-        recv, field, cotangent, pre, dact, kron, low, hi, lo, offset, synth,
-        hbm_out=(1,), vmem_in=(1, 2, 3, 4, 5),
+        [shape(PEERS * ROWS, LANES), pltpu.HBM((C, XY, N), bf16)],
+        [CELLS_KEPT, CELLS_KEPT, pltpu.VMEM((2, 256, 256), bf16), CELLS_LOW,
+         pltpu.SemaphoreType.DMA((6,)), turn, CELLS, square, square, square, square],
+        recv, field, cotangent, pre, dact, kron, table, offset, hbm_in=(3, 4, 5), hbm_out=(1,),
     )
 
 
 def shards(field, cotangent, spec_weight, skip_weight, skip_bias, mlp_in, mlp_out):
-    low, hi, lo, offset, synth = [jnp.asarray(t) for t in tables()]
+    table, offset = [jnp.asarray(t) for t in tables()]
     field = field.reshape(C, XY, N)
     cotangent = cotangent.reshape(C, XY, N)
     weight = spec_weight.reshape(2, C, C, ML * C)
@@ -435,10 +484,7 @@
     wb = jnp.concatenate([-weight[1], weight[1]], axis=2)
     turn = pltpu.VMEM((PX, PY * C, LANES), f32)
     twice = pltpu.VMEM((2 * PX, PY * C, LANES), f32)
-    cells = pltpu.VMEM((C, XY, N), f32)
-    cells_low = pltpu.VMEM((C, XY, N), bf16)
-    own = pltpu.VMEM((8, LANES), f32)
-    plane = pltpu.VMEM((XY, PX * LANES), bf16)
+    whole = pltpu.VMEM((4 * XY + 2 * C, PX * LANES), bf16)
 
     def exchange(block):
         return lax.all_to_all(block, ("px", "py"), 0, 0, tiled=True)
@@ -447,31 +493,35 @@
         return exchange(block.reshape(PEERS, 1, ROWS * LANES)).reshape(PEERS * ROWS, LANES)
 
     sent = call(
-        k_forward, "forward", pltpu.VMEM((PEERS, C, LANES), f32),
-        [cells_low, pltpu.VMEM((2 * C, N), bf16), plane, plane, own, turn, pltpu.SemaphoreType.DMA((8,))],
-        field, low, hi, lo, offset, hbm_in=range(5),
-    )
-    kron, pre, dact, field, cotangent = run_prepare(
+        k_forward, "forward", shape(PEERS, C, LANES),
+        [CELLS_LOW, whole, OWN, turn, pltpu.SemaphoreType.DMA((7,))],
+        field, table, offset, hbm_in=range(3),
+    )
+    kron, pre, dact = run_prepare(
         skip_weight, mlp_in, mlp_out, skip_bias, field, cotangent
     )
     u, sent = call(
-        k_mix, "mix", [shape(C, LANES), pltpu.VMEM((PEERS, C, LANES), f32)], [],
-        exchange(sent), wa, wb, vmem_in=(1, 2),
+        k_mix, "mix", [shape(C, LANES), pltpu.HBM((PEERS, C, LANES), f32)],
+        [pltpu.VMEM((8, C, LANES), f32), pltpu.SemaphoreType.DMA((PEERS // 8,))],
+        exchange(sent), wa, wb, vmem_in=(1, 2), hbm_out=(1,),
     )
     sent, dpre = run_middle(
-        exchange(sent), field, cotangent, pre, dact, kron, low, hi, lo, offset, synth
+        exchange(sent), field, cotangent, pre, dact, kron, table, offset
     )
     sent, g = call(
-        k_mix_back, "mix_back", [pltpu.VMEM((PEERS * ROWS, LANES), f32), shape(C, LANES)], [],
+        k_mix_back, "mix_back", [shape(PEERS * ROWS, LANES), shape(C, LANES)], [],
         exchange_rows(sent), wa, wb, vmem_in=(1, 2),
     )
     back = exchange_rows(sent)
-    share = call(k_share, "share", shape(NB, 2 * C + 8, LANES), [], back, u, g)
+    share = call(
+        k_share, "share", pltpu.HBM((NB, 2 * C + 8, LANES), f32),
+        [pltpu.VMEM((2 * C + 8, LANES), f32), pltpu.SemaphoreType.DMA((NB,))], back, u, g, hbm_out=(0,),
+    )
     share = lax.all_to_all(share, "batch", 0, 0, tiled=True)
     grad_input = call(
         k_input, "input_grad", shape(C, XY, N, dtype=bf16),
-        [cells_low, twice, cells, pltpu.SemaphoreType.DMA((XY // 32,))],
-        back, dpre, kron, hi, lo, offset, synth, hbm_out=(0,),
+        [CELLS_LOW, twice, CELLS, pltpu.SemaphoreType.DMA((STEPS,))],
+        back, dpre, kron, table, offset, hbm_out=(0,),
     )
     spec, skip, b, inner, outer = call(
         k_shared, "shared",

time: 142 us -> 141 us (level)
  local copies, waits for them, and re-layouts: 10.5 us -> 3.2 us
  Pallas kernels: 18.6 us -> 24.1 us
    unnamed x52 -> x32, local copies, waits for them, and re-layouts: 9.88 us -> 2.62 us
    pallas_call x8, Pallas kernels: 18.6 us -> 24.1 us  [call(): pl.pallas_call(body, out_shape=outs, in_specs=[hbm if i in hbm_in else vm...]
  transfers between devices with their start and end apart: 3 -> 3, of which waited for: 3 -> 3; matrix products, arithmetic and copies ran while one was open for 1% -> 1% of each run, Pallas kernels for 4% -> 5%
where the time goes in v5:
time: 141 us; the launch traced here: 140 us
  blocking collectives  47.7 us (34%)
  waiting for transfers between devices  34.3 us (24%)
  starting transfers between devices  28.5 us (20%)
  Pallas kernels  24.1 us (17%)
  local copies, waits for them, and re-layouts  3.2 us (2%)
    all_to_all x2, blocking collectives, exchange(): return lax.all_to_all(block, ('px', 'py'), 0, 0, tiled=True)  47.7 us
    all_to_all x2, waiting for transfers between devices, exchange(): return lax.all_to_all(block, ('px', 'py'), 0, 0, tiled=True)  27 us
    pallas_call x8, Pallas kernels, call(): pl.pallas_call(body, out_shape=outs, in_specs=[hbm if i in hbm_in else vm...  24.1 us
    all_to_all x2, starting transfers between devices, exchange(): return lax.all_to_all(block, ('px', 'py'), 0, 0, tiled=True)  21.9 us
    all_to_all x1, waiting for transfers between devices, shards(): share = lax.all_to_all(share, 'batch', 0, 0, tiled=True)  7.3 us
    all_to_all x1, starting transfers between devices, shards(): share = lax.all_to_all(share, 'batch', 0, 0, tiled=True)  6.61 us
  transfers between devices with their start and end apart: 3, of which 3 were waited for; matrix products, arithmetic and copies ran while one was open for 1% of the time, Pallas kernels for 5%

profile of v5, /device:TPU:1, one launch (start us, length us, event | category | flops | bytes accessed | tf_op | source)
XLA Modules:
  0.0 139.5 jit_solution(7457737219452125135)
XLA Ops:
  0.6 3.6 %forward.1 = f32[64,16,128]{2,1,0:T(8,128)} custom-call(bf16[16,256,128]{2,1,0:T(8,128)(2,1)} %bitcast.13, bf16[1056,512]{1,0:T(8,128)(2,1)} %constant.4.clone.table_hbm.table_ref, f32[64,8,128]{2,1,0:T(8,128)} %constant.5.clone.offset_hbm.offset_ref), custom_call_target="tpu_custom_call" | custom-call | tf_op jit(solution)/shard_map/forward/pallas_call | solution.py:436
  4.3 15.6 %all-to-all-start = ((f32[64,16,128]{2,1,0:T(8,128)}), f32[64,16,128]{2,1,0:T(8,128)}, u32[]{:S(2)}, u32[]{:S(2)}) async-start(f32[64,16,128]{2,1,0:T(8,128)} %forward.1), calls=%async_computation | async-start | bytes 1048576 | tf_op jit(solution)/shard_map/all_to_all | solution.py:490
  19.9 0.1 fusion
  20.0 0.0 copy-start.13
  20.1 0.3 squeeze.9
  20.3 0.3 squeeze.8
  20.6 0.8 pad_maximum_fusion
  21.4 15.6 %all-to-all-done.recv_ref = f32[64,16,128]{2,1,0:T(8,128)} async-done(((f32[64,16,128]{2,1,0:T(8,128)}), f32[64,16,128]{2,1,0:T(8,128)}, u32[]{:S(2)}, u32[]{:S(2)}) %all-to-all-start) | async-done | bytes 524320 | tf_op jit(solution)/shard_map/all_to_all | solution.py:490
  37.0 0.9 copy-done.6
  37.9 0.9 copy-done.8
  38.8 2.1 %mix.1 = (f32[16,128]{1,0:T(8,128)S(1)}, f32[64,16,128]{2,1,0:T(8,128)}) custom-call(f32[64,16,128]{2,1,0:T(8,128)} %all-to-all-done.recv_ref, f32[16,16,128]{2,1,0:T(8,128)S(1)} %copy-done.6, f32[16,16,128]{2,1,0:T(8,128)S(1)} %copy-done.8), custom_call_target="tpu_custom_call" | custom-call | tf_op jit(solution)/shard_map/mix/pallas_call | solution.py:436
  40.9 6.3 %all-to-all-start.1 = ((f32[64,16,128]{2,1,0:T(8,128)}), f32[64,16,128]{2,1,0:T(8,128)}, u32[]{:S(2)}, u32[]{:S(2)}) async-start(f32[64,16,128]{2,1,0:T(8,128)} %get-tuple-element.20), calls=%async_computation.1 | async-start | bytes 1048576 | tf_op jit(solution)/shard_map/all_to_all | solution.py:490
  47.2 4.8 %prepare.1 = (bf16[3,256,256]{2,1,0:T(8,128)(2,1)S(1)}, f32[16,256,128]{2,1,0:T(8,128)}, f32[16,256,128]{2,1,0:T(8,128)}) custom-call(bf16[16,16]{1,0:T(8,128)(2,1)S(1)} %copy-done.11, bf16[16,16]{1,0:T(8,128)(2,1)S(1)} %copy-done.12, bf16[16,16]{1,0:T(8,128)(2,1)S(1)} %copy-done.13, f32[1,16]{1,0:T(1,128)S(1)} %bitcast.23, bf16[16,256,128]{2,1,0:T(8,128)(2,1)} %bitcast.14, ...), custom_call_target="tpu_custom_call" | custom-call | tf_op jit(solution)/shard_map/prepare/pallas_call | solution.py:436
  52.0 0.7 copy-done.4
  52.8 11.5 %all-to-all-done.1.recv_ref = f32[64,16,128]{2,1,0:T(8,128)} async-done(((f32[64,16,128]{2,1,0:T(8,128)}), f32[64,16,128]{2,1,0:T(8,128)}, u32[]{:S(2)}, u32[]{:S(2)}) %all-to-all-start.1) | async-done | bytes 524320 | tf_op jit(solution)/shard_map/all_to_all | solution.py:490
  64.3 7.9 %middle.1 = (f32[1088,128]{1,0:T(8,128)S(1)}, bf16[16,256,128]{2,1,0:T(8,128)(2,1)}) custom-call(f32[64,16,128]{2,1,0:T(8,128)} %all-to-all-done.1.recv_ref, bf16[16,256,128]{2,1,0:T(8,128)(2,1)S(1)} %bitcast.15, bf16[16,256,128]{2,1,0:T(8,128)(2,1)S(1)} %bitcast.19, f32[16,256,128]{2,1,0:T(8,128)} %get-tuple-element.21.pre_hbm, ...), custom_call_target="tpu_custom_call" | custom-call | tf_op jit(solution)/shard_map/middle/pallas_call | solution.py:436
  72.3 23.9 %all_to_all.25 = f32[64,1,2176]{2,1,0:T(1,128)S(1)} all-to-all(f32[64,1,2176]{2,1,0:T(1,128)S(1)} %bitcast.21), channel_id=1, replica_groups=mesh['batch'=8,'px'=4,'py'=16] {'px','py'}, dimensions={0} | all-to-all | bytes 1114112 | tf_op jit(solution)/shard_map/all_to_all | solution.py:490
  96.2 0.2 mix_back.1
  96.4 23.7 %all_to_all.26 = f32[64,1,2176]{2,1,0:T(1,128)S(1)} all-to-all(f32[64,1,2176]{2,1,0:T(1,128)S(1)} %bitcast.22), channel_id=1, replica_groups=mesh['batch'=8,'px'=4,'py'=16] {'px','py'}, dimensions={0} | all-to-all | bytes 1114112 | tf_op jit(solution)/shard_map/all_to_all | solution.py:490
  120.1 0.7 share.1
  120.9 6.6 %all-to-all-start.4 = ((f32[8,40,128]{2,1,0:T(8,128)}), f32[8,40,128]{2,1,0:T(8,128)}, u32[]{:S(2)}, u32[]{:S(2)}) async-start(f32[8,40,128]{2,1,0:T(8,128)} %share.1), calls=%async_computation.4 | async-start | bytes 327680 | tf_op jit(solution)/shard_map/all_to_all | solution.py:520
  127.5 2.5 %input_grad.1 = bf16[16,256,128]{2,1,0:T(8,128)(2,1)} custom-call(f32[1088,128]{1,0:T(8,128)S(1)} %bitcast.17, bf16[16,256,128]{2,1,0:T(8,128)(2,1)S(1)} %copy-done.10, bf16[3,256,256]{2,1,0:T(8,128)(2,1)S(1)} %copy-done.5, bf16[1056,512]{1,0:T(8,128)(2,1)S(1)} %copy-done, f32[64,8,128]{2,1,0:T(8,128)S(1)} %copy-done.3), custom_call_target="tpu_custom_call" | custom-call | tf_op jit(solution)/shard_map/input_grad/pallas_call | solution.py:436
  130.0 7.3 %all-to-all-done.4.recv_ref = f32[8,40,128]{2,1,0:T(8,128)} async-done(((f32[8,40,128]{2,1,0:T(8,128)}), f32[8,40,128]{2,1,0:T(8,128)}, u32[]{:S(2)}, u32[]{:S(2)}) %all-to-all-start.4) | async-done | bytes 163872 | tf_op jit(solution)/shard_map/all_to_all | solution.py:520
  137.3 2.3 %shared.1 = (f32[2,16,4,2,16]{4,3,2,1,0:T(2,128)}, f32[16,16]{1,0:T(8,128)}, f32[16]{0:T(128)}, f32[16,16]{1,0:T(8,128)}, f32[16,16]{1,0:T(8,128)}) custom-call(f32[8,40,128]{2,1,0:T(8,128)} %all-to-all-done.4.recv_ref), custom_call_target="tpu_custom_call" | custom-call | tf_op jit(solution)/shard_map/shared/pallas_call | solution.py:436
  (29 shorter events, 0.1 us)
Async XLA Ops:
  0.6 19.3 %copy-start.15 = (f32[2,16,16,1,4,16]{5,4,3,2,1,0:T(4,128)S(1)}, f32[2,16,16,1,4,16]{5,4,3,2,1,0:T(4,128)}, u32[]{:S(2)}) copy-start(f32[2,16,16,1,4,16]{5,4,3,2,1,0:T(4,128)} %param.11) | copy-start | bytes 393220
  4.3 32.7 %all-to-all-start = ((f32[64,16,128]{2,1,0:T(8,128)}), f32[64,16,128]{2,1,0:T(8,128)}, u32[]{:S(2)}, u32[]{:S(2)}) async-start(f32[64,16,128]{2,1,0:T(8,128)} %forward.1), calls=%async_computation | async-start | bytes 1048576 | tf_op jit(solution)/shard_map/all_to_all | solution.py:490
  20.0 27.2 %copy-start.11 = (bf16[16,16]{1,0:T(8,128)(2,1)S(1)}, bf16[16,16]{1,0:T(8,128)(2,1)}, u32[]{:S(2)}) copy-start(bf16[16,16]{1,0:T(8,128)(2,1)} %skip_ref.1) | copy-start | bytes 1540
  20.0 27.2 %copy-start.12 = (bf16[16,16]{1,0:T(8,128)(2,1)S(1)}, bf16[16,16]{1,0:T(8,128)(2,1)}, u32[]{:S(2)}) copy-start(bf16[16,16]{1,0:T(8,128)(2,1)} %in_ref.1) | copy-start | bytes 1540
  20.0 27.1 %copy-start.13 = (bf16[16,16]{1,0:T(8,128)(2,1)S(1)}, bf16[16,16]{1,0:T(8,128)(2,1)}, u32[]{:S(2)}) copy-start(bf16[16,16]{1,0:T(8,128)(2,1)} %outer_ref.1) | copy-start | bytes 1540
  20.0 27.1 %copy-start.14 = (f32[16]{0:T(128)S(1)}, f32[16]{0:T(128)}, u32[]{:S(2)}) copy-start(f32[16]{0:T(128)} %param.13) | copy-start | bytes 196
  21.4 42.8 %copy-start = (bf16[1056,512]{1,0:T(8,128)(2,1)S(1)}, bf16[1056,512]{1,0:T(8,128)(2,1)}, u32[]{:S(2)}) copy-start(bf16[1056,512]{1,0:T(8,128)(2,1)} %constant.4.clone.table_hbm.table_ref) | copy-start | bytes 3244036
  21.4 42.8 %copy-start.1 = (bf16[1,16,32,8,128]{4,3,2,1,0:T(8,128)(2,1)S(1)}, bf16[1,16,32,8,128]{4,3,2,1,0:T(8,128)(2,1)}, u32[]{:S(2)}) copy-start(bf16[1,16,32,8,128]{4,3,2,1,0:T(8,128)(2,1)} %param.9) | copy-start | bytes 3145732
  21.4 42.8 %copy-start.2 = (bf16[1,16,32,8,128]{4,3,2,1,0:T(8,128)(2,1)S(1)}, bf16[1,16,32,8,128]{4,3,2,1,0:T(8,128)(2,1)}, u32[]{:S(2)}) copy-start(bf16[1,16,32,8,128]{4,3,2,1,0:T(8,128)(2,1)} %param.10) | copy-start | bytes 3145732
  21.4 42.8 %copy-start.3 = (f32[64,8,128]{2,1,0:T(8,128)S(1)}, f32[64,8,128]{2,1,0:T(8,128)}, u32[]{:S(2)}) copy-start(f32[64,8,128]{2,1,0:T(8,128)} %constant.5.clone.offset_hbm.offset_ref) | copy-start | bytes 786436
  37.0 0.9 copy-start.6
  37.9 0.9 copy-start.8
  40.9 23.4 %all-to-all-start.1 = ((f32[64,16,128]{2,1,0:T(8,128)}), f32[64,16,128]{2,1,0:T(8,128)}, u32[]{:S(2)}, u32[]{:S(2)}) async-start(f32[64,16,128]{2,1,0:T(8,128)} %get-tuple-element.20), calls=%async_computation.1 | async-start | bytes 1048576 | tf_op jit(solution)/shard_map/all_to_all | solution.py:490
  52.0 0.8 copy-start.4
  64.3 31.9 %copy-start.7 = (f32[16,16,128]{2,1,0:T(8,128)S(1)}, f32[16,16,128]{2,1,0:T(8,128)}, u32[]{:S(2)}) copy-start(f32[16,16,128]{2,1,0:T(8,128)} %get-tuple-element.48.wa_ref) | copy-start | bytes 393220
  64.3 31.9 %copy-start.9 = (f32[16,16,128]{2,1,0:T(8,128)S(1)}, f32[16,16,128]{2,1,0:T(8,128)}, u32[]{:S(2)}) copy-start(f32[16,16,128]{2,1,0:T(8,128)} %get-tuple-element.49.wb_ref) | copy-start | bytes 393220
  72.2 55.2 %copy-start.5 = (bf16[3,256,256]{2,1,0:T(8,128)(2,1)S(1)}, bf16[3,256,256]{2,1,0:T(8,128)(2,1)}, u32[]{:S(2)}) copy-start(bf16[3,256,256]{2,1,0:T(8,128)(2,1)} %copy-done.4) | copy-start | bytes 1179652
  72.2 55.2 %copy-start.10 = (bf16[16,256,128]{2,1,0:T(8,128)(2,1)S(1)}, bf16[16,256,128]{2,1,0:T(8,128)(2,1)}, u32[]{:S(2)}) copy-start(bf16[16,256,128]{2,1,0:T(8,128)(2,1)} %get-tuple-element.26.dpre_ref) | copy-start | bytes 3145732
  120.9 16.4 %all-to-all-start.4 = ((f32[8,40,128]{2,1,0:T(8,128)}), f32[8,40,128]{2,1,0:T(8,128)}, u32[]{:S(2)}, u32[]{:S(2)}) async-start(f32[8,40,128]{2,1,0:T(8,128)} %share.1), calls=%async_computation.4 | async-start | bytes 327680 | tf_op jit(solution)/shard_map/all_to_all | solution.py:520

commit v6 on v5

--- a/solution.py
+++ b/solution.py
@@ -275,15 +275,15 @@
 
 
 def k_middle(
-    recv_ref, field_ref, cot_ref, pre_hbm, dact_hbm, kron_hbm, table_ref, offset_ref,
+    recv_ref, field_hbm, cot_hbm, pre_hbm, dact_hbm, kron_hbm, table_ref, offset_ref,
     out_ref, dpre_hbm,
-    pre_ref, dact_ref, kron_ref, dpre_ref, sems, turn_ref, g_ref, skip_acc, bias_acc, in_acc, out_acc,
+    field_ref, cot_ref, pre_ref, dact_ref, kron_ref, dpre_ref, sems, turn_ref, g_ref, skip_acc, bias_acc, in_acc, out_acc,
 ):
     pairs = [(kron_hbm.at[0:2], kron_ref)]
     for i in range(2):
         part = pl.ds(i * HALF, HALF)
-        pairs.append((pre_hbm.at[:, part], pre_ref.at[:, part]))
-        pairs.append((dact_hbm.at[:, part], dact_ref.at[:, part]))
+        for a, b in ((pre_hbm, pre_ref), (dact_hbm, dact_ref), (field_hbm, field_ref), (cot_hbm, cot_ref)):
+            pairs.append((a.at[:, part], b.at[:, part]))
     copies = [pltpu.make_async_copy(a, b, sems.at[i]) for i, (a, b) in enumerate(pairs)]
     for copy in copies:
         copy.start()
@@ -315,10 +315,11 @@
     copies[0].wait()
     for p in range(STEPS):
         if p % (STEPS // 2) == 0:
-            copies[1 + 2 * (p // (STEPS // 2))].wait()
-            copies[2 + 2 * (p // (STEPS // 2))].wait()
+            first = 1 + 4 * (p // (STEPS // 2))
+            for copy in copies[first : first + 4]:
+                copy.wait()
         step(p)
-    copy = pltpu.make_async_copy(dpre_ref, dpre_hbm, sems.at[5])
+    copy = pltpu.make_async_copy(dpre_ref, dpre_hbm, sems.at[9])
     copy.start()
     bias = bias_acc[...].reshape(C, 16, 256).sum(axis=1)
     total = jnp.sum(bias, axis=1, keepdims=True)
@@ -469,9 +470,9 @@
     return call(
         k_middle, "middle",
         [shape(PEERS * ROWS, LANES), pltpu.HBM((C, XY, N), bf16)],
-        [CELLS_KEPT, CELLS_KEPT, pltpu.VMEM((2, 256, 256), bf16), CELLS_LOW,
-         pltpu.SemaphoreType.DMA((6,)), turn, CELLS, square, square, square, square],
-        recv, field, cotangent, pre, dact, kron, table, offset, hbm_in=(3, 4, 5), hbm_out=(1,),
+        [CELLS_LOW, CELLS_LOW, CELLS_KEPT, CELLS_KEPT, pltpu.VMEM((2, 256, 256), bf16), CELLS_LOW,
+         pltpu.SemaphoreType.DMA((10,)), turn, CELLS, square, square, square, square],
+        recv, field, cotangent, pre, dact, kron, table, offset, hbm_in=(1, 2, 3, 4, 5), hbm_out=(1,),
     )
 
 

time: 141 us -> 137 us (0.972)
  Pallas kernels: 24.1 us -> 21.4 us
  local copies, waits for them, and re-layouts: 3.2 us -> 1.41 us
    pallas_call x8, Pallas kernels: 24.1 us -> 21.4 us  [call(): pl.pallas_call(body, out_shape=outs, in_specs=[hbm if i in hbm_in else vm...]
    unnamed x32 -> x20, local copies, waits for them, and re-layouts: 2.62 us -> 0.8 us
where the time goes in v6:
time: 137 us; the launch traced here: 135 us
  blocking collectives  47.8 us (35%)
  waiting for transfers between devices  35 us (26%)
  starting transfers between devices  28.1 us (21%)
  Pallas kernels  21.4 us (16%)
  local copies, waits for them, and re-layouts  1.41 us (1%)
    all_to_all x2, blocking collectives, exchange(): return lax.all_to_all(block, ('px', 'py'), 0, 0, tiled=True)  47.8 us
    all_to_all x2, waiting for transfers between devices, exchange(): return lax.all_to_all(block, ('px', 'py'), 0, 0, tiled=True)  27.8 us
    all_to_all x2, starting transfers between devices, exchange(): return lax.all_to_all(block, ('px', 'py'), 0, 0, tiled=True)  21.5 us
    pallas_call x8, Pallas kernels, call(): pl.pallas_call(body, out_shape=outs, in_specs=[hbm if i in hbm_in else vm...  21.4 us
    all_to_all x1, waiting for transfers between devices, shards(): share = lax.all_to_all(share, 'batch', 0, 0, tiled=True)  7.21 us
    all_to_all x1, starting transfers between devices, shards(): share = lax.all_to_all(share, 'batch', 0, 0, tiled=True)  6.61 us
  transfers between devices with their start and end apart: 3, of which 3 were waited for; matrix products, arithmetic and copies ran while one was open for 1% of the time, Pallas kernels for 5%

profile of v6, /device:TPU:1, one launch (start us, length us, event | category | flops | bytes accessed | tf_op | source)
XLA Modules:
  0.0 134.8 jit_solution(15242750871104338577)
XLA Ops:
  0.6 3.6 %forward.1 = f32[64,16,128]{2,1,0:T(8,128)} custom-call(bf16[16,256,128]{2,1,0:T(8,128)(2,1)} %bitcast.19, bf16[1056,512]{1,0:T(8,128)(2,1)} %constant.4.clone.table_hbm.table_ref, f32[64,8,128]{2,1,0:T(8,128)} %constant.5.clone.offset_hbm.offset_ref), custom_call_target="tpu_custom_call" | custom-call | tf_op jit(solution)/shard_map/forward/pallas_call | solution.py:437
  4.3 15.4 %all-to-all-start = ((f32[64,16,128]{2,1,0:T(8,128)}), f32[64,16,128]{2,1,0:T(8,128)S(1)}, u32[]{:S(2)}, u32[]{:S(2)}) async-start(f32[64,16,128]{2,1,0:T(8,128)} %forward.1), calls=%async_computation | async-start | bytes 1048576 | tf_op jit(solution)/shard_map/all_to_all | solution.py:491
  19.7 0.1 fusion
  19.9 0.0 copy-start.7
  19.9 0.3 squeeze.9
  20.2 0.3 squeeze.8
  20.4 0.1 pad_maximum_fusion
  20.6 0.0 copy-start
  20.6 0.0 copy-start.1
  20.6 16.3 %all-to-all-done.recv_ref = f32[64,16,128]{2,1,0:T(8,128)S(1)} async-done(((f32[64,16,128]{2,1,0:T(8,128)}), f32[64,16,128]{2,1,0:T(8,128)S(1)}, u32[]{:S(2)}, u32[]{:S(2)}) %all-to-all-start) | async-done | bytes 524320 | tf_op jit(solution)/shard_map/all_to_all | solution.py:491
  36.9 1.0 mix.1
  37.9 6.1 %all-to-all-start.1 = ((f32[64,16,128]{2,1,0:T(8,128)}), f32[64,16,128]{2,1,0:T(8,128)S(1)}, u32[]{:S(2)}, u32[]{:S(2)}) async-start(f32[64,16,128]{2,1,0:T(8,128)} %get-tuple-element.20), calls=%async_computation.1 | async-start | bytes 1048576 | tf_op jit(solution)/shard_map/all_to_all | solution.py:491
  44.0 4.8 %prepare.1 = (bf16[3,256,256]{2,1,0:T(8,128)(2,1)S(1)}, f32[16,256,128]{2,1,0:T(8,128)}, f32[16,256,128]{2,1,0:T(8,128)}) custom-call(bf16[16,16]{1,0:T(8,128)(2,1)S(1)} %copy-done.5, bf16[16,16]{1,0:T(8,128)(2,1)S(1)} %copy-done.6, bf16[16,16]{1,0:T(8,128)(2,1)S(1)} %copy-done.7, f32[1,16]{1,0:T(1,128)S(1)} %bitcast.18, bf16[16,256,128]{2,1,0:T(8,128)(2,1)} %bitcast.20, ...), custom_call_target="tpu_custom_call" | custom-call | tf_op jit(solution)/shard_map/prepare/pallas_call | solution.py:437
  48.9 0.7 copy-done.2
  49.6 11.5 %all-to-all-done.1.recv_ref = f32[64,16,128]{2,1,0:T(8,128)S(1)} async-done(((f32[64,16,128]{2,1,0:T(8,128)}), f32[64,16,128]{2,1,0:T(8,128)S(1)}, u32[]{:S(2)}, u32[]{:S(2)}) %all-to-all-start.1) | async-done | bytes 524320 | tf_op jit(solution)/shard_map/all_to_all | solution.py:491
  61.2 7.2 %middle.1 = (f32[1088,128]{1,0:T(8,128)S(1)}, bf16[16,256,128]{2,1,0:T(8,128)(2,1)}) custom-call(f32[64,16,128]{2,1,0:T(8,128)S(1)} %all-to-all-done.1.recv_ref, bf16[16,256,128]{2,1,0:T(8,128)(2,1)} %bitcast.21, bf16[16,256,128]{2,1,0:T(8,128)(2,1)} %bitcast.23, f32[16,256,128]{2,1,0:T(8,128)} %get-tuple-element.21.pre_hbm, ...), custom_call_target="tpu_custom_call" | custom-call | tf_op jit(solution)/shard_map/middle/pallas_call | solution.py:437
  68.4 24.0 %all_to_all.25 = f32[64,1,2176]{2,1,0:T(1,128)S(1)} all-to-all(f32[64,1,2176]{2,1,0:T(1,128)S(1)} %bitcast.16), channel_id=1, replica_groups=mesh['batch'=8,'px'=4,'py'=16] {'px','py'}, dimensions={0} | all-to-all | bytes 1114112 | tf_op jit(solution)/shard_map/all_to_all | solution.py:491
  92.3 0.2 mix_back.1
  92.5 23.9 %all_to_all.26 = f32[64,1,2176]{2,1,0:T(1,128)S(1)} all-to-all(f32[64,1,2176]{2,1,0:T(1,128)S(1)} %bitcast.17), channel_id=1, replica_groups=mesh['batch'=8,'px'=4,'py'=16] {'px','py'}, dimensions={0} | all-to-all | bytes 1114112 | tf_op jit(solution)/shard_map/all_to_all | solution.py:491
  116.4 0.7 share.1
  117.1 6.6 %all-to-all-start.4 = ((f32[8,40,128]{2,1,0:T(8,128)}), f32[8,40,128]{2,1,0:T(8,128)S(1)}, u32[]{:S(2)}, u32[]{:S(2)}) async-start(f32[8,40,128]{2,1,0:T(8,128)} %share.1), calls=%async_computation.4 | async-start | bytes 327680 | tf_op jit(solution)/shard_map/all_to_all | solution.py:521
  123.7 2.5 %input_grad.1 = bf16[16,256,128]{2,1,0:T(8,128)(2,1)} custom-call(f32[1088,128]{1,0:T(8,128)S(1)} %bitcast.14, bf16[16,256,128]{2,1,0:T(8,128)(2,1)S(1)} %copy-done.4, bf16[3,256,256]{2,1,0:T(8,128)(2,1)S(1)} %copy-done.3, bf16[1056,512]{1,0:T(8,128)(2,1)S(1)} %copy-done, f32[64,8,128]{2,1,0:T(8,128)S(1)} %copy-done.1), custom_call_target="tpu_custom_call" | custom-call | tf_op jit(solution)/shard_map/input_grad/pallas_call | solution.py:437
  126.2 7.2 %all-to-all-done.4.recv_ref = f32[8,40,128]{2,1,0:T(8,128)S(1)} async-done(((f32[8,40,128]{2,1,0:T(8,128)}), f32[8,40,128]{2,1,0:T(8,128)S(1)}, u32[]{:S(2)}, u32[]{:S(2)}) %all-to-all-start.4) | async-done | bytes 163872 | tf_op jit(solution)/shard_map/all_to_all | solution.py:521
  133.4 1.4 %shared.1 = (f32[2,16,4,2,16]{4,3,2,1,0:T(2,128)}, f32[16,16]{1,0:T(8,128)}, f32[16]{0:T(128)}, f32[16,16]{1,0:T(8,128)}, f32[16,16]{1,0:T(8,128)}) custom-call(f32[8,40,128]{2,1,0:T(8,128)S(1)} %all-to-all-done.4.recv_ref), custom_call_target="tpu_custom_call" | custom-call | tf_op jit(solution)/shard_map/shared/pallas_call | solution.py:437
  (17 shorter events, 0.1 us)
Async XLA Ops:
  0.6 19.1 %copy-start.9 = (f32[2,16,16,1,4,16]{5,4,3,2,1,0:T(4,128)S(1)}, f32[2,16,16,1,4,16]{5,4,3,2,1,0:T(4,128)}, u32[]{:S(2)}) copy-start(f32[2,16,16,1,4,16]{5,4,3,2,1,0:T(4,128)} %param.11) | copy-start | bytes 393220
  4.3 32.6 %all-to-all-start = ((f32[64,16,128]{2,1,0:T(8,128)}), f32[64,16,128]{2,1,0:T(8,128)S(1)}, u32[]{:S(2)}, u32[]{:S(2)}) async-start(f32[64,16,128]{2,1,0:T(8,128)} %forward.1), calls=%async_computation | async-start | bytes 1048576 | tf_op jit(solution)/shard_map/all_to_all | solution.py:491
  19.8 24.2 %copy-start.5 = (bf16[16,16]{1,0:T(8,128)(2,1)S(1)}, bf16[16,16]{1,0:T(8,128)(2,1)}, u32[]{:S(2)}) copy-start(bf16[16,16]{1,0:T(8,128)(2,1)} %skip_ref.1) | copy-start | bytes 1540
  19.9 24.2 %copy-start.6 = (bf16[16,16]{1,0:T(8,128)(2,1)S(1)}, bf16[16,16]{1,0:T(8,128)(2,1)}, u32[]{:S(2)}) copy-start(bf16[16,16]{1,0:T(8,128)(2,1)} %in_ref.1) | copy-start | bytes 1540
  19.9 24.2 %copy-start.7 = (bf16[16,16]{1,0:T(8,128)(2,1)S(1)}, bf16[16,16]{1,0:T(8,128)(2,1)}, u32[]{:S(2)}) copy-start(bf16[16,16]{1,0:T(8,128)(2,1)} %outer_ref.1) | copy-start | bytes 1540
  19.9 24.2 %copy-start.8 = (f32[16]{0:T(128)S(1)}, f32[16]{0:T(128)}, u32[]{:S(2)}) copy-start(f32[16]{0:T(128)} %param.13) | copy-start | bytes 196
  20.6 40.6 %copy-start = (bf16[1056,512]{1,0:T(8,128)(2,1)S(1)}, bf16[1056,512]{1,0:T(8,128)(2,1)}, u32[]{:S(2)}) copy-start(bf16[1056,512]{1,0:T(8,128)(2,1)} %constant.4.clone.table_hbm.table_ref) | copy-start | bytes 3244036
  20.6 40.6 %copy-start.1 = (f32[64,8,128]{2,1,0:T(8,128)S(1)}, f32[64,8,128]{2,1,0:T(8,128)}, u32[]{:S(2)}) copy-start(f32[64,8,128]{2,1,0:T(8,128)} %constant.5.clone.offset_hbm.offset_ref) | copy-start | bytes 786436
  37.9 23.3 %all-to-all-start.1 = ((f32[64,16,128]{2,1,0:T(8,128)}), f32[64,16,128]{2,1,0:T(8,128)S(1)}, u32[]{:S(2)}, u32[]{:S(2)}) async-start(f32[64,16,128]{2,1,0:T(8,128)} %get-tuple-element.20), calls=%async_computation.1 | async-start | bytes 1048576 | tf_op jit(solution)/shard_map/all_to_all | solution.py:491
  48.9 0.8 copy-start.2
  68.3 55.4 %copy-start.3 = (bf16[3,256,256]{2,1,0:T(8,128)(2,1)S(1)}, bf16[3,256,256]{2,1,0:T(8,128)(2,1)}, u32[]{:S(2)}) copy-start(bf16[3,256,256]{2,1,0:T(8,128)(2,1)} %copy-done.2) | copy-start | bytes 1179652
  92.5 31.3 %copy-start.4 = (bf16[16,256,128]{2,1,0:T(8,128)(2,1)S(1)}, bf16[16,256,128]{2,1,0:T(8,128)(2,1)}, u32[]{:S(2)}) copy-start(bf16[16,256,128]{2,1,0:T(8,128)(2,1)} %get-tuple-element.26.dpre_ref) | copy-start | bytes 3145732
  117.1 16.3 %all-to-all-start.4 = ((f32[8,40,128]{2,1,0:T(8,128)}), f32[8,40,128]{2,1,0:T(8,128)S(1)}, u32[]{:S(2)}, u32[]{:S(2)}) async-start(f32[8,40,128]{2,1,0:T(8,128)} %share.1), calls=%async_computation.4 | async-start | bytes 327680 | tf_op jit(solution)/shard_map/all_to_all | solution.py:521

commit v7 on v6

--- a/solution.py
+++ b/solution.py
@@ -95,7 +95,7 @@
     return lax.axis_index("px") * PY + lax.axis_index("py")
 
 
-def forward_part(get, table, off_ref, turn_ref, put, ready=None):
+def forward_part(get, table, off_ref, turn_ref, put, ready=None, done=None):
     low = table.low[...]
     rows = [dot_nt(low, get(c)) for c in range(C)]
     both = jnp.concatenate([r[:C] for r in rows] + [r[C:] for r in rows], axis=0)
@@ -109,9 +109,10 @@
         pb = part[C * C :, mb * LANES : (mb + 1) * LANES]
         co, si = off_ref[mb : mb + 1, :], off_ref[PX + mb : PX + mb + 1, :]
         turn_ref[mb] = (pa * co + pb * si) + turned(pb * co - pa * si)
-    for mb in range(PX):
         for k in range(C):
             put(mb * PY + k, turn_ref[mb, pl.ds(k, C, stride=C), :])
+        if done is not None:
+            done(mb)
 
 
 def inverse_part(block, table, off_ref, turn_ref, g_ref):
@@ -143,7 +144,9 @@
                 g_ref[ob * 8 + half * 4 + o] = g[:, o * N : (o + 1) * N]
 
 
-def k_forward(field_hbm, table_hbm, offset_hbm, out_ref, field_ref, table_ref, off_ref, turn_ref, sems):
+def k_forward(
+    field_hbm, table_hbm, offset_hbm, out_hbm, out_ref, field_ref, table_ref, off_ref, turn_ref, sems
+):
     low_rows, plane_rows = pl.ds(4 * XY, 2 * C), pl.ds(0, 2 * XY)
     pairs = [(table_hbm.at[low_rows], table_ref.at[low_rows])]
     for i in range(4):
@@ -168,7 +171,16 @@
     def put(d, value):
         out_ref[d] = value
 
-    forward_part(get, Table(table_ref), off_ref, turn_ref, put, ready)
+    sent = []
+
+    def done(mb):
+        part = pl.ds(mb * PY, PY)
+        sent.append(pltpu.make_async_copy(out_ref.at[part], out_hbm.at[part], sems.at[7 + mb]))
+        sent[-1].start()
+
+    forward_part(get, Table(table_ref), off_ref, turn_ref, put, ready, done)
+    for copy in sent:
+        copy.wait()
 
 
 def spread_map(w, transpose):
@@ -261,23 +273,36 @@
     ref[:, pl.ds(p * 32 + 16, 16), :] = value[:, N:].reshape(C, 16, N)
 
 
-def pack_rows(acc):
+def thirds(x):
+    hi, rest = x.astype(bf16), x - x.astype(bf16).astype(f32)
+    mid = rest.astype(bf16)
+    return [hi, mid, (rest - mid.astype(f32)).astype(bf16)]
+
+
+def picked(x, pick):
+    n = x.shape[0]
+    out = dot(jnp.concatenate(thirds(x), axis=0), pick)
+    return out[:n] + out[n : 2 * n] + out[2 * n :]
+
+
+def pack_rows(accs):
     r = lax.broadcasted_iota(jnp.int32, (256, 256), 0)
     l = lax.broadcasted_iota(jnp.int32, (256, 256), 1)
-    kept = jnp.where(r % 16 == l % 16, acc, 0.0).reshape(C, 16, 256).sum(axis=1)
+    same = r % 16 == l % 16
+    kept = [jnp.where(same, a, 0.0).reshape(C, 16, 256).sum(axis=1) for a in accs]
     r = lax.broadcasted_iota(jnp.int32, (256, LANES), 0)
     l = lax.broadcasted_iota(jnp.int32, (256, LANES), 1)
-    pick = jnp.where(r // 16 == l % 16, 1.0, 0.0)
-    spread = jnp.dot(kept, pick, precision=lax.Precision.HIGHEST, preferred_element_type=f32)
-    r = lax.broadcasted_iota(jnp.int32, (C, LANES), 0)
-    l = lax.broadcasted_iota(jnp.int32, (C, LANES), 1)
+    pick = jnp.where(r // 16 == l % 16, 1.0, 0.0).astype(bf16)
+    spread = picked(jnp.concatenate(kept, axis=0), pick)
+    r = lax.broadcasted_iota(jnp.int32, (len(accs) * C, LANES), 0)
+    l = lax.broadcasted_iota(jnp.int32, (len(accs) * C, LANES), 1)
     return jnp.where(r % 8 == l // 16, spread, 0.0)
 
 
 def k_middle(
     recv_ref, field_hbm, cot_hbm, pre_hbm, dact_hbm, kron_hbm, table_ref, offset_ref,
     out_ref, dpre_hbm,
-    field_ref, cot_ref, pre_ref, dact_ref, kron_ref, dpre_ref, sems, turn_ref, g_ref, skip_acc, bias_acc, in_acc, out_acc,
+    field_ref, cot_ref, pre_ref, dact_ref, kron_ref, dpre_ref, sems, turn_ref, g_ref, skip_acc, in_acc, out_acc,
 ):
     pairs = [(kron_hbm.at[0:2], kron_ref)]
     for i in range(2):
@@ -293,7 +318,8 @@
     skip_acc[...] = jnp.zeros_like(skip_acc)
     in_acc[...] = jnp.zeros_like(in_acc)
     out_acc[...] = jnp.zeros_like(out_acc)
-    bias_acc[...] = jnp.zeros_like(bias_acc)
+
+    kept, sums = [], []
 
     def step(p):
         f = tile(field_ref, p)
@@ -307,10 +333,13 @@
         dpre = dot(kron_ref[1], d_inner) * d_hid
         dpre = dpre.astype(bf16)
         untile(dpre_ref, p, dpre)
-        skip_acc[...] += dot_nt(dpre, f)
-        in_acc[...] += dot_nt(d_inner, hid)
-        out_acc[...] += dot_nt(cot, act)
-        bias_acc[...] += dpre.astype(f32)
+        kept.append((dpre, f, d_inner, hid, cot, act))
+        if p % 2:
+            wide = lambda i: jnp.concatenate([k[i] for k in kept[-2:]], axis=1)
+            skip_acc[...] += dot_nt(wide(0), wide(1))
+            in_acc[...] += dot_nt(wide(2), wide(3))
+            out_acc[...] += dot_nt(wide(4), wide(5))
+        sums.append(dpre.astype(f32).reshape(C, 16, 256).sum(axis=1))
 
     copies[0].wait()
     for p in range(STEPS):
@@ -321,13 +350,13 @@
         step(p)
     copy = pltpu.make_async_copy(dpre_ref, dpre_hbm, sems.at[9])
     copy.start()
-    bias = bias_acc[...].reshape(C, 16, 256).sum(axis=1)
+    bias = sum(sums)
     total = jnp.sum(bias, axis=1, keepdims=True)
     r = lax.broadcasted_iota(jnp.int32, (C, LANES), 0)
     l = lax.broadcasted_iota(jnp.int32, (C, LANES), 1)
     bias_row = jnp.sum(jnp.where(r == l, total, 0.0), axis=0, keepdims=True)
     small = jnp.concatenate(
-        [pack_rows(skip_acc[...]), pack_rows(in_acc[...]), pack_rows(out_acc[...]),
+        [pack_rows([skip_acc[...], in_acc[...], out_acc[...]]),
          bias_row, jnp.zeros((C - 1, LANES), f32)], axis=0
     )
 
@@ -385,41 +414,33 @@
 
 
 def k_shared(recv_ref, spec_ref, skip_ref, bias_ref, in_ref, outer_ref, pa_ref, pb_ref):
+    gs = [recv_ref[s, C : 2 * C, :] for s in range(NB)]
+    turns = [pltpu.roll(g, LANES // 2, 1) for g in gs]
     for c in range(C):
-        pa = jnp.zeros((C, LANES), f32)
-        pb = jnp.zeros((C, LANES), f32)
-        for s in range(NB):
-            u = recv_ref[s, c : c + 1, :]
-            g = recv_ref[s, C : 2 * C, :]
-            pa = pa + u * g
-            pb = pb + u * pltpu.roll(g, LANES // 2, 1)
-        pa_ref[c * C : (c + 1) * C, :] = pa
-        pb_ref[c * C : (c + 1) * C, :] = pb
+        us = [recv_ref[s, c : c + 1, :] for s in range(NB)]
+        pa_ref[c * C : (c + 1) * C, :] = sum(u * g for u, g in zip(us, gs))
+        pb_ref[c * C : (c + 1) * C, :] = sum(u * g for u, g in zip(us, turns))
     b = lax.axis_index("batch")
     r = lax.broadcasted_iota(jnp.int32, (8, LANES), 0)
     l = lax.broadcasted_iota(jnp.int32, (8, LANES), 1)
     mine = ((l % 64) // C == r // 2) & (l % C == 2 * b + r % 2)
     sel_a = jnp.where(mine, 1.0, 0.0)
     sel_b = jnp.where(l < 64, sel_a, -sel_a)
-    full = lambda x, y: lax.dot_general(
-        x, y, NT, precision=lax.Precision.HIGHEST, preferred_element_type=f32
-    )
-    for i, part in enumerate((full(sel_a, pa_ref[...]), full(sel_b, pb_ref[...]))):
+    for i, (sel, ref) in enumerate(((sel_a, pa_ref), (sel_b, pb_ref))):
+        part = sum(dot_nt(sel.astype(bf16), third) for third in thirds(ref[...]))
         for c in range(C):
             for m in range(ML):
                 spec_ref[i, c, m] = part[2 * m : 2 * m + 2, c * C : (c + 1) * C]
     small = jnp.sum(recv_ref[:, 2 * C :, :], axis=0) * RHO
-    r = lax.broadcasted_iota(jnp.int32, (C, LANES), 0)
-    l = lax.broadcasted_iota(jnp.int32, (C, LANES), 1)
+    r = lax.broadcasted_iota(jnp.int32, (3 * C, LANES), 0)
+    l = lax.broadcasted_iota(jnp.int32, (3 * C, LANES), 1)
     pr = lax.broadcasted_iota(jnp.int32, (LANES, C), 0)
     pc = lax.broadcasted_iota(jnp.int32, (LANES, C), 1)
-    pick = jnp.where(pr % C == pc, 1.0, 0.0)
+    pick = jnp.where(pr % C == pc, 1.0, 0.0).astype(bf16)
+    rows = jnp.concatenate([jnp.broadcast_to(small[i : i + 1], (8, LANES)) for i in range(6)], axis=0)
+    maps = picked(jnp.where(l // C == r % 8, rows, 0.0), pick)
     for i, ref in enumerate((skip_ref, in_ref, outer_ref)):
-        two = jnp.concatenate(
-            [jnp.broadcast_to(small[2 * i + h : 2 * i + h + 1], (8, LANES)) for h in range(2)], axis=0
-        )
-        two = jnp.where(l // C == r % 8, two, 0.0)
-        ref[...] = jnp.dot(two, pick, precision=lax.Precision.HIGHEST, preferred_element_type=f32)
+        ref[...] = maps[i * C : (i + 1) * C]
     bias_ref[...] = small[6, :C]
 
 
@@ -471,7 +492,7 @@
         k_middle, "middle",
         [shape(PEERS * ROWS, LANES), pltpu.HBM((C, XY, N), bf16)],
         [CELLS_LOW, CELLS_LOW, CELLS_KEPT, CELLS_KEPT, pltpu.VMEM((2, 256, 256), bf16), CELLS_LOW,
-         pltpu.SemaphoreType.DMA((10,)), turn, CELLS, square, square, square, square],
+         pltpu.SemaphoreType.DMA((10,)), turn, CELLS, square, square, square],
         recv, field, cotangent, pre, dact, kron, table, offset, hbm_in=(1, 2, 3, 4, 5), hbm_out=(1,),
     )
 
@@ -494,9 +515,9 @@
         return exchange(block.reshape(PEERS, 1, ROWS * LANES)).reshape(PEERS * ROWS, LANES)
 
     sent = call(
-        k_forward, "forward", shape(PEERS, C, LANES),
-        [CELLS_LOW, whole, OWN, turn, pltpu.SemaphoreType.DMA((7,))],
-        field, table, offset, hbm_in=range(3),
+        k_forward, "forward", pltpu.HBM((PEERS, C, LANES), f32),
+        [pltpu.VMEM((PEERS, C, LANES), f32), CELLS_LOW, whole, OWN, turn, pltpu.SemaphoreType.DMA((7 + PX,))],
+        field, table, offset, hbm_in=range(3), hbm_out=(0,),
     )
     kron, pre, dact = run_prepare(
         skip_weight, mlp_in, mlp_out, skip_bias, field, cotangent

time: 137 us -> 136 us (level)
  no operation moved by 1% of the time
where the time goes in v7:
time: 136 us; the launch traced here: 134 us
  blocking collectives  47.8 us (35%)
  waiting for transfers between devices  35 us (26%)
  starting transfers between devices  28.1 us (21%)
  Pallas kernels  20.5 us (15%)
  local copies, waits for them, and re-layouts  1.41 us (1%)
    all_to_all x2, blocking collectives, exchange(): return lax.all_to_all(block, ('px', 'py'), 0, 0, tiled=True)  47.8 us
    all_to_all x2, waiting for transfers between devices, exchange(): return lax.all_to_all(block, ('px', 'py'), 0, 0, tiled=True)  27.8 us
    all_to_all x2, starting transfers between devices, exchange(): return lax.all_to_all(block, ('px', 'py'), 0, 0, tiled=True)  21.5 us
    pallas_call x8, Pallas kernels, call(): pl.pallas_call(body, out_shape=outs, in_specs=[hbm if i in hbm_in else vm...  20.5 us
    all_to_all x1, waiting for transfers between devices, shards(): share = lax.all_to_all(share, 'batch', 0, 0, tiled=True)  7.21 us
    all_to_all x1, starting transfers between devices, shards(): share = lax.all_to_all(share, 'batch', 0, 0, tiled=True)  6.61 us
  transfers between devices with their start and end apart: 3, of which 3 were waited for; matrix products, arithmetic and copies ran while one was open for 1% of the time, Pallas kernels for 5%

profile of v7, /device:TPU:1, one launch (start us, length us, event | category | flops | bytes accessed | tf_op | source)
XLA Modules:
  0.0 133.9 jit_solution(16957591322441428161)
XLA Ops:
  0.6 3.6 %forward.1 = f32[64,16,128]{2,1,0:T(8,128)} custom-call(bf16[16,256,128]{2,1,0:T(8,128)(2,1)} %bitcast.19, bf16[1056,512]{1,0:T(8,128)(2,1)} %constant.4.clone.table_hbm.table_ref, f32[64,8,128]{2,1,0:T(8,128)} %constant.5.clone.offset_hbm.offset_ref), custom_call_target="tpu_custom_call" | custom-call | tf_op jit(solution)/shard_map/forward/pallas_call | solution.py:458
  4.3 15.4 %all-to-all-start = ((f32[64,16,128]{2,1,0:T(8,128)}), f32[64,16,128]{2,1,0:T(8,128)S(1)}, u32[]{:S(2)}, u32[]{:S(2)}) async-start(f32[64,16,128]{2,1,0:T(8,128)} %forward.1), calls=%async_computation | async-start | bytes 1048576 | tf_op jit(solution)/shard_map/all_to_all | solution.py:512
  19.7 0.1 fusion
  19.8 0.0 copy-start.7
  19.9 0.3 squeeze.9
  20.1 0.3 squeeze.8
  20.4 0.1 pad_maximum_fusion
  20.5 0.0 copy-start
  20.6 0.0 copy-start.1
  20.6 16.3 %all-to-all-done.recv_ref = f32[64,16,128]{2,1,0:T(8,128)S(1)} async-done(((f32[64,16,128]{2,1,0:T(8,128)}), f32[64,16,128]{2,1,0:T(8,128)S(1)}, u32[]{:S(2)}, u32[]{:S(2)}) %all-to-all-start) | async-done | bytes 524320 | tf_op jit(solution)/shard_map/all_to_all | solution.py:512
  36.8 1.0 mix.1
  37.9 6.1 %all-to-all-start.1 = ((f32[64,16,128]{2,1,0:T(8,128)}), f32[64,16,128]{2,1,0:T(8,128)S(1)}, u32[]{:S(2)}, u32[]{:S(2)}) async-start(f32[64,16,128]{2,1,0:T(8,128)} %get-tuple-element.20), calls=%async_computation.1 | async-start | bytes 1048576 | tf_op jit(solution)/shard_map/all_to_all | solution.py:512
  44.0 4.8 %prepare.1 = (bf16[3,256,256]{2,1,0:T(8,128)(2,1)S(1)}, f32[16,256,128]{2,1,0:T(8,128)}, f32[16,256,128]{2,1,0:T(8,128)}) custom-call(bf16[16,16]{1,0:T(8,128)(2,1)S(1)} %copy-done.5, bf16[16,16]{1,0:T(8,128)(2,1)S(1)} %copy-done.6, bf16[16,16]{1,0:T(8,128)(2,1)S(1)} %copy-done.7, f32[1,16]{1,0:T(1,128)S(1)} %bitcast.18, bf16[16,256,128]{2,1,0:T(8,128)(2,1)} %bitcast.20, ...), custom_call_target="tpu_custom_call" | custom-call | tf_op jit(solution)/shard_map/prepare/pallas_call | solution.py:458
  48.8 0.7 copy-done.2
  49.6 11.5 %all-to-all-done.1.recv_ref = f32[64,16,128]{2,1,0:T(8,128)S(1)} async-done(((f32[64,16,128]{2,1,0:T(8,128)}), f32[64,16,128]{2,1,0:T(8,128)S(1)}, u32[]{:S(2)}, u32[]{:S(2)}) %all-to-all-start.1) | async-done | bytes 524320 | tf_op jit(solution)/shard_map/all_to_all | solution.py:512
  61.1 6.6 %middle.1 = (f32[1088,128]{1,0:T(8,128)S(1)}, bf16[16,256,128]{2,1,0:T(8,128)(2,1)}) custom-call(f32[64,16,128]{2,1,0:T(8,128)S(1)} %all-to-all-done.1.recv_ref, bf16[16,256,128]{2,1,0:T(8,128)(2,1)} %bitcast.21, bf16[16,256,128]{2,1,0:T(8,128)(2,1)} %bitcast.23, f32[16,256,128]{2,1,0:T(8,128)} %get-tuple-element.21.pre_hbm, ...), custom_call_target="tpu_custom_call" | custom-call | tf_op jit(solution)/shard_map/middle/pallas_call | solution.py:458
  67.7 23.9 %all_to_all.25 = f32[64,1,2176]{2,1,0:T(1,128)S(1)} all-to-all(f32[64,1,2176]{2,1,0:T(1,128)S(1)} %bitcast.16), channel_id=1, replica_groups=mesh['batch'=8,'px'=4,'py'=16] {'px','py'}, dimensions={0} | all-to-all | bytes 1114112 | tf_op jit(solution)/shard_map/all_to_all | solution.py:512
  91.7 0.2 mix_back.1
  91.8 23.9 %all_to_all.26 = f32[64,1,2176]{2,1,0:T(1,128)S(1)} all-to-all(f32[64,1,2176]{2,1,0:T(1,128)S(1)} %bitcast.17), channel_id=1, replica_groups=mesh['batch'=8,'px'=4,'py'=16] {'px','py'}, dimensions={0} | all-to-all | bytes 1114112 | tf_op jit(solution)/shard_map/all_to_all | solution.py:512
  115.7 0.7 share.1
  116.5 6.6 %all-to-all-start.4 = ((f32[8,40,128]{2,1,0:T(8,128)}), f32[8,40,128]{2,1,0:T(8,128)S(1)}, u32[]{:S(2)}, u32[]{:S(2)}) async-start(f32[8,40,128]{2,1,0:T(8,128)} %share.1), calls=%async_computation.4 | async-start | bytes 327680 | tf_op jit(solution)/shard_map/all_to_all | solution.py:542
  123.1 2.5 %input_grad.1 = bf16[16,256,128]{2,1,0:T(8,128)(2,1)} custom-call(f32[1088,128]{1,0:T(8,128)S(1)} %bitcast.14, bf16[16,256,128]{2,1,0:T(8,128)(2,1)S(1)} %copy-done.4, bf16[3,256,256]{2,1,0:T(8,128)(2,1)S(1)} %copy-done.3, bf16[1056,512]{1,0:T(8,128)(2,1)S(1)} %copy-done, f32[64,8,128]{2,1,0:T(8,128)S(1)} %copy-done.1), custom_call_target="tpu_custom_call" | custom-call | tf_op jit(solution)/shard_map/input_grad/pallas_call | solution.py:458
  125.6 7.2 %all-to-all-done.4.recv_ref = f32[8,40,128]{2,1,0:T(8,128)S(1)} async-done(((f32[8,40,128]{2,1,0:T(8,128)}), f32[8,40,128]{2,1,0:T(8,128)S(1)}, u32[]{:S(2)}, u32[]{:S(2)}) %all-to-all-start.4) | async-done | bytes 163872 | tf_op jit(solution)/shard_map/all_to_all | solution.py:542
  132.8 1.1 shared.1
  (17 shorter events, 0.1 us)
Async XLA Ops:
  0.6 19.1 %copy-start.9 = (f32[2,16,16,1,4,16]{5,4,3,2,1,0:T(4,128)S(1)}, f32[2,16,16,1,4,16]{5,4,3,2,1,0:T(4,128)}, u32[]{:S(2)}) copy-start(f32[2,16,16,1,4,16]{5,4,3,2,1,0:T(4,128)} %param.11) | copy-start | bytes 393220
  4.3 32.6 %all-to-all-start = ((f32[64,16,128]{2,1,0:T(8,128)}), f32[64,16,128]{2,1,0:T(8,128)S(1)}, u32[]{:S(2)}, u32[]{:S(2)}) async-start(f32[64,16,128]{2,1,0:T(8,128)} %forward.1), calls=%async_computation | async-start | bytes 1048576 | tf_op jit(solution)/shard_map/all_to_all | solution.py:512
  19.8 24.2 %copy-start.5 = (bf16[16,16]{1,0:T(8,128)(2,1)S(1)}, bf16[16,16]{1,0:T(8,128)(2,1)}, u32[]{:S(2)}) copy-start(bf16[16,16]{1,0:T(8,128)(2,1)} %skip_ref.1) | copy-start | bytes 1540
  19.8 24.2 %copy-start.6 = (bf16[16,16]{1,0:T(8,128)(2,1)S(1)}, bf16[16,16]{1,0:T(8,128)(2,1)}, u32[]{:S(2)}) copy-start(bf16[16,16]{1,0:T(8,128)(2,1)} %in_ref.1) | copy-start | bytes 1540
  19.8 24.2 %copy-start.7 = (bf16[16,16]{1,0:T(8,128)(2,1)S(1)}, bf16[16,16]{1,0:T(8,128)(2,1)}, u32[]{:S(2)}) copy-start(bf16[16,16]{1,0:T(8,128)(2,1)} %outer_ref.1) | copy-start | bytes 1540
  19.9 24.2 %copy-start.8 = (f32[16]{0:T(128)S(1)}, f32[16]{0:T(128)}, u32[]{:S(2)}) copy-start(f32[16]{0:T(128)} %param.13) | copy-start | bytes 196
  20.5 40.6 %copy-start = (bf16[1056,512]{1,0:T(8,128)(2,1)S(1)}, bf16[1056,512]{1,0:T(8,128)(2,1)}, u32[]{:S(2)}) copy-start(bf16[1056,512]{1,0:T(8,128)(2,1)} %constant.4.clone.table_hbm.table_ref) | copy-start | bytes 3244036
  20.6 40.6 %copy-start.1 = (f32[64,8,128]{2,1,0:T(8,128)S(1)}, f32[64,8,128]{2,1,0:T(8,128)}, u32[]{:S(2)}) copy-start(f32[64,8,128]{2,1,0:T(8,128)} %constant.5.clone.offset_hbm.offset_ref) | copy-start | bytes 786436
  37.9 23.3 %all-to-all-start.1 = ((f32[64,16,128]{2,1,0:T(8,128)}), f32[64,16,128]{2,1,0:T(8,128)S(1)}, u32[]{:S(2)}, u32[]{:S(2)}) async-start(f32[64,16,128]{2,1,0:T(8,128)} %get-tuple-element.20), calls=%async_computation.1 | async-start | bytes 1048576 | tf_op jit(solution)/shard_map/all_to_all | solution.py:512
  48.8 0.8 copy-start.2
  67.7 55.4 %copy-start.3 = (bf16[3,256,256]{2,1,0:T(8,128)(2,1)S(1)}, bf16[3,256,256]{2,1,0:T(8,128)(2,1)}, u32[]{:S(2)}) copy-start(bf16[3,256,256]{2,1,0:T(8,128)(2,1)} %copy-done.2) | copy-start | bytes 1179652
  91.8 31.2 %copy-start.4 = (bf16[16,256,128]{2,1,0:T(8,128)(2,1)S(1)}, bf16[16,256,128]{2,1,0:T(8,128)(2,1)}, u32[]{:S(2)}) copy-start(bf16[16,256,128]{2,1,0:T(8,128)(2,1)} %get-tuple-element.26.dpre_ref) | copy-start | bytes 3145732
  116.5 16.3 %all-to-all-start.4 = ((f32[8,40,128]{2,1,0:T(8,128)}), f32[8,40,128]{2,1,0:T(8,128)S(1)}, u32[]{:S(2)}, u32[]{:S(2)}) async-start(f32[8,40,128]{2,1,0:T(8,128)} %share.1), calls=%async_computation.4 | async-start | bytes 327680 | tf_op jit(solution)/shard_map/all_to_all | solution.py:542

commit v8 on v7

--- a/solution.py
+++ b/solution.py
@@ -342,14 +342,17 @@
         sums.append(dpre.astype(f32).reshape(C, 16, 256).sum(axis=1))
 
     copies[0].wait()
+    left = []
     for p in range(STEPS):
         if p % (STEPS // 2) == 0:
             first = 1 + 4 * (p // (STEPS // 2))
             for copy in copies[first : first + 4]:
                 copy.wait()
         step(p)
-    copy = pltpu.make_async_copy(dpre_ref, dpre_hbm, sems.at[9])
-    copy.start()
+        if p % (STEPS // 2) == STEPS // 2 - 1:
+            part = pl.ds((p // (STEPS // 2)) * HALF, HALF)
+            left.append(pltpu.make_async_copy(dpre_ref.at[:, part], dpre_hbm.at[:, part], sems.at[9 + len(left)]))
+            left[-1].start()
     bias = sum(sums)
     total = jnp.sum(bias, axis=1, keepdims=True)
     r = lax.broadcasted_iota(jnp.int32, (C, LANES), 0)
@@ -364,7 +367,8 @@
         out_ref[d * ROWS : (d + 1) * ROWS, :] = jnp.concatenate([value, small[d : d + 1]], axis=0)
 
     forward_part(lambda c: dpre_ref[c], table, off_ref, turn_ref, put)
-    copy.wait()
+    for copy in left:
+        copy.wait()
 
 
 def k_mix_back(recv_ref, wa_ref, wb_ref, out_ref, g_ref):
@@ -492,7 +496,7 @@
         k_middle, "middle",
         [shape(PEERS * ROWS, LANES), pltpu.HBM((C, XY, N), bf16)],
         [CELLS_LOW, CELLS_LOW, CELLS_KEPT, CELLS_KEPT, pltpu.VMEM((2, 256, 256), bf16), CELLS_LOW,
-         pltpu.SemaphoreType.DMA((10,)), turn, CELLS, square, square, square],
+         pltpu.SemaphoreType.DMA((11,)), turn, CELLS, square, square, square],
         recv, field, cotangent, pre, dact, kron, table, offset, hbm_in=(1, 2, 3, 4, 5), hbm_out=(1,),
     )
 

time: 136 us -> 136 us (level)
  no operation moved by 1% of the time
where the time goes in v8:
time: 136 us; the launch traced here: 134 us
  blocking collectives  47.8 us (35%)
  waiting for transfers between devices  35 us (26%)
  starting transfers between devices  28.1 us (21%)
  Pallas kernels  20.5 us (15%)
  local copies, waits for them, and re-layouts  1.41 us (1%)
    all_to_all x2, blocking collectives, exchange(): return lax.all_to_all(block, ('px', 'py'), 0, 0, tiled=True)  47.8 us
    all_to_all x2, waiting for transfers between devices, exchange(): return lax.all_to_all(block, ('px', 'py'), 0, 0, tiled=True)  27.8 us
    all_to_all x2, starting transfers between devices, exchange(): return lax.all_to_all(block, ('px', 'py'), 0, 0, tiled=True)  21.5 us
    pallas_call x8, Pallas kernels, call(): pl.pallas_call(body, out_shape=outs, in_specs=[hbm if i in hbm_in else vm...  20.5 us
    all_to_all x1, waiting for transfers between devices, shards(): share = lax.all_to_all(share, 'batch', 0, 0, tiled=True)  7.21 us
    all_to_all x1, starting transfers between devices, shards(): share = lax.all_to_all(share, 'batch', 0, 0, tiled=True)  6.61 us
  transfers between devices with their start and end apart: 3, of which 3 were waited for; matrix products, arithmetic and copies ran while one was open for 1% of the time, Pallas kernels for 5%

profile of v8, /device:TPU:1, one launch (start us, length us, event | category | flops | bytes accessed | tf_op | source)
XLA Modules:
  0.0 133.9 jit_solution(10442369779500372273)
XLA Ops:
  0.6 3.6 %forward.1 = f32[64,16,128]{2,1,0:T(8,128)} custom-call(bf16[16,256,128]{2,1,0:T(8,128)(2,1)} %bitcast.19, bf16[1056,512]{1,0:T(8,128)(2,1)} %constant.4.clone.table_hbm.table_ref, f32[64,8,128]{2,1,0:T(8,128)} %constant.5.clone.offset_hbm.offset_ref), custom_call_target="tpu_custom_call" | custom-call | tf_op jit(solution)/shard_map/forward/pallas_call | solution.py:462
  4.3 15.4 %all-to-all-start = ((f32[64,16,128]{2,1,0:T(8,128)}), f32[64,16,128]{2,1,0:T(8,128)S(1)}, u32[]{:S(2)}, u32[]{:S(2)}) async-start(f32[64,16,128]{2,1,0:T(8,128)} %forward.1), calls=%async_computation | async-start | bytes 1048576 | tf_op jit(solution)/shard_map/all_to_all | solution.py:516
  19.7 0.1 fusion
  19.8 0.0 copy-start.7
  19.9 0.3 squeeze.9
  20.1 0.3 squeeze.8
  20.4 0.1 pad_maximum_fusion
  20.5 0.0 copy-start
  20.6 0.0 copy-start.1
  20.6 16.3 %all-to-all-done.recv_ref = f32[64,16,128]{2,1,0:T(8,128)S(1)} async-done(((f32[64,16,128]{2,1,0:T(8,128)}), f32[64,16,128]{2,1,0:T(8,128)S(1)}, u32[]{:S(2)}, u32[]{:S(2)}) %all-to-all-start) | async-done | bytes 524320 | tf_op jit(solution)/shard_map/all_to_all | solution.py:516
  36.8 1.0 mix.1
  37.9 6.1 %all-to-all-start.1 = ((f32[64,16,128]{2,1,0:T(8,128)}), f32[64,16,128]{2,1,0:T(8,128)S(1)}, u32[]{:S(2)}, u32[]{:S(2)}) async-start(f32[64,16,128]{2,1,0:T(8,128)} %get-tuple-element.20), calls=%async_computation.1 | async-start | bytes 1048576 | tf_op jit(solution)/shard_map/all_to_all | solution.py:516
  44.0 4.8 %prepare.1 = (bf16[3,256,256]{2,1,0:T(8,128)(2,1)S(1)}, f32[16,256,128]{2,1,0:T(8,128)}, f32[16,256,128]{2,1,0:T(8,128)}) custom-call(bf16[16,16]{1,0:T(8,128)(2,1)S(1)} %copy-done.5, bf16[16,16]{1,0:T(8,128)(2,1)S(1)} %copy-done.6, bf16[16,16]{1,0:T(8,128)(2,1)S(1)} %copy-done.7, f32[1,16]{1,0:T(1,128)S(1)} %bitcast.18, bf16[16,256,128]{2,1,0:T(8,128)(2,1)} %bitcast.20, ...), custom_call_target="tpu_custom_call" | custom-call | tf_op jit(solution)/shard_map/prepare/pallas_call | solution.py:462
  48.8 0.7 copy-done.2
  49.6 11.5 %all-to-all-done.1.recv_ref = f32[64,16,128]{2,1,0:T(8,128)S(1)} async-done(((f32[64,16,128]{2,1,0:T(8,128)}), f32[64,16,128]{2,1,0:T(8,128)S(1)}, u32[]{:S(2)}, u32[]{:S(2)}) %all-to-all-start.1) | async-done | bytes 524320 | tf_op jit(solution)/shard_map/all_to_all | solution.py:516
  61.1 6.6 %middle.1 = (f32[1088,128]{1,0:T(8,128)S(1)}, bf16[16,256,128]{2,1,0:T(8,128)(2,1)}) custom-call(f32[64,16,128]{2,1,0:T(8,128)S(1)} %all-to-all-done.1.recv_ref, bf16[16,256,128]{2,1,0:T(8,128)(2,1)} %bitcast.21, bf16[16,256,128]{2,1,0:T(8,128)(2,1)} %bitcast.23, f32[16,256,128]{2,1,0:T(8,128)} %get-tuple-element.21.pre_hbm, ...), custom_call_target="tpu_custom_call" | custom-call | tf_op jit(solution)/shard_map/middle/pallas_call | solution.py:462
  67.7 23.9 %all_to_all.25 = f32[64,1,2176]{2,1,0:T(1,128)S(1)} all-to-all(f32[64,1,2176]{2,1,0:T(1,128)S(1)} %bitcast.16), channel_id=1, replica_groups=mesh['batch'=8,'px'=4,'py'=16] {'px','py'}, dimensions={0} | all-to-all | bytes 1114112 | tf_op jit(solution)/shard_map/all_to_all | solution.py:516
  91.7 0.2 mix_back.1
  91.9 23.9 %all_to_all.26 = f32[64,1,2176]{2,1,0:T(1,128)S(1)} all-to-all(f32[64,1,2176]{2,1,0:T(1,128)S(1)} %bitcast.17), channel_id=1, replica_groups=mesh['batch'=8,'px'=4,'py'=16] {'px','py'}, dimensions={0} | all-to-all | bytes 1114112 | tf_op jit(solution)/shard_map/all_to_all | solution.py:516
  115.7 0.7 share.1
  116.5 6.6 %all-to-all-start.4 = ((f32[8,40,128]{2,1,0:T(8,128)}), f32[8,40,128]{2,1,0:T(8,128)S(1)}, u32[]{:S(2)}, u32[]{:S(2)}) async-start(f32[8,40,128]{2,1,0:T(8,128)} %share.1), calls=%async_computation.4 | async-start | bytes 327680 | tf_op jit(solution)/shard_map/all_to_all | solution.py:546
  123.1 2.5 %input_grad.1 = bf16[16,256,128]{2,1,0:T(8,128)(2,1)} custom-call(f32[1088,128]{1,0:T(8,128)S(1)} %bitcast.14, bf16[16,256,128]{2,1,0:T(8,128)(2,1)S(1)} %copy-done.4, bf16[3,256,256]{2,1,0:T(8,128)(2,1)S(1)} %copy-done.3, bf16[1056,512]{1,0:T(8,128)(2,1)S(1)} %copy-done, f32[64,8,128]{2,1,0:T(8,128)S(1)} %copy-done.1), custom_call_target="tpu_custom_call" | custom-call | tf_op jit(solution)/shard_map/input_grad/pallas_call | solution.py:462
  125.6 7.2 %all-to-all-done.4.recv_ref = f32[8,40,128]{2,1,0:T(8,128)S(1)} async-done(((f32[8,40,128]{2,1,0:T(8,128)}), f32[8,40,128]{2,1,0:T(8,128)S(1)}, u32[]{:S(2)}, u32[]{:S(2)}) %all-to-all-start.4) | async-done | bytes 163872 | tf_op jit(solution)/shard_map/all_to_all | solution.py:546
  132.8 1.1 shared.1
  (17 shorter events, 0.1 us)
Async XLA Ops:
  0.6 19.1 %copy-start.9 = (f32[2,16,16,1,4,16]{5,4,3,2,1,0:T(4,128)S(1)}, f32[2,16,16,1,4,16]{5,4,3,2,1,0:T(4,128)}, u32[]{:S(2)}) copy-start(f32[2,16,16,1,4,16]{5,4,3,2,1,0:T(4,128)} %param.11) | copy-start | bytes 393220
  4.3 32.6 %all-to-all-start = ((f32[64,16,128]{2,1,0:T(8,128)}), f32[64,16,128]{2,1,0:T(8,128)S(1)}, u32[]{:S(2)}, u32[]{:S(2)}) async-start(f32[64,16,128]{2,1,0:T(8,128)} %forward.1), calls=%async_computation | async-start | bytes 1048576 | tf_op jit(solution)/shard_map/all_to_all | solution.py:516
  19.8 24.2 %copy-start.5 = (bf16[16,16]{1,0:T(8,128)(2,1)S(1)}, bf16[16,16]{1,0:T(8,128)(2,1)}, u32[]{:S(2)}) copy-start(bf16[16,16]{1,0:T(8,128)(2,1)} %skip_ref.1) | copy-start | bytes 1540
  19.8 24.2 %copy-start.6 = (bf16[16,16]{1,0:T(8,128)(2,1)S(1)}, bf16[16,16]{1,0:T(8,128)(2,1)}, u32[]{:S(2)}) copy-start(bf16[16,16]{1,0:T(8,128)(2,1)} %in_ref.1) | copy-start | bytes 1540
  19.8 24.2 %copy-start.7 = (bf16[16,16]{1,0:T(8,128)(2,1)S(1)}, bf16[16,16]{1,0:T(8,128)(2,1)}, u32[]{:S(2)}) copy-start(bf16[16,16]{1,0:T(8,128)(2,1)} %outer_ref.1) | copy-start | bytes 1540
  19.9 24.2 %copy-start.8 = (f32[16]{0:T(128)S(1)}, f32[16]{0:T(128)}, u32[]{:S(2)}) copy-start(f32[16]{0:T(128)} %param.13) | copy-start | bytes 196
  20.5 40.6 %copy-start = (bf16[1056,512]{1,0:T(8,128)(2,1)S(1)}, bf16[1056,512]{1,0:T(8,128)(2,1)}, u32[]{:S(2)}) copy-start(bf16[1056,512]{1,0:T(8,128)(2,1)} %constant.4.clone.table_hbm.table_ref) | copy-start | bytes 3244036
  20.6 40.6 %copy-start.1 = (f32[64,8,128]{2,1,0:T(8,128)S(1)}, f32[64,8,128]{2,1,0:T(8,128)}, u32[]{:S(2)}) copy-start(f32[64,8,128]{2,1,0:T(8,128)} %constant.5.clone.offset_hbm.offset_ref) | copy-start | bytes 786436
  37.9 23.3 %all-to-all-start.1 = ((f32[64,16,128]{2,1,0:T(8,128)}), f32[64,16,128]{2,1,0:T(8,128)S(1)}, u32[]{:S(2)}, u32[]{:S(2)}) async-start(f32[64,16,128]{2,1,0:T(8,128)} %get-tuple-element.20), calls=%async_computation.1 | async-start | bytes 1048576 | tf_op jit(solution)/shard_map/all_to_all | solution.py:516
  48.8 0.8 copy-start.2
  67.7 55.4 %copy-start.3 = (bf16[3,256,256]{2,1,0:T(8,128)(2,1)S(1)}, bf16[3,256,256]{2,1,0:T(8,128)(2,1)}, u32[]{:S(2)}) copy-start(bf16[3,256,256]{2,1,0:T(8,128)(2,1)} %copy-done.2) | copy-start | bytes 1179652
  91.8 31.2 %copy-start.4 = (bf16[16,256,128]{2,1,0:T(8,128)(2,1)S(1)}, bf16[16,256,128]{2,1,0:T(8,128)(2,1)}, u32[]{:S(2)}) copy-start(bf16[16,256,128]{2,1,0:T(8,128)(2,1)} %get-tuple-element.26.dpre_ref) | copy-start | bytes 3145732
  116.5 16.3 %all-to-all-start.4 = ((f32[8,40,128]{2,1,0:T(8,128)}), f32[8,40,128]{2,1,0:T(8,128)S(1)}, u32[]{:S(2)}, u32[]{:S(2)}) async-start(f32[8,40,128]{2,1,0:T(8,128)} %share.1), calls=%async_computation.4 | async-start | bytes 327680 | tf_op jit(solution)/shard_map/all_to_all | solution.py:546

commit v9 on v8

--- a/solution.py
+++ b/solution.py
@@ -147,12 +147,13 @@
 def k_forward(
     field_hbm, table_hbm, offset_hbm, out_hbm, out_ref, field_ref, table_ref, off_ref, turn_ref, sems
 ):
-    low_rows, plane_rows = pl.ds(4 * XY, 2 * C), pl.ds(0, 2 * XY)
+    low_rows, hi_rows, lo_rows = pl.ds(4 * XY, 2 * C), pl.ds(0, XY), pl.ds(XY, XY)
     pairs = [(table_hbm.at[low_rows], table_ref.at[low_rows])]
     for i in range(4):
         part = pl.ds(4 * i, 4)
         pairs.append((field_hbm.at[part], field_ref.at[part]))
-    pairs.append((table_hbm.at[plane_rows], table_ref.at[plane_rows]))
+    for part in (hi_rows, lo_rows):
+        pairs.append((table_hbm.at[part], table_ref.at[part]))
     pairs.append((offset_hbm.at[my_place()], off_ref))
     copies = [pltpu.make_async_copy(a, b, sems.at[i]) for i, (a, b) in enumerate(pairs)]
     for copy in copies:
@@ -175,7 +176,7 @@
 
     def done(mb):
         part = pl.ds(mb * PY, PY)
-        sent.append(pltpu.make_async_copy(out_ref.at[part], out_hbm.at[part], sems.at[7 + mb]))
+        sent.append(pltpu.make_async_copy(out_ref.at[part], out_hbm.at[part], sems.at[8 + mb]))
         sent[-1].start()
 
     forward_part(get, Table(table_ref), off_ref, turn_ref, put, ready, done)
@@ -315,9 +316,6 @@
     off_ref = offset_ref.at[my_place()]
     table = Table(table_ref)
     inverse_part(lambda d: recv_ref[d], table, off_ref, turn_ref, g_ref)
-    skip_acc[...] = jnp.zeros_like(skip_acc)
-    in_acc[...] = jnp.zeros_like(in_acc)
-    out_acc[...] = jnp.zeros_like(out_acc)
 
     kept, sums = [], []
 
@@ -336,9 +334,9 @@
         kept.append((dpre, f, d_inner, hid, cot, act))
         if p % 2:
             wide = lambda i: jnp.concatenate([k[i] for k in kept[-2:]], axis=1)
-            skip_acc[...] += dot_nt(wide(0), wide(1))
-            in_acc[...] += dot_nt(wide(2), wide(3))
-            out_acc[...] += dot_nt(wide(4), wide(5))
+            for i, acc in enumerate((skip_acc, in_acc, out_acc)):
+                pair = dot_nt(wide(2 * i), wide(2 * i + 1))
+                acc[...] = pair if p == 1 else acc[...] + pair
         sums.append(dpre.astype(f32).reshape(C, 16, 256).sum(axis=1))
 
     copies[0].wait()
@@ -520,7 +518,7 @@
 
     sent = call(
         k_forward, "forward", pltpu.HBM((PEERS, C, LANES), f32),
-        [pltpu.VMEM((PEERS, C, LANES), f32), CELLS_LOW, whole, OWN, turn, pltpu.SemaphoreType.DMA((7 + PX,))],
+        [pltpu.VMEM((PEERS, C, LANES), f32), CELLS_LOW, whole, OWN, turn, pltpu.SemaphoreType.DMA((8 + PX,))],
         field, table, offset, hbm_in=range(3), hbm_out=(0,),
     )
     kron, pre, dact = run_prepare(

time: 136 us -> 136 us (level)
  no operation moved by 1% of the time
where the time goes in v9:
time: 136 us; the launch traced here: 134 us
  blocking collectives  47.8 us (35%)
  waiting for transfers between devices  35 us (26%)
  starting transfers between devices  28.1 us (21%)
  Pallas kernels  20.5 us (15%)
  local copies, waits for them, and re-layouts  1.41 us (1%)
    all_to_all x2, blocking collectives, exchange(): return lax.all_to_all(block, ('px', 'py'), 0, 0, tiled=True)  47.8 us
    all_to_all x2, waiting for transfers between devices, exchange(): return lax.all_to_all(block, ('px', 'py'), 0, 0, tiled=True)  27.8 us
    all_to_all x2, starting transfers between devices, exchange(): return lax.all_to_all(block, ('px', 'py'), 0, 0, tiled=True)  21.5 us
    pallas_call x8, Pallas kernels, call(): pl.pallas_call(body, out_shape=outs, in_specs=[hbm if i in hbm_in else vm...  20.5 us
    all_to_all x1, waiting for transfers between devices, shards(): share = lax.all_to_all(share, 'batch', 0, 0, tiled=True)  7.21 us
    all_to_all x1, starting transfers between devices, shards(): share = lax.all_to_all(share, 'batch', 0, 0, tiled=True)  6.6 us
  transfers between devices with their start and end apart: 3, of which 3 were waited for; matrix products, arithmetic and copies ran while one was open for 1% of the time, Pallas kernels for 5%

profile of v9, /device:TPU:1, one launch (start us, length us, event | category | flops | bytes accessed | tf_op | source)
XLA Modules:
  0.0 133.9 jit_solution(12654638670924432587)
XLA Ops:
  0.6 3.6 %forward.1 = f32[64,16,128]{2,1,0:T(8,128)} custom-call(bf16[16,256,128]{2,1,0:T(8,128)(2,1)} %bitcast.19, bf16[1056,512]{1,0:T(8,128)(2,1)} %constant.4.clone.table_hbm.table_ref, f32[64,8,128]{2,1,0:T(8,128)} %constant.5.clone.offset_hbm.offset_ref), custom_call_target="tpu_custom_call" | custom-call | tf_op jit(solution)/shard_map/forward/pallas_call | solution.py:460
  4.3 15.4 %all-to-all-start = ((f32[64,16,128]{2,1,0:T(8,128)}), f32[64,16,128]{2,1,0:T(8,128)S(1)}, u32[]{:S(2)}, u32[]{:S(2)}) async-start(f32[64,16,128]{2,1,0:T(8,128)} %forward.1), calls=%async_computation | async-start | bytes 1048576 | tf_op jit(solution)/shard_map/all_to_all | solution.py:514
  19.7 0.1 fusion
  19.9 0.0 copy-start.7
  19.9 0.3 squeeze.9
  20.2 0.3 squeeze.8
  20.4 0.1 pad_maximum_fusion
  20.6 0.0 copy-start
  20.6 0.0 copy-start.1
  20.6 16.3 %all-to-all-done.recv_ref = f32[64,16,128]{2,1,0:T(8,128)S(1)} async-done(((f32[64,16,128]{2,1,0:T(8,128)}), f32[64,16,128]{2,1,0:T(8,128)S(1)}, u32[]{:S(2)}, u32[]{:S(2)}) %all-to-all-start) | async-done | bytes 524320 | tf_op jit(solution)/shard_map/all_to_all | solution.py:514
  36.9 1.0 mix.1
  37.9 6.1 %all-to-all-start.1 = ((f32[64,16,128]{2,1,0:T(8,128)}), f32[64,16,128]{2,1,0:T(8,128)S(1)}, u32[]{:S(2)}, u32[]{:S(2)}) async-start(f32[64,16,128]{2,1,0:T(8,128)} %get-tuple-element.20), calls=%async_computation.1 | async-start | bytes 1048576 | tf_op jit(solution)/shard_map/all_to_all | solution.py:514
  44.0 4.8 %prepare.1 = (bf16[3,256,256]{2,1,0:T(8,128)(2,1)S(1)}, f32[16,256,128]{2,1,0:T(8,128)}, f32[16,256,128]{2,1,0:T(8,128)}) custom-call(bf16[16,16]{1,0:T(8,128)(2,1)S(1)} %copy-done.5, bf16[16,16]{1,0:T(8,128)(2,1)S(1)} %copy-done.6, bf16[16,16]{1,0:T(8,128)(2,1)S(1)} %copy-done.7, f32[1,16]{1,0:T(1,128)S(1)} %bitcast.18, bf16[16,256,128]{2,1,0:T(8,128)(2,1)} %bitcast.20, ...), custom_call_target="tpu_custom_call" | custom-call | tf_op jit(solution)/shard_map/prepare/pallas_call | solution.py:460
  48.9 0.7 copy-done.2
  49.6 11.5 %all-to-all-done.1.recv_ref = f32[64,16,128]{2,1,0:T(8,128)S(1)} async-done(((f32[64,16,128]{2,1,0:T(8,128)}), f32[64,16,128]{2,1,0:T(8,128)S(1)}, u32[]{:S(2)}, u32[]{:S(2)}) %all-to-all-start.1) | async-done | bytes 524320 | tf_op jit(solution)/shard_map/all_to_all | solution.py:514
  61.1 6.6 %middle.1 = (f32[1088,128]{1,0:T(8,128)S(1)}, bf16[16,256,128]{2,1,0:T(8,128)(2,1)}) custom-call(f32[64,16,128]{2,1,0:T(8,128)S(1)} %all-to-all-done.1.recv_ref, bf16[16,256,128]{2,1,0:T(8,128)(2,1)} %bitcast.21, bf16[16,256,128]{2,1,0:T(8,128)(2,1)} %bitcast.23, f32[16,256,128]{2,1,0:T(8,128)} %get-tuple-element.21.pre_hbm, ...), custom_call_target="tpu_custom_call" | custom-call | tf_op jit(solution)/shard_map/middle/pallas_call | solution.py:460
  67.7 24.0 %all_to_all.25 = f32[64,1,2176]{2,1,0:T(1,128)S(1)} all-to-all(f32[64,1,2176]{2,1,0:T(1,128)S(1)} %bitcast.16), channel_id=1, replica_groups=mesh['batch'=8,'px'=4,'py'=16] {'px','py'}, dimensions={0} | all-to-all | bytes 1114112 | tf_op jit(solution)/shard_map/all_to_all | solution.py:514
  91.7 0.2 mix_back.1
  91.9 23.9 %all_to_all.26 = f32[64,1,2176]{2,1,0:T(1,128)S(1)} all-to-all(f32[64,1,2176]{2,1,0:T(1,128)S(1)} %bitcast.17), channel_id=1, replica_groups=mesh['batch'=8,'px'=4,'py'=16] {'px','py'}, dimensions={0} | all-to-all | bytes 1114112 | tf_op jit(solution)/shard_map/all_to_all | solution.py:514
  115.7 0.7 share.1
  116.5 6.6 %all-to-all-start.4 = ((f32[8,40,128]{2,1,0:T(8,128)}), f32[8,40,128]{2,1,0:T(8,128)S(1)}, u32[]{:S(2)}, u32[]{:S(2)}) async-start(f32[8,40,128]{2,1,0:T(8,128)} %share.1), calls=%async_computation.4 | async-start | bytes 327680 | tf_op jit(solution)/shard_map/all_to_all | solution.py:544
  123.1 2.5 %input_grad.1 = bf16[16,256,128]{2,1,0:T(8,128)(2,1)} custom-call(f32[1088,128]{1,0:T(8,128)S(1)} %bitcast.14, bf16[16,256,128]{2,1,0:T(8,128)(2,1)S(1)} %copy-done.4, bf16[3,256,256]{2,1,0:T(8,128)(2,1)S(1)} %copy-done.3, bf16[1056,512]{1,0:T(8,128)(2,1)S(1)} %copy-done, f32[64,8,128]{2,1,0:T(8,128)S(1)} %copy-done.1), custom_call_target="tpu_custom_call" | custom-call | tf_op jit(solution)/shard_map/input_grad/pallas_call | solution.py:460
  125.6 7.2 %all-to-all-done.4.recv_ref = f32[8,40,128]{2,1,0:T(8,128)S(1)} async-done(((f32[8,40,128]{2,1,0:T(8,128)}), f32[8,40,128]{2,1,0:T(8,128)S(1)}, u32[]{:S(2)}, u32[]{:S(2)}) %all-to-all-start.4) | async-done | bytes 163872 | tf_op jit(solution)/shard_map/all_to_all | solution.py:544
  132.8 1.1 shared.1
  (17 shorter events, 0.1 us)
Async XLA Ops:
  0.6 19.1 %copy-start.9 = (f32[2,16,16,1,4,16]{5,4,3,2,1,0:T(4,128)S(1)}, f32[2,16,16,1,4,16]{5,4,3,2,1,0:T(4,128)}, u32[]{:S(2)}) copy-start(f32[2,16,16,1,4,16]{5,4,3,2,1,0:T(4,128)} %param.11) | copy-start | bytes 393220
  4.3 32.6 %all-to-all-start = ((f32[64,16,128]{2,1,0:T(8,128)}), f32[64,16,128]{2,1,0:T(8,128)S(1)}, u32[]{:S(2)}, u32[]{:S(2)}) async-start(f32[64,16,128]{2,1,0:T(8,128)} %forward.1), calls=%async_computation | async-start | bytes 1048576 | tf_op jit(solution)/shard_map/all_to_all | solution.py:514
  19.8 24.2 %copy-start.5 = (bf16[16,16]{1,0:T(8,128)(2,1)S(1)}, bf16[16,16]{1,0:T(8,128)(2,1)}, u32[]{:S(2)}) copy-start(bf16[16,16]{1,0:T(8,128)(2,1)} %skip_ref.1) | copy-start | bytes 1540
  19.8 24.2 %copy-start.6 = (bf16[16,16]{1,0:T(8,128)(2,1)S(1)}, bf16[16,16]{1,0:T(8,128)(2,1)}, u32[]{:S(2)}) copy-start(bf16[16,16]{1,0:T(8,128)(2,1)} %in_ref.1) | copy-start | bytes 1540
  19.9 24.2 %copy-start.7 = (bf16[16,16]{1,0:T(8,128)(2,1)S(1)}, bf16[16,16]{1,0:T(8,128)(2,1)}, u32[]{:S(2)}) copy-start(bf16[16,16]{1,0:T(8,128)(2,1)} %outer_ref.1) | copy-start | bytes 1540
  19.9 24.2 %copy-start.8 = (f32[16]{0:T(128)S(1)}, f32[16]{0:T(128)}, u32[]{:S(2)}) copy-start(f32[16]{0:T(128)} %param.13) | copy-start | bytes 196
  20.6 40.6 %copy-start = (bf16[1056,512]{1,0:T(8,128)(2,1)S(1)}, bf16[1056,512]{1,0:T(8,128)(2,1)}, u32[]{:S(2)}) copy-start(bf16[1056,512]{1,0:T(8,128)(2,1)} %constant.4.clone.table_hbm.table_ref) | copy-start | bytes 3244036
  20.6 40.6 %copy-start.1 = (f32[64,8,128]{2,1,0:T(8,128)S(1)}, f32[64,8,128]{2,1,0:T(8,128)}, u32[]{:S(2)}) copy-start(f32[64,8,128]{2,1,0:T(8,128)} %constant.5.clone.offset_hbm.offset_ref) | copy-start | bytes 786436
  37.9 23.3 %all-to-all-start.1 = ((f32[64,16,128]{2,1,0:T(8,128)}), f32[64,16,128]{2,1,0:T(8,128)S(1)}, u32[]{:S(2)}, u32[]{:S(2)}) async-start(f32[64,16,128]{2,1,0:T(8,128)} %get-tuple-element.20), calls=%async_computation.1 | async-start | bytes 1048576 | tf_op jit(solution)/shard_map/all_to_all | solution.py:514
  48.9 0.8 copy-start.2
  67.7 55.4 %copy-start.3 = (bf16[3,256,256]{2,1,0:T(8,128)(2,1)S(1)}, bf16[3,256,256]{2,1,0:T(8,128)(2,1)}, u32[]{:S(2)}) copy-start(bf16[3,256,256]{2,1,0:T(8,128)(2,1)} %copy-done.2) | copy-start | bytes 1179652
  91.9 31.2 %copy-start.4 = (bf16[16,256,128]{2,1,0:T(8,128)(2,1)S(1)}, bf16[16,256,128]{2,1,0:T(8,128)(2,1)}, u32[]{:S(2)}) copy-start(bf16[16,256,128]{2,1,0:T(8,128)(2,1)} %get-tuple-element.26.dpre_ref) | copy-start | bytes 3145732
  116.5 16.3 %all-to-all-start.4 = ((f32[8,40,128]{2,1,0:T(8,128)}), f32[8,40,128]{2,1,0:T(8,128)S(1)}, u32[]{:S(2)}, u32[]{:S(2)}) async-start(f32[8,40,128]{2,1,0:T(8,128)} %share.1), calls=%async_computation.4 | async-start | bytes 327680 | tf_op jit(solution)/shard_map/all_to_all | solution.py:544
